TPU v7x, 32 devices: a whole 2x2x4 slice. The times are simulated.
32 devices in a mesh: dp: 16 (over z, y, x), tensor: 2 (over core).
Axes of the slice: x: 2, y: 2, z: 4, core: 2. Of those that a mesh axis runs over, the one named last changes fastest.
Arguments:
- tokens: bfloat16 [16384, 768], P('dp'), may hold values from -6 to 6
- upper_delta: bfloat16 [16384, 768], P(('dp', 'tensor')), may hold values from -0.119628906 to 0.119628906
- segments: int32 [32, 512], P('dp'), may hold values from 0 to 3, as said below
- summary_index: int32 [32, 4], P('dp'), may hold values from 0 to 419, as said below
- validity: int32 [32, 512], P('dp'), may hold values from 0 to 1, as said below
- queries: bfloat16 [128, 768], P('dp'), may hold values from -15 to 15
- positives: int32 [128], P('dp'), may hold values from 0 to 127
- query_weight: bfloat16 [768, 768], P(None, 'tensor'), may hold values from -0.21875 to 0.21875
- key_weight: bfloat16 [768, 768], P(None, 'tensor'), may hold values from -0.21875 to 0.21875
- value_weight: bfloat16 [768, 768], P(None, 'tensor'), may hold values from -0.21875 to 0.21875
- query_bias: bfloat16 [768], P('tensor'), may hold values from -3 to 3
- value_bias: bfloat16 [768], P('tensor'), may hold values from -3 to 3
- output_weight: bfloat16 [768, 768], P('tensor'), may hold values from -1.25 to 1.25
- output_bias: bfloat16 [768], replicated, may hold values from -3 to 3
- first_gain: bfloat16 [768], replicated, may hold values from 0.25 to 1.75
- first_shift: bfloat16 [768], replicated, may hold values from -3 to 3
- up_weight: bfloat16 [768, 3072], P(None, 'tensor'), may hold values from -0.21875 to 0.21875
- up_bias: bfloat16 [3072], P('tensor'), may hold values from -3 to 3
- down_weight: bfloat16 [3072, 768], P('tensor'), may hold values from -0.109375 to 0.109375
- down_bias: bfloat16 [768], replicated, may hold values from -3 to 3
- second_gain: bfloat16 [768], replicated, may hold values from 0.25 to 1.75
Outputs:
- loss_terms: float32 [128], P('dp')
- query_gradient: float32 [128, 768], P('dp')
- token_gradient: bfloat16 [16384, 768], P(('dp', 'tensor'))
- query_weight_gradient: float32 [768, 768], P(None, 'tensor')
- key_weight_gradient: float32 [768, 768], P(None, 'tensor')
- value_weight_gradient: float32 [768, 768], P(None, 'tensor')
- query_bias_gradient: float32 [768], P('tensor')
- value_bias_gradient: float32 [768], P('tensor')
- output_weight_gradient: float32 [768, 768], P('tensor')
- output_bias_gradient: float32 [768], replicated
- first_gain_gradient: float32 [768], replicated
- first_shift_gradient: float32 [768], replicated
- up_weight_gradient: float32 [768, 3072], P(None, 'tensor')
- up_bias_gradient: float32 [3072], P('tensor')
- down_weight_gradient: float32 [3072, 768], P('tensor')
- down_bias_gradient: float32 [768], replicated
- second_gain_gradient: float32 [768], replicated
Inputs may be any that keep to these rules, and one draw needn't show every extreme that they name: `segments`: along each row the numbers never fall; every one of the 4 passages of a row holds at least an eighth of 512 consecutive tokens, and padding tokens carry the last passage's number. `summary_index`: each entry is a valid token of passage k of its row, among that passage's first four tokens. `validity`: each row ends in a run of 1 to 64 padding tokens that lies inside its last passage; all other tokens are 1.
All inputs are finite; a program needn't handle non-finite values.
Results may differ from a plain program's by a relative error of at most 0.04.
Values may be sent and summed in bfloat16 or wider, within the bound.
No kernel may reach another device: no remote copies, remote signals or barrier semaphores. Data moves between devices by JAX's collectives and lax.ppermute only.
A program may use at most 192 MiB of HBM per device.

v0:
```python
import math

import jax
import jax.numpy as jnp
from jax import lax
from jax.sharding import PartitionSpec as P

D = 768
HD = 64


norm_eps = 1e-05
neg_large = -1e30
root_half = 0.7071067811865476
inv_root_tau = 0.3989422804014327


def layer_norm(inputs, norm_gain, norm_shift):
    center = inputs - jnp.mean(inputs, -1, keepdims=True)
    spread = jnp.mean(center * center, -1, keepdims=True)
    row_scale = lax.rsqrt(spread + norm_eps)
    normed = center * row_scale
    return (normed * norm_gain + norm_shift, normed, row_scale)


def norm_back(out_delta, normed, row_scale, norm_gain):
    scaled = out_delta * norm_gain
    first_mean = jnp.mean(scaled, -1, keepdims=True)
    second_mean = jnp.mean(scaled * normed, -1, keepdims=True)
    in_delta = row_scale * (scaled - first_mean - normed * second_mean)
    return (in_delta, jnp.sum(out_delta * normed, 0), jnp.sum(out_delta, 0))


def shards(
    tokens,
    upper_delta,
    segments,
    summary_index,
    validity,
    queries,
    positives,
    query_weight,
    key_weight,
    value_weight,
    query_bias,
    value_bias,
    output_weight,
    output_bias,
    first_gain,
    first_shift,
    up_weight,
    up_bias,
    down_weight,
    down_bias,
    second_gain,
):
    row_count, length = segments.shape
    token_count = row_count * length
    width_local = query_weight.shape[1]
    heads_local = width_local // HD
    head_shape = (row_count, length, heads_local, HD)
    scaling = 1.0 / math.sqrt(HD)
    score_scale = 1.0 / math.sqrt(D)
    visible = ((segments[:, :, None] == segments[:, None, :]) & (validity[:, None, :] > 0))[:, None]
    upper_rows = lax.all_gather(upper_delta, "tensor", axis=0, tiled=True)
    query_heads = (
        (
            jnp.dot(tokens, query_weight, preferred_element_type=jnp.float32)
            + query_bias.astype(jnp.float32)
        )
        .astype(jnp.bfloat16)
        .reshape(head_shape)
    )
    key_heads = (
        jnp.dot(tokens, key_weight, preferred_element_type=jnp.float32)
        .astype(jnp.bfloat16)
        .reshape(head_shape)
    )
    value_heads = (
        (
            jnp.dot(tokens, value_weight, preferred_element_type=jnp.float32)
            + value_bias.astype(jnp.float32)
        )
        .astype(jnp.bfloat16)
        .reshape(head_shape)
    )

    def masked_logits():
        product = (
            jnp.einsum(
                "rqhd,rkhd->rhqk", query_heads, key_heads, preferred_element_type=jnp.float32
            )
            * scaling
        )
        return jnp.where(visible, product, neg_large)

    logits = masked_logits()
    row_peak = jnp.max(logits, -1, keepdims=True)
    row_exp = jnp.exp(logits - row_peak)
    row_total = jnp.sum(row_exp, -1, keepdims=True)
    weights_low = (row_exp / row_total).astype(jnp.bfloat16)
    log_total = row_peak + jnp.log(row_total)
    context = jnp.einsum(
        "rhqk,rkhd->rqhd", weights_low, value_heads, preferred_element_type=jnp.float32
    )
    context = context.astype(jnp.bfloat16).reshape(token_count, width_local)
    head_sum = lax.psum(
        jnp.dot(context, output_weight, preferred_element_type=jnp.float32).astype(jnp.bfloat16),
        "tensor",
    ).astype(jnp.float32)
    first_out, first_normed, first_scale = layer_norm(
        tokens.astype(jnp.float32) + (head_sum + output_bias.astype(jnp.float32)),
        first_gain.astype(jnp.float32),
        first_shift.astype(jnp.float32),
    )
    first_low = first_out.astype(jnp.bfloat16)
    hidden = jnp.dot(first_low, up_weight, preferred_element_type=jnp.float32) + up_bias.astype(
        jnp.float32
    )
    activated = (0.5 * hidden * (1.0 + lax.erf(hidden * root_half))).astype(jnp.bfloat16)
    unit_sum = lax.psum(
        jnp.dot(activated, down_weight, preferred_element_type=jnp.float32).astype(jnp.bfloat16),
        "tensor",
    ).astype(jnp.float32)
    second_out, second_normed, second_scale = layer_norm(
        first_out + (unit_sum + down_bias.astype(jnp.float32)), second_gain.astype(jnp.float32), 0.0
    )
    flat_index = (jnp.arange(row_count, dtype=jnp.int32)[:, None] * length + summary_index).reshape(
        -1
    )
    summary_low = second_out[flat_index].astype(jnp.bfloat16)
    passages = lax.all_gather(summary_low, "dp", axis=0, tiled=True)
    score_rows, score_labels = (queries, positives)
    scores = (
        jnp.einsum("qd,pd->qp", score_rows, passages, preferred_element_type=jnp.float32)
        * score_scale
    )
    score_peak = jnp.max(scores, -1, keepdims=True)
    score_exp = jnp.exp(scores - score_peak)
    score_total = jnp.sum(score_exp, -1, keepdims=True)
    chosen = jnp.arange(scores.shape[1], dtype=jnp.int32)[None, :] == score_labels[:, None]
    row_losses = (
        score_peak[:, 0] + jnp.log(score_total[:, 0]) - jnp.sum(jnp.where(chosen, scores, 0.0), -1)
    )
    score_delta = (score_exp / score_total - chosen.astype(jnp.float32)).astype(jnp.bfloat16)
    selected = score_delta
    passage_delta = lax.psum_scatter(
        jnp.einsum("qp,qd->pd", selected, queries, preferred_element_type=jnp.float32)
        * score_scale,
        "dp",
        scatter_dimension=0,
        tiled=True,
    )
    query_gradient = (
        jnp.einsum("qp,pd->qd", score_delta, passages, preferred_element_type=jnp.float32)
        * score_scale
    )
    out_delta = upper_rows.astype(jnp.float32).at[flat_index].add(passage_delta)
    second_parts = norm_back(
        out_delta, second_normed, second_scale, second_gain.astype(jnp.float32)
    )
    second_delta = second_parts[0]
    second_gain_gradient = second_parts[1]
    down_bias_gradient = jnp.sum(second_delta, 0)
    unit_delta = second_delta.astype(jnp.bfloat16)
    down_weight_gradient = jnp.einsum(
        "tf,td->fd", activated, unit_delta, preferred_element_type=jnp.float32
    )
    act_delta = jnp.einsum("td,fd->tf", unit_delta, down_weight, preferred_element_type=jnp.float32)
    gelu_slope = (
        0.5 * (1.0 + lax.erf(hidden * root_half))
        + hidden * jnp.exp(-0.5 * hidden * hidden) * inv_root_tau
    )
    hidden_delta = (act_delta * gelu_slope).astype(jnp.bfloat16)
    up_bias_gradient = jnp.sum(hidden_delta, 0, dtype=jnp.float32)
    up_weight_gradient = jnp.einsum(
        "td,tf->df", first_low, hidden_delta, preferred_element_type=jnp.float32
    )
    back_sum = lax.psum(
        jnp.einsum("tf,df->td", hidden_delta, up_weight, preferred_element_type=jnp.float32).astype(
            jnp.bfloat16
        ),
        "tensor",
    ).astype(jnp.float32)
    first_delta, first_gain_gradient, first_shift_gradient = norm_back(
        second_delta + back_sum, first_normed, first_scale, first_gain.astype(jnp.float32)
    )
    output_bias_gradient = jnp.sum(first_delta, 0)
    branch_delta = first_delta.astype(jnp.bfloat16)
    output_weight_gradient = jnp.einsum(
        "tc,td->cd", context, branch_delta, preferred_element_type=jnp.float32
    )
    context_delta = jnp.einsum(
        "td,cd->tc", branch_delta, output_weight, preferred_element_type=jnp.float32
    )
    context_delta = context_delta.astype(jnp.bfloat16).reshape(head_shape)
    weights_again = jnp.exp(masked_logits() - log_total)
    weight_delta = jnp.einsum(
        "rqhd,rkhd->rhqk", context_delta, value_heads, preferred_element_type=jnp.float32
    )
    inner_sum = jnp.sum(weights_again * weight_delta, -1, keepdims=True)
    logit_delta = (weights_again * (weight_delta - inner_sum)).astype(jnp.bfloat16)
    query_delta = (
        (
            jnp.einsum(
                "rhqk,rkhd->rqhd", logit_delta, key_heads, preferred_element_type=jnp.float32
            )
            * scaling
        )
        .astype(jnp.bfloat16)
        .reshape(token_count, width_local)
    )
    key_delta = (
        (
            jnp.einsum(
                "rhqk,rqhd->rkhd", logit_delta, query_heads, preferred_element_type=jnp.float32
            )
            * scaling
        )
        .astype(jnp.bfloat16)
        .reshape(token_count, width_local)
    )
    value_delta = (
        jnp.einsum(
            "rhqk,rqhd->rkhd",
            weights_again.astype(jnp.bfloat16),
            context_delta,
            preferred_element_type=jnp.float32,
        )
        .astype(jnp.bfloat16)
        .reshape(token_count, width_local)
    )
    query_weight_gradient = jnp.einsum(
        "td,tc->dc", tokens, query_delta, preferred_element_type=jnp.float32
    )
    key_weight_gradient = jnp.einsum(
        "td,tc->dc", tokens, key_delta, preferred_element_type=jnp.float32
    )
    value_weight_gradient = jnp.einsum(
        "td,tc->dc", tokens, value_delta, preferred_element_type=jnp.float32
    )
    query_bias_gradient = jnp.sum(query_delta, 0, dtype=jnp.float32)
    value_bias_gradient = jnp.sum(value_delta, 0, dtype=jnp.float32)
    half_rows = token_count // lax.axis_size("tensor")
    summed = jnp.zeros((half_rows * lax.axis_size("tensor"), tokens.shape[1]), jnp.float32)
    for part_delta, part_weight in (
        (query_delta, query_weight),
        (key_delta, key_weight),
        (value_delta, value_weight),
    ):
        selected = part_delta
        summed = summed + jnp.einsum(
            "tc,dc->td", selected, part_weight, preferred_element_type=jnp.float32
        )
    scattered = lax.psum_scatter(
        summed.astype(jnp.bfloat16), "tensor", scatter_dimension=0, tiled=True
    ).astype(jnp.float32)
    own_rows = lax.dynamic_slice_in_dim(
        first_delta, lax.axis_index("tensor") * half_rows, half_rows, 0
    )
    token_gradient = (own_rows + scattered).astype(jnp.bfloat16)
    all_totals = lax.psum(
        (
            down_weight_gradient,
            down_bias_gradient,
            second_gain_gradient,
            up_weight_gradient,
            up_bias_gradient,
            first_gain_gradient,
            first_shift_gradient,
            output_weight_gradient,
            output_bias_gradient,
            query_weight_gradient,
            key_weight_gradient,
            value_weight_gradient,
            query_bias_gradient,
            value_bias_gradient,
        ),
        "dp",
    )
    return (
        row_losses,
        query_gradient,
        token_gradient,
        all_totals[9],
        all_totals[10],
        all_totals[11],
        all_totals[12],
        all_totals[13],
        all_totals[7],
        all_totals[8],
        all_totals[5],
        all_totals[6],
        all_totals[3],
        all_totals[4],
        all_totals[0],
        all_totals[1],
        all_totals[2],
    )


def solution(mesh):
    in_specs = (
        P("dp", None),
        P(("dp", "tensor"), None),
        P("dp", None),
        P("dp", None),
        P("dp", None),
        P("dp", None),
        P("dp"),
        P(None, "tensor"),
        P(None, "tensor"),
        P(None, "tensor"),
        P("tensor"),
        P("tensor"),
        P("tensor", None),
        P(),
        P(),
        P(),
        P(None, "tensor"),
        P("tensor"),
        P("tensor", None),
        P(),
        P(),
    )
    out_specs = (
        P("dp"),
        P("dp", None),
        P(("dp", "tensor"), None),
        P(None, "tensor"),
        P(None, "tensor"),
        P(None, "tensor"),
        P("tensor"),
        P("tensor"),
        P("tensor", None),
        P(),
        P(),
        P(),
        P(None, "tensor"),
        P("tensor"),
        P("tensor", None),
        P(),
        P(),
    )
    return jax.shard_map(shards, mesh=mesh, in_specs=in_specs, out_specs=out_specs, check_vma=False)
```

profile of v0, /device:TPU:0, one launch (start us, length us, event | category | flops | bytes accessed | tf_op | source)
XLA Modules:
  0.0 813.2 jit_solution(5994558659590932006)
XLA Ops:
  9.5 2.5 add_convert_fusion.3
  12.0 1.2 copy.53
  13.2 2.6 reshape.164
  15.7 3.4 add_convert_fusion.2
  19.1 2.3 copy.54
  21.4 3.2 reshape.165
  24.6 3.4 convolution_convert_fusion.4
  28.1 2.3 copy.55
  30.3 3.2 reshape.166
  34.1 3.7 fusion.51
  37.8 1.9 fusion
  39.7 2.7 copy-done.2
  42.4 2.8 fusion.24
  47.1 2.2 convolution_convert_fusion
  49.4 23.1 %all-reduce.7.cloned.1.call-done = bf16[1024,768]{1,0:T(8,128)(2,1)} async-done(((bf16[1024,768]{1,0:T(8,128)(2,1)}), bf16[1024,768]{1,0:T(8,128)(2,1)}) %all-reduce.7.cloned.1.call-update) | async-done | bytes 1572880 | tf_op jit(solution)/shard_map/psum | solution.py:107
  72.6 2.6 fusion.13
  76.3 5.3 multiply_convert_fusion.1
  81.6 1.7 copy-done.44
  83.3 3.7 convolution_convert_fusion.2
  88.0 20.8 %all-reduce.9.cloned.1.call-done = bf16[1024,768]{1,0:T(8,128)(2,1)} async-done(((bf16[1024,768]{1,0:T(8,128)(2,1)}), bf16[1024,768]{1,0:T(8,128)(2,1)}) %all-reduce.9.cloned.1.call-update) | async-done | bytes 1572880 | tf_op jit(solution)/shard_map/psum | solution.py:121
  108.8 3.3 fusion.50
  112.7 1.1 copy-done.3
  113.7 1.6 fusion.14
  115.3 2.2 gather_fusion
  117.5 41.9 %all_gather.6 = bf16[128,768]{1,0:T(8,128)(2,1)S(1)} all-gather(bf16[8,768]{1,0:T(8,128)(2,1)S(1)} %gather_fusion), channel_id=1, replica_groups=mesh['dp'=16,'tensor'=2] {'dp'}, dimensions={0}, use_global_device_ids=true | all-gather | bytes 208896 | tf_op jit(solution)/shard_map/all_gather | solution.py:132
  159.9 1.1 convolution_multiply_fusion
  161.1 3.3 convert_element_type.163
  164.4 114.0 %reduce-scatter.3.cloned.1.call-done = f32[8,768]{1,0:T(8,128)} async-done(((f32[128,768]{1,0:T(8,128)}), f32[8,768]{1,0:T(8,128)}) %reduce-scatter.3.cloned.1.call-update) | async-done | bytes 24592 | tf_op jit(solution)/shard_map/reduce_scatter | solution.py:147
  278.4 4.4 scatter_fusion
  282.7 4.2 multiply_reduce_fusion.1
  289.1 3.0 copy-done.45
  292.1 4.7 convert_reduce_fusion
  296.8 1.6 copy-done.42
  298.5 3.7 convolution_convert_fusion.1
  302.3 19.6 %all-reduce.11.cloned.1.call-done = bf16[1024,768]{1,0:T(8,128)(2,1)} async-done(((bf16[1024,768]{1,0:T(8,128)(2,1)}), bf16[1024,768]{1,0:T(8,128)(2,1)}) %all-reduce.11.cloned.1.call-update) | async-done | bytes 1572880 | tf_op jit(solution)/shard_map/psum | solution.py:179
  321.9 4.9 multiply_reduce_fusion.2
  327.0 1.7 fusion.49
  328.7 1.7 copy-done.10
  330.5 1.0 convolution_convert_fusion.3
  331.5 1.2 copy.61
  332.6 2.6 reshape.169
  335.2 6.9 convert_reduce_fusion.1
  342.1 8.9 %multiply_reduce_fusion = (f32[2,6,512]{2,1,0:T(8,128)S(1)}, f32[2,6,512,512]{2,3,1,0:T(8,128)}) fusion(f32[2,6,512,512]{2,3,1,0:T(8,128)} %copy-done.2, f32[2,6,512]{2,1,0:T(8,128)S(1)} %log_add_fusion, bf16[2,512,6,64]{1,0,3,2:T(2,128)(2,1)S(1)} %reshape.164, bf16[2,512,6,64]{1,0,3,2:T(2,128)(2,1)S(1)} %reshape.169), kind=kOutput, calls=%fused_computation.3 | convolution fusion | flops 412084224 | bytes 26787840 | tf_op jit(solution)/shard_map/rqhd,rkhd->rhqk/dot_general | solution.py:198
  351.0 7.1 multiply_convert_fusion
  358.2 2.0 fusion.23
  360.2 1.2 convert_reduce_fusion.2
  364.3 1.0 fusion.54
  365.3 1.0 fusion.53
  366.4 2.2 add_convert_fusion
  368.7 7.8 fusion.28
  376.6 4.9 fusion.40
  381.5 1.8 convolution_bitcast_fusion
  383.3 1.8 convolution_bitcast_fusion.2
  385.1 1.8 convolution_bitcast_fusion.1
  387.6 1.8 fusion.25
  390.9 82.0 %all-reduce = (f32[384]{0:T(512)}, f32[384]{0:T(512)}, f32[768]{0:T(1024)}, f32[768]{0:T(1024)}, f32[768]{0:T(1024)}, /*index=5*/f32[1536]{0:T(1024)}, f32[768]{0:T(1024)}, f32[768]{0:T(1024)}) all-reduce(f32[384]{0:T(512)S(1)} %reduce_sum.197, f32[384]{0:T(512)S(1)} %reduce_sum.199, ...), channel_id=1, replica_groups=mesh['dp'=16,'tensor'=2] {'dp'}, use_global_device_ids=true, to_apply=%region_24.25 | all-reduce | flops 6144 | bytes 49152 | tf_op jit(solution)/shard_map/psum | solution.py:262
  472.9 2.8 add_convert_fusion.1
  475.7 315.8 %all-reduce.13.cloned.1.call-done = (f32[768,384]{0,1:T(8,128)}, f32[768,384]{0,1:T(8,128)}, f32[768,384]{0,1:T(8,128)}, f32[384,768]{1,0:T(8,128)}, f32[768,1536]{1,0:T(8,128)}, /*index=5*/f32[1536,768]{1,0:T(8,128)}) async-done(((f32[768,384]{0,1:T(8,128)}, f32[768,384]{0,1:T(8,128)}, f32[768,384]{0,1:T(8,128)}, f32[384,768]{1,0:T(8,128)}, f32[768,1536]{1,0:T(8,128)}, /*index=5*/f32[1536,768]{1,0:T(8,128)}), ...) | async-done | bytes 14155792 | tf_op jit(solution)/shard_map/psum | solution.py:262
  791.6 2.8 copy.73
  794.4 1.4 copy.74
  795.8 1.4 copy.75
  797.1 1.0 copy.122
  798.2 5.5 copy.123
  803.7 2.2 copy.124
  (154 shorter events, 15.5 us)
Async XLA Ops:
  7.2 69.0 %copy-start = (bf16[768,1536]{1,0:T(8,128)(2,1)S(1)}, bf16[768,1536]{1,0:T(8,128)(2,1)}, u32[]{:S(2)}) copy-start(bf16[768,1536]{1,0:T(8,128)(2,1)} %param.37) | copy-start | bytes 7077892
  7.2 65.3 %all-reduce.7.cloned.1.call-start = ((), (), s32[]{:S(2)}) async-start(), calls=%async_computation.2 | async-start | bytes 3145728 | tf_op jit(solution)/shard_map/psum | solution.py:107
  24.6 8.9 %copy-start.31 = (s32[2,512]{1,0:T(2,128)S(1)}, s32[2,512]{1,0:T(2,128)}, u32[]{:S(2)}) copy-start(s32[2,512]{1,0:T(2,128)} %param.23) | copy-start | bytes 12292
  37.8 4.6 copy-start.2
  45.2 1.9 copy-start.25
  46.0 3.3 copy-start.34
  46.0 3.3 copy-start.35
  46.0 3.3 copy-start.36
  46.0 3.3 copy-start.32
  46.2 0.9 copy-start.16
  49.3 59.5 %all-reduce.9.cloned.1.call-start = ((), (), s32[]{:S(2)}) async-start(), calls=%async_computation.3 | async-start | bytes 3145728 | tf_op jit(solution)/shard_map/psum | solution.py:121
  72.6 2.6 copy-start.5
  72.6 2.8 copy-start.7
  76.2 7.1 copy-start.40
  81.6 1.7 copy-start.44
  83.3 4.5 copy-start.39
  83.3 4.7 copy-start.37
  83.3 4.7 copy-start.38
  87.0 74.1 %all-gather.2.cloned.1.call-start = ((), (), s32[]{:S(2)}) async-start(), calls=%async_computation.4 | async-start | bytes 2359296 | tf_op jit(solution)/shard_map/all_gather | solution.py:65
  87.7 190.6 %reduce-scatter.3.cloned.1.call-start = ((), (), s32[]{:S(2)}) async-start(), calls=%async_computation.5 | async-start | bytes 417792 | tf_op jit(solution)/shard_map/reduce_scatter | solution.py:147
  112.1 1.7 copy-start.3
  112.6 46.8 %copy-start.30 = (bf16[8,768]{1,0:T(8,128)(2,1)S(1)}, bf16[8,768]{1,0:T(8,128)(2,1)}, u32[]{:S(2)}) copy-start(bf16[8,768]{1,0:T(8,128)(2,1)} %param.26) | copy-start | bytes 36868
  112.6 47.1 %copy-start.33 = (s32[8]{0:T(128)S(1)}, s32[8]{0:T(128)}, u32[]{:S(2)}) copy-start(s32[8]{0:T(128)} %param.27) | copy-start | bytes 100
  161.1 160.8 %all-reduce.11.cloned.1.call-start = ((), (), s32[]{:S(2)}) async-start(), calls=%async_computation.6 | async-start | bytes 3145728 | tf_op jit(solution)/shard_map/psum | solution.py:179
  282.7 4.2 copy-start.4
  282.7 4.7 copy-start.12
  287.5 1.7 copy-start.41
  287.5 4.6 copy-start.45
  288.5 8.4 %copy-start.13 = (f32[1024,768]{1,0:T(8,128)}, f32[1024,768]{1,0:T(8,128)S(1)}, u32[]{:S(2)}) copy-start(f32[1024,768]{1,0:T(8,128)S(1)} %subtract_multiply_fusion.1) | copy-start | bytes 9437188
  296.8 1.6 copy-start.42
  302.2 170.7 %reduce-scatter.5.cloned.1.call-start = ((), (), s32[]{:S(2)}) async-start(), calls=%async_computation.7 | async-start | bytes 2359296 | tf_op jit(solution)/shard_map/reduce_scatter | solution.py:255
  302.3 24.5 %copy-start.6 = (bf16[1024,768]{1,0:T(8,128)(2,1)S(1)}, bf16[1024,768]{1,0:T(8,128)(2,1)}, u32[]{:S(2)}) copy-start(bf16[1024,768]{1,0:T(8,128)(2,1)} %param.21) | copy-start | bytes 4718596
  321.9 4.9 copy-start.8
  321.9 4.9 copy-start.14
  321.9 5.1 copy-start.15
  327.0 3.4 copy-start.26
  328.7 1.7 copy-start.10
  335.2 15.8 %slice-start = ((s8[12582912]{0:T(1024)(128)(4,1)}), s8[4194304]{0:T(1024)(128)(4,1)S(1)}, s32[]{:S(2)}) async-start(s8[12582912]{0:T(1024)(128)(4,1)} %bitcast.93), calls=%async_computation.9 | async-start | bytes 8388608
  335.2 15.8 %slice-start.1 = ((s8[12582912]{0:T(1024)(128)(4,1)}), s8[4194304]{0:T(1024)(128)(4,1)S(1)}, s32[]{:S(2)}) async-start(s8[12582912]{0:T(1024)(128)(4,1)} %bitcast.93), calls=%async_computation.10 | async-start | bytes 8388608
  342.1 8.9 %slice-start.2 = ((s8[12582912]{0:T(1024)(128)(4,1)}), s8[4194304]{0:T(1024)(128)(4,1)S(1)}, s32[]{:S(2)}) async-start(s8[12582912]{0:T(1024)(128)(4,1)} %bitcast.93), calls=%async_computation.11 | async-start | bytes 8388608
  351.0 7.2 copy-start.21
  358.1 2.0 copy-start.18
  362.3 1.9 copy-start.27
  364.1 1.2 copy-start.28
  364.3 2.1 copy-start.19
  365.3 1.1 copy-start.29
  368.6 422.9 %all-reduce.13.cloned.1.call-start = ((), (), s32[]{:S(2)}) async-start(), calls=%async_computation.8 | async-start | bytes 28311552 | tf_op jit(solution)/shard_map/psum | solution.py:262
  368.7 7.9 copy-start.9
  368.7 7.9 copy-start.43
  381.5 1.8 copy-start.20
  385.1 2.3 copy-start.11
  385.1 2.5 copy-start.17
  791.6 2.8 copy-start.24
  791.6 4.2 copy-start.23
  791.6 5.6 copy-start.22
  797.1 6.5 slice-start.3
  798.2 5.5 slice-start.4
  798.2 7.7 copy-start.1
Sparse Core Ops, SparseCore 0:
  49.4 23.1 all-reduce.6
  87.1 21.5 all-reduce.8
  110.3 10.9 all-gather.1
  161.2 117.1 reduce-scatter.2
  302.4 19.4 all-reduce.10
  368.8 10.2 reduce-scatter.4
  389.6 401.9 all-reduce.12
where the time goes:
time: 822 us; the launch traced here: 813 us
  waiting for transfers between devices  494 us (60%)
  blocking collectives  124 us (15%)
  matrix products  81.8 us (10%)
  local copies, waits for them, and re-layouts  54.1 us (7%)
  other arithmetic  43.7 us (5%)
  between operations  15.3 us (2%)
    psum x1, waiting for transfers between devices, shards(): lax.psum((down_weight_gradient, down_bias_gradient, second_gain_gradient,...  316 us
    reduce_scatter x1, waiting for transfers between devices, shards(): lax.psum_scatter(jnp.einsum('qp,qd->pd', selected, queries, preferred_ele...  114 us
    psum x1, blocking collectives, shards(): lax.psum((down_weight_gradient, down_bias_gradient, second_gain_gradient,...  82 us
    all_gather x1, blocking collectives, shards(): passages = lax.all_gather(summary_low, 'dp', axis=0, tiled=True)  41.9 us
    unnamed x112, local copies, waits for them, and re-layouts  30 us
    psum x1, waiting for transfers between devices, shards(): lax.psum(jnp.dot(context, output_weight, preferred_element_type=jnp.float...  23.1 us
    psum x1, waiting for transfers between devices, shards(): lax.psum(jnp.dot(activated, down_weight, preferred_element_type=jnp.float...  20.8 us
    psum x1, waiting for transfers between devices, shards(): lax.psum(jnp.einsum('tf,df->td', hidden_delta, up_weight, preferred_eleme...  19.6 us
  transfers between devices with their start and end apart: 7, of which 5 were waited for; matrix products, arithmetic and copies ran while one was open for 5% of the time, Pallas kernels for 0%

commit v1 on v0

v1 whole, which is shorter than its diff:
```python
import math

import jax
import jax.numpy as jnp
from jax import lax
from jax.sharding import PartitionSpec as P

D = 768
HD = 64


norm_eps = 1e-05
neg_large = -1e30
root_half = 0.7071067811865476
inv_root_tau = 0.3989422804014327


def bits_of(axis):
    return lax.axis_size(axis).bit_length() - 1


def flip(value, axis, bit):
    size = lax.axis_size(axis)
    return lax.ppermute(value, axis, [(i, i ^ (1 << bit)) for i in range(size)])


def swap(value):
    return flip(value, "tensor", 0)


def own_bit(axis, bit):
    return (lax.axis_index(axis) >> bit) & 1


def join(value, other, high):
    return jnp.where(
        high == 1, jnp.concatenate([other, value], 0), jnp.concatenate([value, other], 0)
    )


def gather_dp(value):
    for bit in range(bits_of("dp")):
        value = join(value, flip(value, "dp", bit), own_bit("dp", bit))
    return value


def gather_all(value):
    value = join(value, swap(value), own_bit("tensor", 0))
    return gather_dp(value)


def reduce_small(value):
    for bit in range(bits_of("dp")):
        value = value + flip(value, "dp", bit)
    return value


def reduce_rows(value, order):
    for bit in order:
        half = value.shape[0] // 2
        mine = own_bit("dp", bit)
        sent = lax.dynamic_slice_in_dim(value, (1 - mine) * half, half, 0)
        kept = lax.dynamic_slice_in_dim(value, mine * half, half, 0)
        arrived = flip(sent, "dp", bit)
        value = (kept.astype(jnp.float32) + arrived.astype(jnp.float32)).astype(jnp.bfloat16)
    for bit in reversed(order):
        value = join(value, flip(value, "dp", bit), own_bit("dp", bit))
    return value


def reduce_halves(value):
    count = bits_of("dp")
    first = list(range(count))
    second = [1, 0] + first[2:]
    half = value.shape[0] // 2
    return jnp.concatenate(
        [reduce_rows(value[:half], first), reduce_rows(value[half:], second)], 0
    ).astype(jnp.float32)


def layer_norm(inputs, norm_gain, norm_shift):
    center = inputs - jnp.mean(inputs, -1, keepdims=True)
    spread = jnp.mean(center * center, -1, keepdims=True)
    row_scale = lax.rsqrt(spread + norm_eps)
    normed = center * row_scale
    return (normed * norm_gain + norm_shift, normed, row_scale)


def norm_back(out_delta, normed, row_scale, norm_gain):
    scaled = out_delta * norm_gain
    first_mean = jnp.mean(scaled, -1, keepdims=True)
    second_mean = jnp.mean(scaled * normed, -1, keepdims=True)
    in_delta = row_scale * (scaled - first_mean - normed * second_mean)
    return (in_delta, jnp.sum(out_delta * normed, 0), jnp.sum(out_delta, 0))


def dot(left, right):
    return jnp.dot(left, right, preferred_element_type=jnp.float32)


def dot_t(left, right):
    return lax.dot_general(left, right, (((1,), (1,)), ((), ())), preferred_element_type=jnp.float32)


def t_dot(left, right):
    return lax.dot_general(left, right, (((0,), (0,)), ((), ())), preferred_element_type=jnp.float32)


def shards(
    tokens,
    upper_delta,
    segments,
    summary_index,
    validity,
    queries,
    positives,
    query_weight,
    key_weight,
    value_weight,
    query_bias,
    value_bias,
    output_weight,
    output_bias,
    first_gain,
    first_shift,
    up_weight,
    up_bias,
    down_weight,
    down_bias,
    second_gain,
):
    f32, bf16 = jnp.float32, jnp.bfloat16
    row_count, length = segments.shape
    token_count = row_count * length
    members = lax.axis_size("tensor")
    place = lax.axis_index("tensor")
    own_count = token_count // members
    width_local = query_weight.shape[1]
    heads_local = width_local // HD
    head_shape = (row_count, length, heads_local, HD)
    scaling = 1.0 / math.sqrt(HD)
    score_scale = 1.0 / math.sqrt(D)

    def own(value):
        part = value.shape[0] // members
        return lax.dynamic_slice_in_dim(value, place * part, part, 0)

    def others(value):
        part = value.shape[0] // members
        return lax.dynamic_slice_in_dim(value, (1 - place) * part, part, 0)

    output_other = swap(output_weight)
    up_other = swap(up_weight)
    up_bias_other = swap(up_bias.reshape(1, -1))
    down_other = swap(down_weight)
    all_queries = gather_dp(queries)
    all_positives = gather_dp(positives.reshape(-1, 1)).reshape(-1)

    visible = ((segments[:, :, None] == segments[:, None, :]) & (validity[:, None, :] > 0))[:, None]
    query_heads = (
        (dot(tokens, query_weight) + query_bias.astype(f32)).astype(bf16).reshape(head_shape)
    )
    key_heads = dot(tokens, key_weight).astype(bf16).reshape(head_shape)
    value_heads = (
        (dot(tokens, value_weight) + value_bias.astype(f32)).astype(bf16).reshape(head_shape)
    )

    def masked_logits():
        product = (
            jnp.einsum("rqhd,rkhd->rhqk", query_heads, key_heads, preferred_element_type=f32)
            * scaling
        )
        return jnp.where(visible, product, neg_large)

    logits = masked_logits()
    row_peak = jnp.max(logits, -1, keepdims=True)
    row_exp = jnp.exp(logits - row_peak)
    row_total = jnp.sum(row_exp, -1, keepdims=True)
    weights_low = (row_exp / row_total).astype(bf16)
    log_total = row_peak + jnp.log(row_total)
    context = jnp.einsum("rhqk,rkhd->rqhd", weights_low, value_heads, preferred_element_type=f32)
    context = context.astype(bf16).reshape(token_count, width_local)

    context_in = swap(others(context))
    head_sum = dot(own(context), output_weight) + dot(context_in, output_other)
    own_tokens = own(tokens)
    first_out, first_normed, first_scale = layer_norm(
        own_tokens.astype(f32) + (head_sum + output_bias.astype(f32)),
        first_gain.astype(f32),
        first_shift.astype(f32),
    )
    first_low = first_out.astype(bf16)
    first_in = swap(first_low)

    def gelu(hidden):
        return (0.5 * hidden * (1.0 + lax.erf(hidden * root_half))).astype(bf16)

    def gelu_slope(hidden):
        return (
            0.5 * (1.0 + lax.erf(hidden * root_half))
            + hidden * jnp.exp(-0.5 * hidden * hidden) * inv_root_tau
        )

    hidden_other = dot(first_low, up_other) + up_bias_other.astype(f32)
    active_other = gelu(hidden_other)
    active_in = swap(active_other)
    hidden = dot(first_low, up_weight) + up_bias.astype(f32)
    active = gelu(hidden)
    unit_sum = dot(active, down_weight) + dot(active_other, down_other)
    second_out, second_normed, second_scale = layer_norm(
        first_out + (unit_sum + down_bias.astype(f32)), second_gain.astype(f32), 0.0
    )

    positions = own(summary_index).reshape(-1)
    at_summary = jnp.arange(own_count, dtype=jnp.int32)[None, :] == (
        positions + jnp.arange(own_count // length, dtype=jnp.int32).repeat(summary_index.shape[1]) * length
    )[:, None]
    summary_low = dot(at_summary.astype(bf16), second_out.astype(bf16)).astype(bf16)
    passages = gather_all(summary_low)
    scores = dot_t(all_queries, passages) * score_scale
    score_peak = jnp.max(scores, -1, keepdims=True)
    score_exp = jnp.exp(scores - score_peak)
    score_total = jnp.sum(score_exp, -1, keepdims=True)
    chosen = jnp.arange(scores.shape[1], dtype=jnp.int32)[None, :] == all_positives[:, None]
    losses = (
        score_peak[:, 0] + jnp.log(score_total[:, 0]) - jnp.sum(jnp.where(chosen, scores, 0.0), -1)
    )
    score_delta = (score_exp / score_total - chosen.astype(f32)).astype(bf16)
    query_count = queries.shape[0]
    query_start = lax.axis_index("dp") * query_count
    row_losses = lax.dynamic_slice_in_dim(losses, query_start, query_count, 0)
    query_gradient = (
        dot(lax.dynamic_slice_in_dim(score_delta, query_start, query_count, 0), passages)
        * score_scale
    )
    own_passages = summary_low.shape[0]
    passage_start = (lax.axis_index("dp") * members + place) * own_passages
    passage_delta = (
        t_dot(lax.dynamic_slice_in_dim(score_delta, passage_start, own_passages, 1), all_queries)
        * score_scale
    )

    out_delta = upper_delta.astype(f32)
    for k in range(own_passages):
        out_delta = out_delta + jnp.where(at_summary[k][:, None], passage_delta[k][None, :], 0.0)
    second_delta, second_gain_gradient, _ = norm_back(
        out_delta, second_normed, second_scale, second_gain.astype(f32)
    )
    down_bias_gradient = jnp.sum(second_delta, 0)
    unit_delta = second_delta.astype(bf16)
    unit_in = swap(unit_delta)
    delta_other = (dot_t(unit_delta, down_other) * gelu_slope(hidden_other)).astype(bf16)
    delta_in = swap(delta_other)
    hidden_delta = (dot_t(unit_delta, down_weight) * gelu_slope(hidden)).astype(bf16)
    down_weight_gradient = (t_dot(active, unit_delta) + t_dot(active_in, unit_in)).astype(bf16)
    up_weight_gradient = (t_dot(first_low, hidden_delta) + t_dot(first_in, delta_in)).astype(bf16)
    up_bias_gradient = jnp.sum(hidden_delta, 0, dtype=f32) + jnp.sum(delta_in, 0, dtype=f32)
    back_sum = dot_t(hidden_delta, up_weight) + dot_t(delta_other, up_other)
    first_delta, first_gain_gradient, first_shift_gradient = norm_back(
        second_delta + back_sum, first_normed, first_scale, first_gain.astype(f32)
    )
    output_bias_gradient = jnp.sum(first_delta, 0)
    branch_own = first_delta.astype(bf16)
    branch_delta = join(branch_own, swap(branch_own), place)

    output_weight_gradient = t_dot(branch_delta, context).astype(bf16)
    context_delta = dot_t(branch_delta, output_weight).astype(bf16).reshape(head_shape)
    weights_again = jnp.exp(masked_logits() - log_total)
    weight_delta = jnp.einsum(
        "rqhd,rkhd->rhqk", context_delta, value_heads, preferred_element_type=f32
    )
    inner_sum = jnp.sum(weights_again * weight_delta, -1, keepdims=True)
    logit_delta = (weights_again * (weight_delta - inner_sum)).astype(bf16)
    query_delta = (
        (
            jnp.einsum("rhqk,rkhd->rqhd", logit_delta, key_heads, preferred_element_type=f32)
            * scaling
        )
        .astype(bf16)
        .reshape(token_count, width_local)
    )
    key_delta = (
        (
            jnp.einsum("rhqk,rqhd->rkhd", logit_delta, query_heads, preferred_element_type=f32)
            * scaling
        )
        .astype(bf16)
        .reshape(token_count, width_local)
    )
    value_delta = (
        jnp.einsum(
            "rhqk,rqhd->rkhd",
            weights_again.astype(bf16),
            context_delta,
            preferred_element_type=f32,
        )
        .astype(bf16)
        .reshape(token_count, width_local)
    )
    query_bias_gradient = jnp.sum(query_delta, 0, dtype=f32)
    value_bias_gradient = jnp.sum(value_delta, 0, dtype=f32)

    def input_part(rows):
        return (
            dot_t(rows(query_delta), query_weight)
            + dot_t(rows(key_delta), key_weight)
            + dot_t(rows(value_delta), value_weight)
        )

    input_in = swap(input_part(others).astype(bf16))
    token_gradient = (first_delta + input_part(own) + input_in.astype(f32)).astype(bf16)

    head_gradients = jnp.concatenate(
        [
            t_dot(tokens, query_delta).astype(bf16),
            t_dot(tokens, key_delta).astype(bf16),
            t_dot(tokens, value_delta).astype(bf16),
            output_weight_gradient,
        ],
        1,
    )
    down_total = reduce_halves(down_weight_gradient)
    up_total = reduce_halves(up_weight_gradient)
    head_total = reduce_halves(head_gradients)

    shared = jnp.stack(
        [
            output_bias_gradient,
            first_gain_gradient,
            first_shift_gradient,
            down_bias_gradient,
            second_gain_gradient,
        ]
    )
    shared = shared + swap(shared)
    small = reduce_small(
        jnp.concatenate(
            [
                shared.reshape(-1),
                up_bias_gradient,
                query_bias_gradient,
                value_bias_gradient,
            ]
        ).reshape(1, -1)
    ).reshape(-1)
    width = D
    units = up_bias.shape[0]
    parts = [small[i * width : (i + 1) * width] for i in range(5)]
    rest = small[5 * width :]
    return (
        row_losses,
        query_gradient,
        token_gradient,
        head_total[:, :width_local],
        head_total[:, width_local : 2 * width_local],
        head_total[:, 2 * width_local : 3 * width_local],
        rest[units : units + width_local],
        rest[units + width_local :],
        head_total[:, 3 * width_local :].T,
        parts[0],
        parts[1],
        parts[2],
        up_total,
        rest[:units],
        down_total,
        parts[3],
        parts[4],
    )


def solution(mesh):
    in_specs = (
        P("dp", None),
        P(("dp", "tensor"), None),
        P("dp", None),
        P("dp", None),
        P("dp", None),
        P("dp", None),
        P("dp"),
        P(None, "tensor"),
        P(None, "tensor"),
        P(None, "tensor"),
        P("tensor"),
        P("tensor"),
        P("tensor", None),
        P(),
        P(),
        P(),
        P(None, "tensor"),
        P("tensor"),
        P("tensor", None),
        P(),
        P(),
    )
    out_specs = (
        P("dp"),
        P("dp", None),
        P(("dp", "tensor"), None),
        P(None, "tensor"),
        P(None, "tensor"),
        P(None, "tensor"),
        P("tensor"),
        P("tensor"),
        P("tensor", None),
        P(),
        P(),
        P(),
        P(None, "tensor"),
        P("tensor"),
        P("tensor", None),
        P(),
        P(),
    )
    return jax.shard_map(shards, mesh=mesh, in_specs=in_specs, out_specs=out_specs, check_vma=False)
```

time: 822 us -> 365 us (0.44)
  waiting for transfers between devices: 494 us -> 124 us
  blocking collectives: 124 us -> 0 us
  starting transfers between devices: 0.29 us -> 66.5 us
  local copies, waits for them, and re-layouts: 54.1 us -> 30.7 us
  between operations: 15.3 us -> 2.55 us
  matrix products: 81.8 us -> 92.2 us
    psum x4 -> x0, waiting for transfers between devices: 379 us -> none  [the longest x1 316 us: shards(): lax.psum((down_weight_gradient, down_bias_gradient, second_gain_gradient,...]
    ppermute x0 -> x77, waiting for transfers between devices: none -> 124 us  [flip(): return lax.ppermute(value, axis, [(i, i ^ 1 << bit) for i in range(size)])]
    reduce_scatter x2 -> x0, waiting for transfers between devices: 114 us -> none  [the longest x1 114 us: shards(): lax.psum_scatter(jnp.einsum('qp,qd->pd', selected, queries, preferred_ele...]
    psum x1 -> x0, blocking collectives: 82 us -> none  [shards(): lax.psum((down_weight_gradient, down_bias_gradient, second_gain_gradient,...]
    ppermute x0 -> x77, starting transfers between devices: none -> 66.5 us  [flip(): return lax.ppermute(value, axis, [(i, i ^ 1 << bit) for i in range(size)])]
    all_gather x1 -> x0, blocking collectives: 41.9 us -> none  [shards(): passages = lax.all_gather(summary_low, 'dp', axis=0, tiled=True)]
    unnamed x112 -> x109, local copies, waits for them, and re-layouts: 30 us -> 9.01 us
    convert_element_type x11 -> x40, other arithmetic: 14.7 us -> 25.4 us  [the longest x1 10 us: shards(): logit_delta = (weights_again * (weight_delta - inner_sum)).astype(bf16)]
  transfers between devices with their start and end apart: 7 -> 77, of which waited for: 5 -> 41; matrix products, arithmetic and copies ran while one was open for 5% -> 38% of each run, Pallas kernels for 0% -> 0%
where the time goes in v1:
time: 365 us; the launch traced here: 360 us
  waiting for transfers between devices  124 us (34%)
  matrix products  92.2 us (25%)
  starting transfers between devices  66.5 us (18%)
  other arithmetic  44.4 us (12%)
  local copies, waits for them, and re-layouts  30.7 us (8%)
    ppermute x77, waiting for transfers between devices, flip(): return lax.ppermute(value, axis, [(i, i ^ 1 << bit) for i in range(size)])  124 us
    ppermute x77, starting transfers between devices, flip(): return lax.ppermute(value, axis, [(i, i ^ 1 << bit) for i in range(size)])  66.5 us
    dot_general x11, matrix products, dot(): return jnp.dot(left, right, preferred_element_type=jnp.float32)  23.8 us
    dot_general x9, matrix products, t_dot(): lax.dot_general(left, right, (((0,), (0,)), ((), ())), preferred_element_...  23.6 us
    dot_general x12, matrix products, dot_t(): lax.dot_general(left, right, (((1,), (1,)), ((), ())), preferred_element_...  22.8 us
    dot_general x1, matrix products, shards(): jnp.einsum('rqhd,rkhd->rhqk', context_delta, value_heads, preferred_eleme...  10.6 us
    convert_element_type x1, other arithmetic, shards(): logit_delta = (weights_again * (weight_delta - inner_sum)).astype(bf16)  10 us
    unnamed x109, local copies, waits for them, and re-layouts  9.01 us
  transfers between devices with their start and end apart: 77, of which 41 were waited for; matrix products, arithmetic and copies ran while one was open for 38% of the time, Pallas kernels for 0%

profile of v1, /device:TPU:0, one launch (start us, length us, event | category | flops | bytes accessed | tf_op | source)
XLA Modules:
  0.0 360.2 jit_solution(12279364032938546525)
XLA Ops:
  0.7 2.6 convolution_convert_fusion.1
  4.2 2.7 add_convert_fusion.4
  8.7 2.4 add_convert_fusion.5
  12.7 3.7 %fusion.75 = (f32[2,6,512]{2,1,0:T(8,128)S(1)}, f32[2,6,512,512]{2,3,1,0:T(8,128)S(1)}) fusion(bf16[2,512,6,64]{1,0,3,2:T(2,128)(2,1)S(1)} %reshape.510, bf16[2,512,6,64]{1,0,3,2:T(2,128)(2,1)} %reshape.509, pred[2,512,512]{1,2,0:T(8,128)(4,1)S(1)} %compare_and_fusion), kind=kOutput, calls=%fused_computation.258 | convolution fusion | flops 412084224 | bytes 14704640 | tf_op jit(solution)/shard_map/rqhd,rkhd->rhqk/dot_general | solution.py:170
  16.4 1.9 fusion
  18.3 2.6 copy-done.1
  21.2 2.3 fusion.26
  27.0 2.9 collective-permute-start.14
  40.7 1.9 collective-permute-done.16
  43.5 2.2 fusion.76
  48.0 3.1 multiply_convert_fusion.2
  52.5 4.6 %multiply_convert_fusion.1 = (bf16[512,1536]{1,0:T(8,128)(2,1)}, f32[512,1536]{1,0:T(8,128)S(1)}) fusion(f32[1536]{0:T(1024)S(1)} %convert_reduce_fusion.4, bf16[512,768]{1,0:T(8,128)(2,1)} %fusion.20, bf16[768,1536]{1,0:T(8,128)(2,1)} %collective-permute-done.6), kind=kOutput, calls=%fused_computation.29 | convolution fusion | flops 1212678144 | bytes 7870464 | tf_op jit(solution)/shard_map/dot_general | solution.py:98
  57.1 3.0 fusion.77
  61.4 2.8 collective-permute-start.17
  78.0 3.6 collective-permute-done.3
  81.6 2.1 collective-permute-done.13
  88.7 2.8 convert_reduce_fusion.1
  93.0 3.4 fusion.15
  96.5 4.0 %multiply_reduce_fusion.2 = (f32[768]{0:T(1024)S(1)}, f32[512]{0:T(512)S(1)}, f32[512]{0:T(512)S(1)}, f32[768]{0:T(1024)S(1)}, f32[512,768]{1,0:T(8,128)S(1)}) fusion(f32[512,768]{1,0:T(8,128)S(1)} %get-tuple-element.126, f32[512]{0:T(512)S(1)} %add_rsqrt_fusion.1, f32[512]{0:T(512)S(1)} %broadcast_multiply_fusion.5, f32[768]{0:T(1024)S(1)} %convert_element_type.397, ...), kind=kOutput, calls=%fused_computation.44 | convolution fusion | flops 1212282368 | bytes 10241024 | tf_op jit(solution)/shard_map/dot_general | solution.py:102
  102.5 4.7 %fusion.81 = f32[768,1536]{1,0:T(8,128)} fusion(bf16[512,768]{1,0:T(8,128)(2,1)} %fusion.20, bf16[512,1536]{1,0:T(8,128)(2,1)S(1)} %get-tuple-element.143), kind=kOutput, calls=%fused_computation.264 | convolution fusion | flops 1207959552 | bytes 7077888 | tf_op jit(solution)/shard_map/dot_general | solution.py:106
  109.9 5.1 %fusion.82 = f32[1536,768]{1,0:T(8,128)} fusion(bf16[512,1536]{1,0:T(8,128)(2,1)} %copy-done.19, bf16[512,768]{1,0:T(8,128)(2,1)S(1)} %convert_element_type.410), kind=kOutput, calls=%fused_computation.265 | convolution fusion | flops 1207959552 | bytes 7077888 | tf_op jit(solution)/shard_map/dot_general | solution.py:106
  116.5 2.9 convolution_convert_fusion
  120.6 2.6 reshape.514
  123.2 10.6 %multiply_reduce_fusion = (f32[2,6,512]{2,1,0:T(8,128)S(1)}, f32[2,6,512,512]{2,3,1,0:T(8,128)}) fusion(f32[2,6,512,512]{2,3,1,0:T(8,128)} %copy-done.1, f32[2,6,512]{2,1,0:T(8,128)S(1)} %copy-done.22, bf16[2,512,6,64]{1,0,3,2:T(2,128)(2,1)} %copy-done.5, bf16[2,512,6,64]{1,0,3,2:T(2,128)(2,1)S(1)} %reshape.514), kind=kOutput, calls=%fused_computation.1 | convolution fusion | flops 412084224 | bytes 26787840 | tf_op jit(solution)/shard_map/rqhd,rkhd->rhqk/dot_general | solution.py:269
  133.8 10.0 %multiply_convert_fusion = bf16[2,6,512,512]{2,3,1,0:T(8,128)(2,1)S(1)} fusion(f32[2,6,512,512]{2,3,1,0:T(8,128)} %get-tuple-element.137, f32[2,6,512,512]{2,3,1,0:T(8,128)} %copy-done.1, f32[2,6,512]{2,1,0:T(8,128)S(1)} %get-tuple-element.136, f32[2,6,512]{2,1,0:T(8,128)S(1)} %copy-done.22), kind=kLoop, calls=%fused_computation | loop fusion | flops 12582912 | bytes 31506432 | tf_op jit(solution)/shard_map/convert_element_type | solution.py:273
  145.1 2.0 fusion.25
  147.1 2.1 convert_reduce_fusion.2
  150.8 1.8 fusion.50
  159.5 3.2 convolution_convert_fusion.2
  169.8 10.2 %collective-permute-done.28 = bf16[192,1536]{1,0:T(8,128)(2,1)} collective-permute-done((bf16[192,1536]{1,0:T(8,128)(2,1)}, bf16[192,1536]{1,0:T(8,128)(2,1)}, u32[]{:S(2)}, u32[]{:S(2)}) %collective-permute-start.28) | collective-permute-done | bytes 589856 | tf_op jit(solution)/shard_map/ppermute | solution.py:24
  185.3 4.2 %add_convert_fusion = bf16[1536,768]{1,0:T(8,128)(2,1)S(1)} fusion(f32[1536,768]{1,0:T(8,128)} %fusion.82, bf16[512,1536]{1,0:T(8,128)(2,1)} %collective-permute-done.59, bf16[512,768]{1,0:T(8,128)(2,1)S(1)} %collective-permute-done.60), kind=kOutput, calls=%fused_computation.13 | convolution fusion | flops 1210318848 | bytes 9437184 | tf_op jit(solution)/shard_map/dot_general | solution.py:106
  192.3 3.2 add_convert_fusion.1
  201.1 5.2 %collective-permute-done.38 = f32[1,6144]{1,0:T(1,128)S(1)} collective-permute-done((f32[1,6144]{1,0:T(1,128)S(1)}, f32[1,6144]{1,0:T(1,128)S(1)}, u32[]{:S(2)}, u32[]{:S(2)}) %collective-permute-start.38) | collective-permute-done | bytes 24608 | tf_op jit(solution)/shard_map/ppermute | solution.py:24
  207.5 2.7 collective-permute-done.39
  211.3 2.8 collective-permute-done.40
  217.4 4.1 %collective-permute-done.41 = f32[1,6144]{1,0:T(1,128)S(1)} collective-permute-done((f32[1,6144]{1,0:T(1,128)S(1)}, f32[1,6144]{1,0:T(1,128)S(1)}, u32[]{:S(2)}, u32[]{:S(2)}) %collective-permute-start.41) | collective-permute-done | bytes 24608 | tf_op jit(solution)/shard_map/ppermute | solution.py:24
  223.5 3.1 collective-permute-done.30
  226.8 4.9 %collective-permute-done.22 = bf16[48,1536]{1,0:T(8,128)(2,1)S(1)} collective-permute-done((bf16[48,1536]{1,0:T(8,128)(2,1)S(1)}, bf16[48,1536]{1,0:T(8,128)(2,1)S(1)}, u32[]{:S(2)}, u32[]{:S(2)}) %collective-permute-start.22) | collective-permute-done | bytes 147488 | tf_op jit(solution)/shard_map/ppermute | solution.py:24
  232.4 6.5 %collective-permute-done.31 = bf16[24,1536]{1,0:T(8,128)(2,1)S(1)} collective-permute-done((bf16[24,1536]{1,0:T(8,128)(2,1)S(1)}, bf16[24,1536]{1,0:T(8,128)(2,1)S(1)}, u32[]{:S(2)}, u32[]{:S(2)}) %collective-permute-start.31) | collective-permute-done | bytes 73760 | tf_op jit(solution)/shard_map/ppermute | solution.py:24
  238.9 6.0 %collective-permute-done.23 = bf16[24,1536]{1,0:T(8,128)(2,1)S(1)} collective-permute-done((bf16[24,1536]{1,0:T(8,128)(2,1)S(1)}, bf16[24,1536]{1,0:T(8,128)(2,1)S(1)}, u32[]{:S(2)}, u32[]{:S(2)}) %collective-permute-start.23) | collective-permute-done | bytes 73760 | tf_op jit(solution)/shard_map/ppermute | solution.py:24
  244.9 5.6 %collective-permute-done.32 = bf16[24,1536]{1,0:T(8,128)(2,1)S(1)} collective-permute-done((bf16[24,1536]{1,0:T(8,128)(2,1)S(1)}, bf16[24,1536]{1,0:T(8,128)(2,1)S(1)}, u32[]{:S(2)}, u32[]{:S(2)}) %collective-permute-start.32) | collective-permute-done | bytes 73760 | tf_op jit(solution)/shard_map/ppermute | solution.py:24
  250.9 5.1 %collective-permute-done.24 = bf16[24,1536]{1,0:T(8,128)(2,1)S(1)} collective-permute-done((bf16[24,1536]{1,0:T(8,128)(2,1)S(1)}, bf16[24,1536]{1,0:T(8,128)(2,1)S(1)}, u32[]{:S(2)}, u32[]{:S(2)}) %collective-permute-start.24) | collective-permute-done | bytes 73760 | tf_op jit(solution)/shard_map/ppermute | solution.py:24
  256.0 2.1 collective-permute-start.25
  259.5 3.1 collective-permute-done.33
  272.0 2.4 collective-permute-done.34
  277.1 3.0 collective-permute-done.63
  280.2 2.9 collective-permute-start.64
  283.5 4.4 %collective-permute-done.72 = bf16[48,768]{1,0:T(8,128)(2,1)S(1)} collective-permute-done((bf16[48,768]{1,0:T(8,128)(2,1)S(1)}, bf16[48,768]{1,0:T(8,128)(2,1)S(1)}, u32[]{:S(2)}, u32[]{:S(2)}) %collective-permute-start.72) | collective-permute-done | bytes 73760 | tf_op jit(solution)/shard_map/ppermute | solution.py:24
  290.4 5.1 %collective-permute-done.73 = bf16[48,768]{1,0:T(8,128)(2,1)S(1)} collective-permute-done((bf16[48,768]{1,0:T(8,128)(2,1)S(1)}, bf16[48,768]{1,0:T(8,128)(2,1)S(1)}, u32[]{:S(2)}, u32[]{:S(2)}) %collective-permute-start.73) | collective-permute-done | bytes 73760 | tf_op jit(solution)/shard_map/ppermute | solution.py:24
  296.4 5.2 %collective-permute-done.65 = bf16[48,768]{1,0:T(8,128)(2,1)S(1)} collective-permute-done((bf16[48,768]{1,0:T(8,128)(2,1)S(1)}, bf16[48,768]{1,0:T(8,128)(2,1)S(1)}, u32[]{:S(2)}, u32[]{:S(2)}) %collective-permute-start.65) | collective-permute-done | bytes 73760 | tf_op jit(solution)/shard_map/ppermute | solution.py:24
  301.6 2.1 collective-permute-start.66
  304.5 4.9 %collective-permute-done.54 = bf16[24,1536]{1,0:T(8,128)(2,1)S(1)} collective-permute-done((bf16[24,1536]{1,0:T(8,128)(2,1)S(1)}, bf16[24,1536]{1,0:T(8,128)(2,1)S(1)}, u32[]{:S(2)}, u32[]{:S(2)}) %collective-permute-start.54) | collective-permute-done | bytes 73760 | tf_op jit(solution)/shard_map/ppermute | solution.py:24
  309.4 2.1 collective-permute-start.46
  311.5 3.1 collective-permute-done.46
  314.7 2.1 collective-permute-start.55
  317.9 2.0 collective-permute-done.55
  322.8 5.1 %collective-permute-done.56 = bf16[48,1536]{1,0:T(8,128)(2,1)S(1)} collective-permute-done((bf16[48,1536]{1,0:T(8,128)(2,1)S(1)}, bf16[48,1536]{1,0:T(8,128)(2,1)S(1)}, u32[]{:S(2)}, u32[]{:S(2)}) %collective-permute-start.56) | collective-permute-done | bytes 147488 | tf_op jit(solution)/shard_map/ppermute | solution.py:24
  327.9 5.0 %collective-permute-done.48 = bf16[48,1536]{1,0:T(8,128)(2,1)S(1)} collective-permute-done((bf16[48,1536]{1,0:T(8,128)(2,1)S(1)}, bf16[48,1536]{1,0:T(8,128)(2,1)S(1)}, u32[]{:S(2)}, u32[]{:S(2)}) %collective-permute-start.48) | collective-permute-done | bytes 147488 | tf_op jit(solution)/shard_map/ppermute | solution.py:24
  335.6 1.9 slice_bitcast_fusion
  340.5 1.9 collective-permute-start.68
  345.9 3.1 collective-permute-done.76
  350.9 2.5 maximum_convert_fusion.2
  353.4 1.9 collective-permute-done.58
  357.1 2.8 maximum_convert_fusion.1
  (404 shorter events, 125.8 us)
Async XLA Ops:
  25.3 18.2 %collective-permute-start.4 = (bf16[512,384]{0,1:T(8,128)(2,1)}, bf16[512,384]{0,1:T(8,128)(2,1)}, u32[]{:S(2)}, u32[]{:S(2)}) collective-permute-start(bf16[512,384]{0,1:T(8,128)(2,1)} %constant_dynamic-slice_fusion.25), channel_id=1, source_target_pairs={{0,1},{1,0},{2,3},{3,2},{4,5},{5,4},{6,7},{7,6},{8,9},{9,8},{10,11... | collective-permute-start | bytes 1179656 | tf_op jit(solution)/shard_map/ppermute | solution.py:24
  25.8 17.7 %collective-permute-start.5 = (bf16[384,768]{1,0:T(8,128)(2,1)S(1)}, bf16[384,768]{1,0:T(8,128)(2,1)}, u32[]{:S(2)}, u32[]{:S(2)}) collective-permute-start(bf16[384,768]{1,0:T(8,128)(2,1)S(1)} %copy-done.21), channel_id=1, source_target_pairs={{0,1},{1,0},{2,3},{3,2},{4,5},{5,4},{6,7},{7,6},{8,9},{9,8},{10,11... | collective-permute-start | bytes 1769480 | tf_op jit(solution)/shard_map/ppermute | solution.py:24
  26.4 16.2 %collective-permute-start.7 = (bf16[1,1536]{1,0:T(2,128)(2,1)}, bf16[1,1536]{1,0:T(2,128)(2,1)}, u32[]{:S(2)}, u32[]{:S(2)}) collective-permute-start(bf16[1,1536]{1,0:T(2,128)(2,1)} %reshape.512), channel_id=1, source_target_pairs={{0,1},{1,0},{2,3},{3,2},{4,5},{5,4},{6,7},{7,6},{8,9},{9,8},{10,11... | collective-permute-start | bytes 9224 | tf_op jit(solution)/shard_map/ppermute | solution.py:24
  26.9 25.6 %collective-permute-start.6 = (bf16[768,1536]{1,0:T(8,128)(2,1)}, bf16[768,1536]{1,0:T(8,128)(2,1)}, u32[]{:S(2)}, u32[]{:S(2)}) collective-permute-start(bf16[768,1536]{1,0:T(8,128)(2,1)} %param.37), channel_id=1, source_target_pairs={{0,1},{1,0},{2,3},{3,2},{4,5},{5,4},{6,7},{7,6},{8,9},{9,8},{10,11... | collective-permute-start | bytes 7077896 | tf_op jit(solution)/shard_map/ppermute | solution.py:24
  27.0 7.6 %collective-permute-start.14 = (s32[8,1]{0,1:T(1,128)}, s32[8,1]{0,1:T(1,128)}, u32[]{:S(2)}, u32[]{:S(2)}) collective-permute-start(s32[8,1]{0,1:T(1,128)} %bitcast.2), channel_id=1, source_target_pairs={{0,2},{2,0},{4,6},{6,4},{8,10},{10,8},{12,14},{14,12},{16,18},{18,... | collective-permute-start | bytes 104 | tf_op jit(solution)/shard_map/ppermute | solution.py:24
  42.6 14.5 %collective-permute-start.8 = (bf16[1536,768]{1,0:T(8,128)(2,1)}, bf16[1536,768]{1,0:T(8,128)(2,1)S(1)}, u32[]{:S(2)}, u32[]{:S(2)}) collective-permute-start(bf16[1536,768]{1,0:T(8,128)(2,1)} %param.39), channel_id=1, source_target_pairs={{0,1},{1,0},{2,3},{3,2},{4,5},{5,4},{6,7},{7,6},{8,9},{9,8},{10,11... | collective-permute-start | bytes 7077896 | tf_op jit(solution)/shard_map/ppermute | solution.py:24
  42.7 23.2 %collective-permute-start = (bf16[8,768]{1,0:T(8,128)(2,1)}, bf16[8,768]{1,0:T(8,128)(2,1)S(1)}, u32[]{:S(2)}, u32[]{:S(2)}) collective-permute-start(bf16[8,768]{1,0:T(8,128)(2,1)} %param.26), channel_id=1, source_target_pairs={{0,2},{2,0},{4,6},{6,4},{8,10},{10,8},{12,14},{14,12},{16,18},{18,... | collective-permute-start | bytes 36872 | tf_op jit(solution)/shard_map/ppermute | solution.py:24
  61.4 16.0 %collective-permute-start.17 = (s32[64,1]{0,1:T(1,128)S(1)}, s32[64,1]{0,1:T(1,128)S(1)}, u32[]{:S(2)}, u32[]{:S(2)}) collective-permute-start(s32[64,1]{0,1:T(1,128)S(1)} %broadcast_select_fusion.5), channel_id=1, source_target_pairs={{0,16},{2,18},{4,20},{6,22},{8,24},{10,26},{12,28},{14,30},{16,0},... | collective-permute-start | bytes 776 | tf_op jit(solution)/shard_map/ppermute | solution.py:24
  74.1 7.4 %collective-permute-start.3 = (bf16[64,768]{1,0:T(8,128)(2,1)S(1)}, bf16[64,768]{1,0:T(8,128)(2,1)S(1)}, u32[]{:S(2)}, u32[]{:S(2)}) collective-permute-start(bf16[64,768]{1,0:T(8,128)(2,1)S(1)} %maximum_select_fusion.29), channel_id=1, source_target_pairs={{0,16},{2,18},{4,20},{6,22},{8,24},{10,26},{12,28},{14,30},{16,0},... | collective-permute-start | bytes 294920 | tf_op jit(solution)/shard_map/ppermute | solution.py:24
  76.6 7.0 %collective-permute-start.13 = (bf16[64,768]{1,0:T(8,128)(2,1)S(1)}, bf16[64,768]{1,0:T(8,128)(2,1)S(1)}, u32[]{:S(2)}, u32[]{:S(2)}) collective-permute-start(bf16[64,768]{1,0:T(8,128)(2,1)S(1)} %maximum_select_fusion.30), channel_id=1, source_target_pairs={{0,16},{2,18},{4,20},{6,22},{8,24},{10,26},{12,28},{14,30},{16,0},... | collective-permute-start | bytes 294920 | tf_op jit(solution)/shard_map/ppermute | solution.py:24
  77.5 112.3 %collective-permute-start.42 = (bf16[512,768]{1,0:T(8,128)(2,1)}, bf16[512,768]{1,0:T(8,128)(2,1)}, u32[]{:S(2)}, u32[]{:S(2)}) collective-permute-start(bf16[512,768]{1,0:T(8,128)(2,1)} %fusion.20), channel_id=1, source_target_pairs={{0,1},{1,0},{2,3},{3,2},{4,5},{5,4},{6,7},{7,6},{8,9},{9,8},{10,11... | collective-permute-start | bytes 2359304 | tf_op jit(solution)/shard_map/ppermute | solution.py:24
  77.5 107.1 %collective-permute-start.59 = (bf16[512,1536]{1,0:T(8,128)(2,1)}, bf16[512,1536]{1,0:T(8,128)(2,1)}, u32[]{:S(2)}, u32[]{:S(2)}) collective-permute-start(bf16[512,1536]{1,0:T(8,128)(2,1)} %get-tuple-element.129), channel_id=1, source_target_pairs={{0,1},{1,0},{2,3},{3,2},{4,5},{5,4},{6,7},{7,6},{8,9},{9,8},{10,11... | collective-permute-start | bytes 4718600 | tf_op jit(solution)/shard_map/ppermute | solution.py:24
  96.4 94.8 %collective-permute-start.37 = (bf16[512,1536]{1,0:T(8,128)(2,1)}, bf16[512,1536]{1,0:T(8,128)(2,1)}, u32[]{:S(2)}, u32[]{:S(2)}) collective-permute-start(bf16[512,1536]{1,0:T(8,128)(2,1)} %fusion.15), channel_id=1, source_target_pairs={{0,1},{1,0},{2,3},{3,2},{4,5},{5,4},{6,7},{7,6},{8,9},{9,8},{10,11... | collective-permute-start | bytes 4718600 | tf_op jit(solution)/shard_map/ppermute | solution.py:24
  102.0 14.5 %collective-permute-start.18 = (bf16[512,768]{1,0:T(8,128)(2,1)}, bf16[512,768]{1,0:T(8,128)(2,1)}, u32[]{:S(2)}, u32[]{:S(2)}) collective-permute-start(bf16[512,768]{1,0:T(8,128)(2,1)} %convert_element_type.413), channel_id=1, source_target_pairs={{0,1},{1,0},{2,3},{3,2},{4,5},{5,4},{6,7},{7,6},{8,9},{9,8},{10,11... | collective-permute-start | bytes 2359304 | tf_op jit(solution)/shard_map/ppermute | solution.py:24
  109.1 7.3 %collective-permute-start.36 = (f32[5,768]{1,0:T(8,128)}, f32[5,768]{1,0:T(8,128)S(1)}, u32[]{:S(2)}, u32[]{:S(2)}) collective-permute-start(f32[5,768]{1,0:T(8,128)} %stack.23), channel_id=1, source_target_pairs={{0,1},{1,0},{2,3},{3,2},{4,5},{5,4},{6,7},{7,6},{8,9},{9,8},{10,11... | collective-permute-start | bytes 46088 | tf_op jit(solution)/shard_map/ppermute | solution.py:24
  163.9 16.0 %collective-permute-start.28 = (bf16[192,1536]{1,0:T(8,128)(2,1)}, bf16[192,1536]{1,0:T(8,128)(2,1)}, u32[]{:S(2)}, u32[]{:S(2)}) collective-permute-start(bf16[192,1536]{1,0:T(8,128)(2,1)} %constant_dynamic-slice_fusion.19), channel_id=1, source_target_pairs={{0,4},{2,6},{4,0},{6,2},{8,12},{10,14},{12,8},{14,10},{16,20},{18,... | collective-permute-start | bytes 1769480 | tf_op jit(solution)/shard_map/ppermute | solution.py:24
  166.3 15.8 %collective-permute-start.20 = (bf16[192,1536]{1,0:T(8,128)(2,1)}, bf16[192,1536]{1,0:T(8,128)(2,1)}, u32[]{:S(2)}, u32[]{:S(2)}) collective-permute-start(bf16[192,1536]{1,0:T(8,128)(2,1)} %constant_dynamic-slice_fusion.23), channel_id=1, source_target_pairs={{0,2},{2,0},{4,6},{6,4},{8,10},{10,8},{12,14},{14,12},{16,18},{18,... | collective-permute-start | bytes 1769480 | tf_op jit(solution)/shard_map/ppermute | solution.py:24
  182.1 15.3 %collective-permute-start.19 = (bf16[512,768]{1,0:T(8,128)(2,1)S(1)}, bf16[512,768]{1,0:T(8,128)(2,1)S(1)}, u32[]{:S(2)}, u32[]{:S(2)}) collective-permute-start(bf16[512,768]{1,0:T(8,128)(2,1)S(1)} %copy-done.20), channel_id=1, source_target_pairs={{0,1},{1,0},{2,3},{3,2},{4,5},{5,4},{6,7},{7,6},{8,9},{9,8},{10,11... | collective-permute-start | bytes 2359304 | tf_op jit(solution)/shard_map/ppermute | solution.py:24
  183.6 31.6 %collective-permute-start.29 = (bf16[96,1536]{1,0:T(8,128)(2,1)S(1)}, bf16[96,1536]{1,0:T(8,128)(2,1)S(1)}, u32[]{:S(2)}, u32[]{:S(2)}) collective-permute-start(bf16[96,1536]{1,0:T(8,128)(2,1)S(1)} %constant_dynamic-slice_fusion.18), channel_id=1, source_target_pairs={{0,2},{2,0},{4,6},{6,4},{8,10},{10,8},{12,14},{14,12},{16,18},{18,... | collective-permute-start | bytes 884744 | tf_op jit(solution)/shard_map/ppermute | solution.py:24
  184.6 32.1 %collective-permute-start.21 = (bf16[96,1536]{1,0:T(8,128)(2,1)S(1)}, bf16[96,1536]{1,0:T(8,128)(2,1)S(1)}, u32[]{:S(2)}, u32[]{:S(2)}) collective-permute-start(bf16[96,1536]{1,0:T(8,128)(2,1)S(1)} %constant_dynamic-slice_fusion.22), channel_id=1, source_target_pairs={{0,4},{2,6},{4,0},{6,2},{8,12},{10,14},{12,8},{14,10},{16,20},{18,... | collective-permute-start | bytes 884744 | tf_op jit(solution)/shard_map/ppermute | solution.py:24
  189.8 66.2 %collective-permute-start.69 = (bf16[384,768]{1,0:T(8,128)(2,1)S(1)}, bf16[384,768]{1,0:T(8,128)(2,1)S(1)}, u32[]{:S(2)}, u32[]{:S(2)}) collective-permute-start(bf16[384,768]{1,0:T(8,128)(2,1)S(1)} %constant_dynamic-slice_fusion.3), channel_id=1, source_target_pairs={{0,4},{2,6},{4,0},{6,2},{8,12},{10,14},{12,8},{14,10},{16,20},{18,... | collective-permute-start | bytes 1769480 | tf_op jit(solution)/shard_map/ppermute | solution.py:24
  191.2 67.1 %collective-permute-start.61 = (bf16[384,768]{1,0:T(8,128)(2,1)S(1)}, bf16[384,768]{1,0:T(8,128)(2,1)S(1)}, u32[]{:S(2)}, u32[]{:S(2)}) collective-permute-start(bf16[384,768]{1,0:T(8,128)(2,1)S(1)} %constant_dynamic-slice_fusion.7), channel_id=1, source_target_pairs={{0,2},{2,0},{4,6},{6,4},{8,10},{10,8},{12,14},{14,12},{16,18},{18,... | collective-permute-start | bytes 1769480 | tf_op jit(solution)/shard_map/ppermute | solution.py:24
  197.4 8.8 %collective-permute-start.38 = (f32[1,6144]{1,0:T(1,128)S(1)}, f32[1,6144]{1,0:T(1,128)S(1)}, u32[]{:S(2)}, u32[]{:S(2)}) collective-permute-start(f32[1,6144]{1,0:T(1,128)S(1)} %bitcast.123), channel_id=1, source_target_pairs={{0,2},{2,0},{4,6},{6,4},{8,10},{10,8},{12,14},{14,12},{16,18},{18,... | collective-permute-start | bytes 73736 | tf_op jit(solution)/shard_map/ppermute | solution.py:24
  214.1 51.2 %collective-permute-start.51 = (bf16[192,1536]{1,0:T(8,128)(2,1)S(1)}, bf16[192,1536]{1,0:T(8,128)(2,1)S(1)}, u32[]{:S(2)}, u32[]{:S(2)}) collective-permute-start(bf16[192,1536]{1,0:T(8,128)(2,1)S(1)} %constant_dynamic-slice_fusion.11), channel_id=1, source_target_pairs={{0,4},{2,6},{4,0},{6,2},{8,12},{10,14},{12,8},{14,10},{16,20},{18,... | collective-permute-start | bytes 1769480 | tf_op jit(solution)/shard_map/ppermute | solution.py:24
  215.2 51.4 %collective-permute-start.43 = (bf16[192,1536]{1,0:T(8,128)(2,1)S(1)}, bf16[192,1536]{1,0:T(8,128)(2,1)S(1)}, u32[]{:S(2)}, u32[]{:S(2)}) collective-permute-start(bf16[192,1536]{1,0:T(8,128)(2,1)S(1)} %constant_dynamic-slice_fusion.15), channel_id=1, source_target_pairs={{0,2},{2,0},{4,6},{6,4},{8,10},{10,8},{12,14},{14,12},{16,18},{18,... | collective-permute-start | bytes 1769480 | tf_op jit(solution)/shard_map/ppermute | solution.py:24
  221.5 5.1 %collective-permute-start.30 = (bf16[48,1536]{1,0:T(8,128)(2,1)S(1)}, bf16[48,1536]{1,0:T(8,128)(2,1)S(1)}, u32[]{:S(2)}, u32[]{:S(2)}) collective-permute-start(bf16[48,1536]{1,0:T(8,128)(2,1)S(1)} %constant_dynamic-slice_fusion.17), channel_id=1, source_target_pairs={{0,8},{2,10},{4,12},{6,14},{8,0},{10,2},{12,4},{14,6},{16,24},{18,... | collective-permute-start | bytes 442376 | tf_op jit(solution)/shard_map/ppermute | solution.py:24
  226.6 5.1 %collective-permute-start.22 = (bf16[48,1536]{1,0:T(8,128)(2,1)S(1)}, bf16[48,1536]{1,0:T(8,128)(2,1)S(1)}, u32[]{:S(2)}, u32[]{:S(2)}) collective-permute-start(bf16[48,1536]{1,0:T(8,128)(2,1)S(1)} %constant_dynamic-slice_fusion.21), channel_id=1, source_target_pairs={{0,8},{2,10},{4,12},{6,14},{8,0},{10,2},{12,4},{14,6},{16,24},{18,... | collective-permute-start | bytes 442376 | tf_op jit(solution)/shard_map/ppermute | solution.py:24
  231.8 7.2 %collective-permute-start.31 = (bf16[24,1536]{1,0:T(8,128)(2,1)S(1)}, bf16[24,1536]{1,0:T(8,128)(2,1)S(1)}, u32[]{:S(2)}, u32[]{:S(2)}) collective-permute-start(bf16[24,1536]{1,0:T(8,128)(2,1)S(1)} %constant_dynamic-slice_fusion.16), channel_id=1, source_target_pairs={{0,16},{2,18},{4,20},{6,22},{8,24},{10,26},{12,28},{14,30},{16,0},... | collective-permute-start | bytes 221192 | tf_op jit(solution)/shard_map/ppermute | solution.py:24
  238.9 6.0 %collective-permute-start.23 = (bf16[24,1536]{1,0:T(8,128)(2,1)S(1)}, bf16[24,1536]{1,0:T(8,128)(2,1)S(1)}, u32[]{:S(2)}, u32[]{:S(2)}) collective-permute-start(bf16[24,1536]{1,0:T(8,128)(2,1)S(1)} %constant_dynamic-slice_fusion.20), channel_id=1, source_target_pairs={{0,16},{2,18},{4,20},{6,22},{8,24},{10,26},{12,28},{14,30},{16,0},... | collective-permute-start | bytes 221192 | tf_op jit(solution)/shard_map/ppermute | solution.py:24
  244.9 5.6 %collective-permute-start.32 = (bf16[24,1536]{1,0:T(8,128)(2,1)S(1)}, bf16[24,1536]{1,0:T(8,128)(2,1)S(1)}, u32[]{:S(2)}, u32[]{:S(2)}) collective-permute-start(bf16[24,1536]{1,0:T(8,128)(2,1)S(1)} %add_convert_fusion.28), channel_id=1, source_target_pairs={{0,16},{2,18},{4,20},{6,22},{8,24},{10,26},{12,28},{14,30},{16,0},... | collective-permute-start | bytes 221192 | tf_op jit(solution)/shard_map/ppermute | solution.py:24
  250.5 5.4 %collective-permute-start.24 = (bf16[24,1536]{1,0:T(8,128)(2,1)S(1)}, bf16[24,1536]{1,0:T(8,128)(2,1)S(1)}, u32[]{:S(2)}, u32[]{:S(2)}) collective-permute-start(bf16[24,1536]{1,0:T(8,128)(2,1)S(1)} %add_convert_fusion.29), channel_id=1, source_target_pairs={{0,16},{2,18},{4,20},{6,22},{8,24},{10,26},{12,28},{14,30},{16,0},... | collective-permute-start | bytes 221192 | tf_op jit(solution)/shard_map/ppermute | solution.py:24
  256.0 6.6 %collective-permute-start.33 = (bf16[48,1536]{1,0:T(8,128)(2,1)S(1)}, bf16[48,1536]{1,0:T(8,128)(2,1)S(1)}, u32[]{:S(2)}, u32[]{:S(2)}) collective-permute-start(bf16[48,1536]{1,0:T(8,128)(2,1)S(1)} %maximum_select_fusion.24), channel_id=1, source_target_pairs={{0,8},{2,10},{4,12},{6,14},{8,0},{10,2},{12,4},{14,6},{16,24},{18,... | collective-permute-start | bytes 442376 | tf_op jit(solution)/shard_map/ppermute | solution.py:24
  256.0 8.2 %collective-permute-start.25 = (bf16[48,1536]{1,0:T(8,128)(2,1)S(1)}, bf16[48,1536]{1,0:T(8,128)(2,1)S(1)}, u32[]{:S(2)}, u32[]{:S(2)}) collective-permute-start(bf16[48,1536]{1,0:T(8,128)(2,1)S(1)} %maximum_select_fusion.23), channel_id=1, source_target_pairs={{0,8},{2,10},{4,12},{6,14},{8,0},{10,2},{12,4},{14,6},{16,24},{18,... | collective-permute-start | bytes 442376 | tf_op jit(solution)/shard_map/ppermute | solution.py:24
  258.3 9.9 %collective-permute-start.70 = (bf16[192,768]{1,0:T(8,128)(2,1)S(1)}, bf16[192,768]{1,0:T(8,128)(2,1)S(1)}, u32[]{:S(2)}, u32[]{:S(2)}) collective-permute-start(bf16[192,768]{1,0:T(8,128)(2,1)S(1)} %constant_dynamic-slice_fusion.2), channel_id=1, source_target_pairs={{0,2},{2,0},{4,6},{6,4},{8,10},{10,8},{12,14},{14,12},{16,18},{18,... | collective-permute-start | bytes 884744 | tf_op jit(solution)/shard_map/ppermute | solution.py:24
  262.6 8.0 %collective-permute-start.62 = (bf16[192,768]{1,0:T(8,128)(2,1)S(1)}, bf16[192,768]{1,0:T(8,128)(2,1)S(1)}, u32[]{:S(2)}, u32[]{:S(2)}) collective-permute-start(bf16[192,768]{1,0:T(8,128)(2,1)S(1)} %constant_dynamic-slice_fusion.6), channel_id=1, source_target_pairs={{0,4},{2,6},{4,0},{6,2},{8,12},{10,14},{12,8},{14,10},{16,20},{18,... | collective-permute-start | bytes 884744 | tf_op jit(solution)/shard_map/ppermute | solution.py:24
  264.2 10.1 %collective-permute-start.34 = (bf16[96,1536]{1,0:T(8,128)(2,1)S(1)}, bf16[96,1536]{1,0:T(8,128)(2,1)S(1)}, u32[]{:S(2)}, u32[]{:S(2)}) collective-permute-start(bf16[96,1536]{1,0:T(8,128)(2,1)S(1)} %maximum_select_fusion.14), channel_id=1, source_target_pairs={{0,2},{2,0},{4,6},{6,4},{8,10},{10,8},{12,14},{14,12},{16,18},{18,... | collective-permute-start | bytes 884744 | tf_op jit(solution)/shard_map/ppermute | solution.py:24
  265.3 9.4 %collective-permute-start.26 = (bf16[96,1536]{1,0:T(8,128)(2,1)S(1)}, bf16[96,1536]{1,0:T(8,128)(2,1)S(1)}, u32[]{:S(2)}, u32[]{:S(2)}) collective-permute-start(bf16[96,1536]{1,0:T(8,128)(2,1)S(1)} %maximum_select_fusion.13), channel_id=1, source_target_pairs={{0,4},{2,6},{4,0},{6,2},{8,12},{10,14},{12,8},{14,10},{16,20},{18,... | collective-permute-start | bytes 884744 | tf_op jit(solution)/shard_map/ppermute | solution.py:24
  266.6 13.6 %collective-permute-start.52 = (bf16[96,1536]{1,0:T(8,128)(2,1)S(1)}, bf16[96,1536]{1,0:T(8,128)(2,1)S(1)}, u32[]{:S(2)}, u32[]{:S(2)}) collective-permute-start(bf16[96,1536]{1,0:T(8,128)(2,1)S(1)} %constant_dynamic-slice_fusion.10), channel_id=1, source_target_pairs={{0,2},{2,0},{4,6},{6,4},{8,10},{10,8},{12,14},{14,12},{16,18},{18,... | collective-permute-start | bytes 884744 | tf_op jit(solution)/shard_map/ppermute | solution.py:24
  268.3 15.0 %collective-permute-start.44 = (bf16[96,1536]{1,0:T(8,128)(2,1)S(1)}, bf16[96,1536]{1,0:T(8,128)(2,1)S(1)}, u32[]{:S(2)}, u32[]{:S(2)}) collective-permute-start(bf16[96,1536]{1,0:T(8,128)(2,1)S(1)} %constant_dynamic-slice_fusion.14), channel_id=1, source_target_pairs={{0,4},{2,6},{4,0},{6,2},{8,12},{10,14},{12,8},{14,10},{16,20},{18,... | collective-permute-start | bytes 884744 | tf_op jit(solution)/shard_map/ppermute | solution.py:24
  270.6 5.4 %collective-permute-start.71 = (bf16[96,768]{1,0:T(8,128)(2,1)S(1)}, bf16[96,768]{1,0:T(8,128)(2,1)S(1)}, u32[]{:S(2)}, u32[]{:S(2)}) collective-permute-start(bf16[96,768]{1,0:T(8,128)(2,1)S(1)} %constant_dynamic-slice_fusion.1), channel_id=1, source_target_pairs={{0,8},{2,10},{4,12},{6,14},{8,0},{10,2},{12,4},{14,6},{16,24},{18,... | collective-permute-start | bytes 442376 | tf_op jit(solution)/shard_map/ppermute | solution.py:24
  274.3 5.8 %collective-permute-start.63 = (bf16[96,768]{1,0:T(8,128)(2,1)S(1)}, bf16[96,768]{1,0:T(8,128)(2,1)S(1)}, u32[]{:S(2)}, u32[]{:S(2)}) collective-permute-start(bf16[96,768]{1,0:T(8,128)(2,1)S(1)} %constant_dynamic-slice_fusion.5), channel_id=1, source_target_pairs={{0,8},{2,10},{4,12},{6,14},{8,0},{10,2},{12,4},{14,6},{16,24},{18,... | collective-permute-start | bytes 442376 | tf_op jit(solution)/shard_map/ppermute | solution.py:24
  274.7 58.5 %collective-permute-start.35 = (bf16[192,1536]{1,0:T(8,128)(2,1)S(1)}, bf16[192,1536]{1,0:T(8,128)(2,1)S(1)}, u32[]{:S(2)}, u32[]{:S(2)}) collective-permute-start(bf16[192,1536]{1,0:T(8,128)(2,1)S(1)} %maximum_select_fusion.8), channel_id=1, source_target_pairs={{0,4},{2,6},{4,0},{6,2},{8,12},{10,14},{12,8},{14,10},{16,20},{18,... | collective-permute-start | bytes 1769480 | tf_op jit(solution)/shard_map/ppermute | solution.py:24
  276.0 58.6 %collective-permute-start.27 = (bf16[192,1536]{1,0:T(8,128)(2,1)S(1)}, bf16[192,1536]{1,0:T(8,128)(2,1)S(1)}, u32[]{:S(2)}, u32[]{:S(2)}) collective-permute-start(bf16[192,1536]{1,0:T(8,128)(2,1)S(1)} %maximum_select_fusion.7), channel_id=1, source_target_pairs={{0,2},{2,0},{4,6},{6,4},{8,10},{10,8},{12,14},{14,12},{16,18},{18,... | collective-permute-start | bytes 1769480 | tf_op jit(solution)/shard_map/ppermute | solution.py:24
  280.1 7.7 %collective-permute-start.72 = (bf16[48,768]{1,0:T(8,128)(2,1)S(1)}, bf16[48,768]{1,0:T(8,128)(2,1)S(1)}, u32[]{:S(2)}, u32[]{:S(2)}) collective-permute-start(bf16[48,768]{1,0:T(8,128)(2,1)S(1)} %constant_dynamic-slice_fusion), channel_id=1, source_target_pairs={{0,16},{2,18},{4,20},{6,22},{8,24},{10,26},{12,28},{14,30},{16,0},... | collective-permute-start | bytes 221192 | tf_op jit(solution)/shard_map/ppermute | solution.py:24
  280.2 8.4 %collective-permute-start.64 = (bf16[48,768]{1,0:T(8,128)(2,1)S(1)}, bf16[48,768]{1,0:T(8,128)(2,1)S(1)}, u32[]{:S(2)}, u32[]{:S(2)}) collective-permute-start(bf16[48,768]{1,0:T(8,128)(2,1)S(1)} %constant_dynamic-slice_fusion.4), channel_id=1, source_target_pairs={{0,16},{2,18},{4,20},{6,22},{8,24},{10,26},{12,28},{14,30},{16,0},... | collective-permute-start | bytes 221192 | tf_op jit(solution)/shard_map/ppermute | solution.py:24
  283.3 18.3 %collective-permute-start.53 = (bf16[48,1536]{1,0:T(8,128)(2,1)S(1)}, bf16[48,1536]{1,0:T(8,128)(2,1)S(1)}, u32[]{:S(2)}, u32[]{:S(2)}) collective-permute-start(bf16[48,1536]{1,0:T(8,128)(2,1)S(1)} %constant_dynamic-slice_fusion.9), channel_id=1, source_target_pairs={{0,8},{2,10},{4,12},{6,14},{8,0},{10,2},{12,4},{14,6},{16,24},{18,... | collective-permute-start | bytes 442376 | tf_op jit(solution)/shard_map/ppermute | solution.py:24
  287.8 16.1 %collective-permute-start.45 = (bf16[48,1536]{1,0:T(8,128)(2,1)S(1)}, bf16[48,1536]{1,0:T(8,128)(2,1)S(1)}, u32[]{:S(2)}, u32[]{:S(2)}) collective-permute-start(bf16[48,1536]{1,0:T(8,128)(2,1)S(1)} %constant_dynamic-slice_fusion.13), channel_id=1, source_target_pairs={{0,8},{2,10},{4,12},{6,14},{8,0},{10,2},{12,4},{14,6},{16,24},{18,... | collective-permute-start | bytes 442376 | tf_op jit(solution)/shard_map/ppermute | solution.py:24
  288.6 6.9 %collective-permute-start.73 = (bf16[48,768]{1,0:T(8,128)(2,1)S(1)}, bf16[48,768]{1,0:T(8,128)(2,1)S(1)}, u32[]{:S(2)}, u32[]{:S(2)}) collective-permute-start(bf16[48,768]{1,0:T(8,128)(2,1)S(1)} %add_convert_fusion.24), channel_id=1, source_target_pairs={{0,16},{2,18},{4,20},{6,22},{8,24},{10,26},{12,28},{14,30},{16,0},... | collective-permute-start | bytes 221192 | tf_op jit(solution)/shard_map/ppermute | solution.py:24
  295.5 6.0 %collective-permute-start.65 = (bf16[48,768]{1,0:T(8,128)(2,1)S(1)}, bf16[48,768]{1,0:T(8,128)(2,1)S(1)}, u32[]{:S(2)}, u32[]{:S(2)}) collective-permute-start(bf16[48,768]{1,0:T(8,128)(2,1)S(1)} %add_convert_fusion.25), channel_id=1, source_target_pairs={{0,16},{2,18},{4,20},{6,22},{8,24},{10,26},{12,28},{14,30},{16,0},... | collective-permute-start | bytes 221192 | tf_op jit(solution)/shard_map/ppermute | solution.py:24
  301.5 15.3 %collective-permute-start.74 = (bf16[96,768]{1,0:T(8,128)(2,1)S(1)}, bf16[96,768]{1,0:T(8,128)(2,1)S(1)}, u32[]{:S(2)}, u32[]{:S(2)}) collective-permute-start(bf16[96,768]{1,0:T(8,128)(2,1)S(1)} %maximum_select_fusion.28), channel_id=1, source_target_pairs={{0,8},{2,10},{4,12},{6,14},{8,0},{10,2},{12,4},{14,6},{16,24},{18,... | collective-permute-start | bytes 442376 | tf_op jit(solution)/shard_map/ppermute | solution.py:24
  301.6 16.2 %collective-permute-start.66 = (bf16[96,768]{1,0:T(8,128)(2,1)S(1)}, bf16[96,768]{1,0:T(8,128)(2,1)S(1)}, u32[]{:S(2)}, u32[]{:S(2)}) collective-permute-start(bf16[96,768]{1,0:T(8,128)(2,1)S(1)} %maximum_select_fusion.27), channel_id=1, source_target_pairs={{0,8},{2,10},{4,12},{6,14},{8,0},{10,2},{12,4},{14,6},{16,24},{18,... | collective-permute-start | bytes 442376 | tf_op jit(solution)/shard_map/ppermute | solution.py:24
  304.0 5.4 %collective-permute-start.54 = (bf16[24,1536]{1,0:T(8,128)(2,1)S(1)}, bf16[24,1536]{1,0:T(8,128)(2,1)S(1)}, u32[]{:S(2)}, u32[]{:S(2)}) collective-permute-start(bf16[24,1536]{1,0:T(8,128)(2,1)S(1)} %constant_dynamic-slice_fusion.8), channel_id=1, source_target_pairs={{0,16},{2,18},{4,20},{6,22},{8,24},{10,26},{12,28},{14,30},{16,0},... | collective-permute-start | bytes 221192 | tf_op jit(solution)/shard_map/ppermute | solution.py:24
  309.4 5.3 %collective-permute-start.46 = (bf16[24,1536]{1,0:T(8,128)(2,1)S(1)}, bf16[24,1536]{1,0:T(8,128)(2,1)S(1)}, u32[]{:S(2)}, u32[]{:S(2)}) collective-permute-start(bf16[24,1536]{1,0:T(8,128)(2,1)S(1)} %constant_dynamic-slice_fusion.12), channel_id=1, source_target_pairs={{0,16},{2,18},{4,20},{6,22},{8,24},{10,26},{12,28},{14,30},{16,0},... | collective-permute-start | bytes 221192 | tf_op jit(solution)/shard_map/ppermute | solution.py:24
  314.7 5.3 %collective-permute-start.55 = (bf16[24,1536]{1,0:T(8,128)(2,1)S(1)}, bf16[24,1536]{1,0:T(8,128)(2,1)S(1)}, u32[]{:S(2)}, u32[]{:S(2)}) collective-permute-start(bf16[24,1536]{1,0:T(8,128)(2,1)S(1)} %add_convert_fusion.26), channel_id=1, source_target_pairs={{0,16},{2,18},{4,20},{6,22},{8,24},{10,26},{12,28},{14,30},{16,0},... | collective-permute-start | bytes 221192 | tf_op jit(solution)/shard_map/ppermute | solution.py:24
  316.8 5.9 %collective-permute-start.47 = (bf16[24,1536]{1,0:T(8,128)(2,1)S(1)}, bf16[24,1536]{1,0:T(8,128)(2,1)S(1)}, u32[]{:S(2)}, u32[]{:S(2)}) collective-permute-start(bf16[24,1536]{1,0:T(8,128)(2,1)S(1)} %add_convert_fusion.27), channel_id=1, source_target_pairs={{0,16},{2,18},{4,20},{6,22},{8,24},{10,26},{12,28},{14,30},{16,0},... | collective-permute-start | bytes 221192 | tf_op jit(solution)/shard_map/ppermute | solution.py:24
  317.8 21.1 %collective-permute-start.75 = (bf16[192,768]{1,0:T(8,128)(2,1)S(1)}, bf16[192,768]{1,0:T(8,128)(2,1)S(1)}, u32[]{:S(2)}, u32[]{:S(2)}) collective-permute-start(bf16[192,768]{1,0:T(8,128)(2,1)S(1)} %maximum_select_fusion.18), channel_id=1, source_target_pairs={{0,2},{2,0},{4,6},{6,4},{8,10},{10,8},{12,14},{14,12},{16,18},{18,... | collective-permute-start | bytes 884744 | tf_op jit(solution)/shard_map/ppermute | solution.py:24
  319.9 20.4 %collective-permute-start.67 = (bf16[192,768]{1,0:T(8,128)(2,1)S(1)}, bf16[192,768]{1,0:T(8,128)(2,1)S(1)}, u32[]{:S(2)}, u32[]{:S(2)}) collective-permute-start(bf16[192,768]{1,0:T(8,128)(2,1)S(1)} %maximum_select_fusion.17), channel_id=1, source_target_pairs={{0,4},{2,6},{4,0},{6,2},{8,12},{10,14},{12,8},{14,10},{16,20},{18,... | collective-permute-start | bytes 884744 | tf_op jit(solution)/shard_map/ppermute | solution.py:24
  322.7 5.1 %collective-permute-start.56 = (bf16[48,1536]{1,0:T(8,128)(2,1)S(1)}, bf16[48,1536]{1,0:T(8,128)(2,1)S(1)}, u32[]{:S(2)}, u32[]{:S(2)}) collective-permute-start(bf16[48,1536]{1,0:T(8,128)(2,1)S(1)} %maximum_select_fusion.26), channel_id=1, source_target_pairs={{0,8},{2,10},{4,12},{6,14},{8,0},{10,2},{12,4},{14,6},{16,24},{18,... | collective-permute-start | bytes 442376 | tf_op jit(solution)/shard_map/ppermute | solution.py:24
  333.0 9.4 %collective-permute-start.57 = (bf16[96,1536]{1,0:T(8,128)(2,1)S(1)}, bf16[96,1536]{1,0:T(8,128)(2,1)}, u32[]{:S(2)}, u32[]{:S(2)}) collective-permute-start(bf16[96,1536]{1,0:T(8,128)(2,1)S(1)} %maximum_select_fusion.16), channel_id=1, source_target_pairs={{0,2},{2,0},{4,6},{6,4},{8,10},{10,8},{12,14},{14,12},{16,18},{18,... | collective-permute-start | bytes 884744 | tf_op jit(solution)/shard_map/ppermute | solution.py:24
  333.3 11.4 %collective-permute-start.49 = (bf16[96,1536]{1,0:T(8,128)(2,1)S(1)}, bf16[96,1536]{1,0:T(8,128)(2,1)}, u32[]{:S(2)}, u32[]{:S(2)}) collective-permute-start(bf16[96,1536]{1,0:T(8,128)(2,1)S(1)} %maximum_select_fusion.15), channel_id=1, source_target_pairs={{0,4},{2,6},{4,0},{6,2},{8,12},{10,14},{12,8},{14,10},{16,20},{18,... | collective-permute-start | bytes 884744 | tf_op jit(solution)/shard_map/ppermute | solution.py:24
  339.1 9.9 %collective-permute-start.76 = (bf16[384,768]{1,0:T(8,128)(2,1)S(1)}, bf16[384,768]{1,0:T(8,128)(2,1)S(1)}, u32[]{:S(2)}, u32[]{:S(2)}) collective-permute-start(bf16[384,768]{1,0:T(8,128)(2,1)S(1)} %maximum_select_fusion.12), channel_id=1, source_target_pairs={{0,4},{2,6},{4,0},{6,2},{8,12},{10,14},{12,8},{14,10},{16,20},{18,... | collective-permute-start | bytes 1769480 | tf_op jit(solution)/shard_map/ppermute | solution.py:24
  340.5 9.9 %collective-permute-start.68 = (bf16[384,768]{1,0:T(8,128)(2,1)S(1)}, bf16[384,768]{1,0:T(8,128)(2,1)S(1)}, u32[]{:S(2)}, u32[]{:S(2)}) collective-permute-start(bf16[384,768]{1,0:T(8,128)(2,1)S(1)} %maximum_select_fusion.11), channel_id=1, source_target_pairs={{0,2},{2,0},{4,6},{6,4},{8,10},{10,8},{12,14},{14,12},{16,18},{18,... | collective-permute-start | bytes 1769480 | tf_op jit(solution)/shard_map/ppermute | solution.py:24
  343.5 11.8 %collective-permute-start.58 = (bf16[192,1536]{1,0:T(8,128)(2,1)S(1)}, bf16[192,1536]{1,0:T(8,128)(2,1)S(1)}, u32[]{:S(2)}, u32[]{:S(2)}) collective-permute-start(bf16[192,1536]{1,0:T(8,128)(2,1)S(1)} %maximum_select_fusion.10), channel_id=1, source_target_pairs={{0,4},{2,6},{4,0},{6,2},{8,12},{10,14},{12,8},{14,10},{16,20},{18,... | collective-permute-start | bytes 1769480 | tf_op jit(solution)/shard_map/ppermute | solution.py:24
  345.8 10.9 %collective-permute-start.50 = (bf16[192,1536]{1,0:T(8,128)(2,1)S(1)}, bf16[192,1536]{1,0:T(8,128)(2,1)S(1)}, u32[]{:S(2)}, u32[]{:S(2)}) collective-permute-start(bf16[192,1536]{1,0:T(8,128)(2,1)S(1)} %maximum_select_fusion.9), channel_id=1, source_target_pairs={{0,2},{2,0},{4,6},{6,4},{8,10},{10,8},{12,14},{14,12},{16,18},{18,... | collective-permute-start | bytes 1769480 | tf_op jit(solution)/shard_map/ppermute | solution.py:24
  (65 other events, 339.9 us)

commit v2 on v1

v2 whole, which is shorter than its diff:
```python
import functools
import math

import jax
import jax.numpy as jnp
from jax import lax
from jax.experimental import pallas as pl
from jax.experimental.pallas import tpu as pltpu
from jax.sharding import PartitionSpec as P

D = 768
HD = 64
LANES = 128

norm_eps = 1e-05
neg_large = -1e30
root_half = 0.7071067811865476
inv_root_tau = 0.3989422804014327
log2_e = 1.4426950408889634

f32, bf16 = jnp.float32, jnp.bfloat16
COSTS = dict(
    attend_far=9, attend_near=9, forward=17, loss_back=6, unit_back_far=6, unit_back_near=6, down_gradient=7,
    up_gradient=7, first_back=9, attend_back_near=10, attend_back_far=10, head_gradients=8, add_halves=3,
    add_chunks=2, add_four=2, join_chunks=2, join_quarters=2, finish_down=4, finish_up=4, finish_heads=4,
)
FLOPS = int(2.3e9)
VMEM_GRANT = 63 << 20
SMALL = 16


def bits_of(axis):
    return lax.axis_size(axis).bit_length() - 1


def flip_by(value, axis, mask):
    size = lax.axis_size(axis)
    return lax.ppermute(value, axis, [(i, i ^ mask) for i in range(size)])


def swap(value):
    return flip_by(value, "tensor", 1)


def own_bit(axis, bit):
    return (lax.axis_index(axis) >> bit) & 1


def join(value, other, high):
    return jnp.where(
        high == 1, jnp.concatenate([other, value], 0), jnp.concatenate([value, other], 0)
    )


def gather_dp(value):
    for bit in range(bits_of("dp")):
        value = join(value, flip_by(value, "dp", 1 << bit), own_bit("dp", bit))
    return value


def gather_all(value):
    value = join(value, swap(value), own_bit("tensor", 0))
    return gather_dp(value)


def dot(left, right):
    return jnp.dot(left, right, preferred_element_type=f32)


def dot_t(left, right):
    return lax.dot_general(left, right, (((1,), (1,)), ((), ())), preferred_element_type=f32)


def t_dot(left, right):
    return lax.dot_general(left, right, (((0,), (0,)), ((), ())), preferred_element_type=f32)


class Late:
    def __init__(self, source, held, semaphore):
        self.held, self.waited = held, False
        self.shape, self.dtype = held.shape, held.dtype
        self.copy = pltpu.make_async_copy(source, held, semaphore)
        self.copy.start()

    def wait(self):
        if not self.waited:
            self.copy.wait()
        self.waited = True
        return self.held


class Early:
    def __init__(self, held, target, semaphore):
        self.held, self.target, self.semaphore, self.sent = held, target, semaphore, False
        self.shape, self.dtype = held.shape, held.dtype

    def __getitem__(self, at):
        return self.held[at]

    def __setitem__(self, at, value):
        self.held[at] = value

    def send(self, *at):
        source, target = (self.held.at[at], self.target.at[at]) if at else (self.held, self.target)
        pltpu.make_async_copy(source, target, self.semaphore).start()
        self.sent = True

    def finish(self):
        if not self.sent:
            self.send()
        pltpu.make_async_copy(self.held, self.target, self.semaphore).wait()


def ready(*values):
    return [value.wait() if isinstance(value, Late) else value for value in values]


def call(kernel, name, outs, *args, scratch=(), late=(), early=(), order=None, parts=None):
    parts, after = parts or {}, order or []
    count, waits, made = len(args), len(after), len(outs)
    held = [
        pltpu.VMEM(parts[i][0] if i in parts else args[i].shape, args[i].dtype) for i in late
    ] + [pltpu.VMEM(*outs[i]) for i in early]

    def body(*refs):
        inputs = list(refs[:count])
        results = list(refs[count + waits : count + waits + made])
        rest = refs[count + waits + made :]
        scratches, rest = rest[: len(scratch)], rest[len(scratch) :]
        for k, i in enumerate(late):
            source = parts[i][1](inputs[0], inputs[i]) if i in parts else inputs[i]
            inputs[i] = Late(source, rest[k], rest[-1].at[k])
        for k, i in enumerate(early):
            k += len(late)
            results[i] = Early(rest[k], results[i], rest[-1].at[k])
        kernel(*inputs, *results, *scratches)
        for i in late:
            inputs[i].wait()
        for i in early:
            results[i].finish()

    specs = [pl.BlockSpec(memory_space=pltpu.SMEM)]
    specs += [pl.BlockSpec(memory_space=pl.ANY if i in late else pltpu.VMEM) for i in range(1, count)]
    specs += [pl.BlockSpec(memory_space=pl.ANY)] * waits
    own = [pltpu.SemaphoreType.DMA((len(held),))] if held else []
    made_by = pl.pallas_call(
        body,
        name=name,
        out_shape=[jax.ShapeDtypeStruct(s, t) for s, t in outs],
        in_specs=specs,
        out_specs=[pl.BlockSpec(memory_space=pl.ANY if i in early else pltpu.VMEM) for i in range(made)],
        scratch_shapes=[*scratch, *held, *own],
        compiler_params=pltpu.CompilerParams(vmem_limit_bytes=VMEM_GRANT),
        cost_estimate=pl.CostEstimate(
            flops=int(COSTS[name] * FLOPS), bytes_accessed=1, transcendentals=0
        ),
    )(*args, *after)
    if order is not None:
        order[:] = [made_by[-1]]
    return made_by


def rows_at(index, size):
    return pl.ds(pl.multiple_of(index * size, size), size)


def add_low(left, right):
    return (left.astype(f32) + right.astype(f32)).astype(bf16)


BX, BY, BZ, BT, BD, PLACES = range(6)


def add_halves(info, keep_a, came_a, keep_b, came_b, send_a, kept_a, send_b, kept_b):
    quarter = keep_b.shape[0] // 2
    for bit, keep, came, send, kept in (
        (info[BY], keep_a, came_a, send_a, kept_a),
        (info[BX], keep_b, came_b, send_b, kept_b),
    ):
        mine, other = rows_at(bit, quarter), rows_at(1 - bit, quarter)
        send[:quarter] = add_low(keep[other], came[other])
        kept[:quarter] = add_low(keep[mine], came[mine])
        if keep.shape[0] > 2 * quarter:
            extra = add_low(keep[2 * quarter :], came[2 * quarter :])
            send[quarter:] = extra
            kept[quarter:] = extra


def add_chunks(info, keep_a, came_a, keep_b, came_b, own, one, two, three):
    quarter = keep_b.shape[0]
    chunk = quarter // 4
    for step, out in enumerate((own, one, two, three)):
        at = rows_at(info[BZ] ^ step, chunk)
        out[:chunk] = add_low(keep_a[at], came_a[at])
        out[chunk : 2 * chunk] = add_low(keep_b[at], came_b[at])
        if keep_a.shape[0] > quarter:
            out[2 * chunk :] = add_low(keep_a[quarter:], came_a[quarter:])


def add_four(info, own, one, two, three, total):
    total[...] = (
        (own[...].astype(f32) + one[...].astype(f32))
        + (two[...].astype(f32) + three[...].astype(f32))
    ).astype(bf16)


def join_chunks(info, own, one, two, three, quarter_a, quarter_b):
    chunk = quarter_a.shape[0] // 4
    for step, part in enumerate((own, one, two, three)):
        at = rows_at(info[BZ] ^ step, chunk)
        quarter_a[at] = part[:chunk]
        quarter_b[at] = part[chunk : 2 * chunk]


def join_quarters(info, own_a, came_a, own_b, came_b, half_a, half_b):
    size = own_a.shape[0]
    for bit, own, came, half in (
        (info[BY], own_a, came_a, half_a),
        (info[BX], own_b, came_b, half_b),
    ):
        half[rows_at(bit, size)] = own[...]
        half[rows_at(1 - bit, size)] = came[...]


def finish_down(info, own_a, came_a, own_b, came_b, out):
    size = own_a.shape[0]
    for part, bit, own, came in ((0, info[BX], own_a, came_a), (1, info[BY], own_b, came_b)):
        out[rows_at(2 * part + bit, size)] = own[...].astype(f32)
        out[rows_at(2 * part + 1 - bit, size)] = came[...].astype(f32)


def finish_up(info, own_a, came_a, own_b, came_b, out):
    size, width = own_a.shape
    for part, bit, own, came in ((0, info[BX], own_a, came_a), (1, info[BY], own_b, came_b)):
        columns = pl.ds(part * width, width)
        out[rows_at(bit, size), columns] = own[...].astype(f32)
        out[rows_at(1 - bit, size), columns] = came[...].astype(f32)


def finish_heads(info, own_a, came_a, own_b, came_b, query, key, value, output):
    size, width = own_a.shape
    half = width // 2
    for part, bit, own, came in ((0, info[BX], own_a, came_a), (1, info[BY], own_b, came_b)):
        left, right = ((query, key), (value, None))[part]
        for at, source in ((bit, own), (1 - bit, came)):
            left[rows_at(at, size)] = source[:, :half].astype(f32)
            if right is None:
                output[:, rows_at(at, size)] = source[:, half:].astype(f32).T
            else:
                right[rows_at(at, size)] = source[:, half:].astype(f32)


class Reduction:
    def __init__(self, info, order, halves):
        self.info, self.order = info, order
        self.made = halves
        send_a, send_b, self.keep_a, self.keep_b = halves
        self.came = [flip_by(send_a, "dp", 1), flip_by(send_b, "dp", 2)]

    def staged(self, kernel, outs, *args):
        self.made = call(kernel, kernel.__name__, outs, self.info, *args, order=self.order)
        return self.made

    def quarters(self):
        (first, width), half = self.keep_a.shape, self.keep_b.shape[0]
        self.extra, self.quarter = first - half, half // 2
        a, b = ((self.quarter + self.extra, width), bf16), ((self.quarter, width), bf16)
        send_a, keep_a, send_b, keep_b = self.staged(
            add_halves, [a, a, b, b], self.keep_a, self.came[0], self.keep_b, self.came[1]
        )
        self.keep_a, self.keep_b, self.width = keep_a, keep_b, width
        self.came = [flip_by(send_a, "dp", 2), flip_by(send_b, "dp", 1)]

    def chunks(self):
        self.piece = ((self.quarter // 2 + self.extra, self.width), bf16)
        self.own, *sent = self.staged(
            add_chunks, [self.piece] * 4, self.keep_a, self.came[0], self.keep_b, self.came[1]
        )
        self.came = [flip_by(s, "dp", 4 * (k + 1)) for k, s in enumerate(sent)]

    def total(self):
        (total,) = self.staged(add_four, [self.piece], self.own, *self.came)
        for bit in range(4, bits_of("dp")):
            total = add_low(total, flip_by(total, "dp", 1 << bit))
        rows = self.quarter // 2
        self.small = total[rows:] if self.extra else None
        self.own = total[:rows] if self.extra else total
        self.came = [flip_by(self.own, "dp", 4 * (k + 1)) for k in range(3)]

    def join_four(self):
        whole = ((self.quarter, self.width), bf16)
        self.keep_a, self.keep_b = self.staged(join_chunks, [whole] * 2, self.own, *self.came)
        self.came = [flip_by(self.keep_a, "dp", 2), flip_by(self.keep_b, "dp", 1)]

    def join_two(self):
        whole = ((2 * self.quarter, self.width), bf16)
        self.keep_a, self.keep_b = self.staged(
            join_quarters, [whole] * 2, self.keep_a, self.came[0], self.keep_b, self.came[1]
        )
        self.came = [flip_by(self.keep_a, "dp", 1), flip_by(self.keep_b, "dp", 2)]

    def finish(self, kernel, outs):
        return self.staged(kernel, outs, self.keep_a, self.came[0], self.keep_b, self.came[1])


def down_gradient(info, unit, active, unit_in, active_in, send_a, send_b, keep_a, keep_b):
    size = send_a.shape[0]
    unit, active, unit_in, active_in = ready(unit, active, unit_in, active_in)
    for side in range(2):
        for part, bit, outs in ((0, info[BX], (send_a, keep_a)), (1, info[BY], (send_b, keep_b))):
            at = rows_at(2 * part + (bit if side else 1 - bit), size)
            outs[side][...] = (
                t_dot(active[:, at], unit[...]) + t_dot(active_in[:, at], unit_in[...])
            ).astype(bf16)
            outs[side].send()


def up_gradient(info, delta, first, delta_in, first_in, send_a, send_b, keep_a, keep_b, bias):
    size, width = send_a.shape
    delta, first, delta_in, first_in = ready(delta, first, delta_in, first_in)
    for side in range(2):
        for part, bit, outs in ((0, info[BX], (send_a, keep_a)), (1, info[BY], (send_b, keep_b))):
            columns = pl.ds(part * width, width)
            at = rows_at(bit if side else 1 - bit, size)
            outs[side][...] = (
                t_dot(first[:, at], delta[:, columns]) + t_dot(first_in[:, at], delta_in[:, columns])
            ).astype(bf16)
            outs[side].send()
    ones = jnp.ones((8, delta.shape[0]), bf16)
    bias[...] = dot(ones, delta[...]) + dot(ones, delta_in[...])


def head_gradients(
    info, tokens, query, query_far, key, key_far, value, value_far, branch, branch_far,
    context, context_far, shared, shared_in, bias, send_a, send_b, keep_a, keep_b,
):
    half, width = send_b.shape
    tokens, branch, branch_far, context, context_far = ready(tokens, branch, branch_far, context, context_far)
    value, value_far, query, query_far, key, key_far = ready(value, value_far, query, query_far, key, key_far)
    narrow = query.shape[1]
    length = query.shape[0]
    near, far = rows_at(info[BT], length), rows_at(1 - info[BT], length)
    for side in range(2):
        for part, bit, outs in ((1, info[BY], (send_b, keep_b)), (0, info[BX], (send_a, keep_a))):
            out = outs[side]
            at = rows_at(bit if side else 1 - bit, half)
            tokens_near, tokens_far = tokens[near, at], tokens[far, at]
            if part == 0:
                left = t_dot(tokens_near, query[...]) + t_dot(tokens_far, query_far[...])
                right = t_dot(tokens_near, key[...]) + t_dot(tokens_far, key_far[...])
            else:
                left = t_dot(tokens_near, value[...]) + t_dot(tokens_far, value_far[...])
                right = t_dot(branch[:, at], context[...]) + t_dot(branch_far[:, at], context_far[...])
            out[:half, :narrow] = left.astype(bf16)
            out[:half, narrow:] = right.astype(bf16)
            out.send(pl.ds(0, half))
    ones = jnp.ones((8, length), bf16)
    query_sum = dot(ones, query[...]) + dot(ones, query_far[...])
    value_sum = dot(ones, value[...]) + dot(ones, value_far[...])
    last = jnp.concatenate([query_sum, value_sum], 1)
    rows = lax.broadcasted_iota(jnp.int32, (8, width), 0)
    block = shared[...] + shared_in[...]
    block = jnp.where(rows == 5, bias[:, :width], jnp.where(rows == 6, bias[:, width:], block))
    block = jnp.where(rows == 7, last, block)
    block = jnp.concatenate([block, jnp.zeros_like(block)], 0).astype(bf16)
    for out in (send_a, keep_a):
        out[half:] = block
        out.send(pl.ds(half, SMALL))


def pair_columns(pair):
    return pl.ds(pl.multiple_of(pair * LANES, LANES), LANES)


def attend(
    info, tokens, query_weight, key_weight, value_weight, query_bias, value_bias, segments, validity,
    context, query, key, value, weights, shade, *, far,
):
    length = context.shape[0]
    row = 1 - info[BT] if far else info[BT]
    mark = segments[pl.ds(row, 1)]
    seen = jnp.where(validity[pl.ds(row, 1)] > 0, mark, -1)
    column = jnp.broadcast_to(mark.astype(f32), (8, length)).T[:, :1]
    shade[...] = jnp.where(column == seen.astype(f32), 0.0, neg_large)
    x, query_weight = ready(tokens, query_weight)
    query[...] = (dot(x[...], query_weight[...]) + query_bias[...].astype(f32)[None]).astype(bf16)
    query.send()
    (key_weight,) = ready(key_weight)
    key[...] = dot(x[...], key_weight[...]).astype(bf16)
    key.send()
    (value_weight,) = ready(value_weight)
    value[...] = (dot(x[...], value_weight[...]) + value_bias[...].astype(f32)[None]).astype(bf16)
    value.send()
    low = lax.broadcasted_iota(jnp.int32, (length, LANES), 1) < HD
    scale = log2_e / math.sqrt(HD)

    def body(pair, _):
        at = pair_columns(pair)
        q, k, v = query[:, at], key[:, at], value[:, at]
        parts = []
        for member in range(2):
            side = jnp.where(low if member == 0 else ~low, q, jnp.zeros_like(q))
            logits = dot_t(side, k) * scale + shade[...]
            peak = jnp.max(logits, -1, keepdims=True)
            raised = jnp.exp2(logits - peak)
            total = jnp.sum(raised, -1, keepdims=True)
            share = (raised * (1.0 / total)).astype(bf16)
            weights[2 * pair + member] = share
            weights.send(2 * pair + member)
            parts.append(dot(share, v))
        context[:, at] = jnp.where(low, parts[0], parts[1]).astype(bf16)
        return 0

    lax.fori_loop(0, context.shape[1] // LANES, body, 0)


def attend_back(
    info, branch, output_weight, value, context, weights, key, query, query_weight, key_weight, value_weight,
    query_delta, key_delta, value_delta, part, context_delta,
):
    length = part.shape[0]
    branch, output_weight = ready(branch, output_weight)
    context_delta[...] = dot_t(branch[...], output_weight[...]).astype(bf16)
    value, context, weights, key, query = ready(value, context, weights, key, query)
    low = lax.broadcasted_iota(jnp.int32, (length, LANES), 1) < HD
    scale = 1.0 / math.sqrt(HD)

    def body(pair, _):
        at = pair_columns(pair)
        q, k, v, delta = query[:, at], key[:, at], value[:, at], context_delta[:, at]
        product = delta.astype(f32) * context[:, at].astype(f32)
        queries, keys, values = [], [], []
        for member in range(2):
            mine = low if member == 0 else ~low
            inner = jnp.sum(jnp.where(mine, product, 0.0), -1, keepdims=True)
            side = jnp.where(mine, delta, jnp.zeros_like(delta))
            share = weights[2 * pair + member]
            logit_delta = (share.astype(f32) * (dot_t(side, v) - inner)).astype(bf16)
            queries.append(dot(logit_delta, k))
            keys.append(t_dot(logit_delta, q))
            values.append(t_dot(share, delta))
        query_delta[:, at] = (jnp.where(low, queries[0], queries[1]) * scale).astype(bf16)
        key_delta[:, at] = (jnp.where(low, keys[0], keys[1]) * scale).astype(bf16)
        value_delta[:, at] = jnp.where(low, values[0], values[1]).astype(bf16)
        return 0

    lax.fori_loop(0, query.shape[1] // LANES, body, 0)
    query_delta.send()
    key_delta.send()
    value_delta.send()
    query_weight, key_weight, value_weight = ready(query_weight, key_weight, value_weight)
    part[...] = (
        dot_t(query_delta[...], query_weight[...])
        + dot_t(key_delta[...], key_weight[...])
        + dot_t(value_delta[...], value_weight[...])
    ).astype(part.dtype)


OB, FG, FS, DB, SG = range(5)


def center(inputs):
    shifted = inputs - jnp.mean(inputs, -1, keepdims=True)
    spread = jnp.mean(shifted * shifted, -1, keepdims=True)
    row_scale = lax.rsqrt(spread + norm_eps)
    return shifted * row_scale, row_scale


def norm_back(out_delta, normed, row_scale, norm_gain):
    scaled = out_delta * norm_gain
    first_mean = jnp.mean(scaled, -1, keepdims=True)
    second_mean = jnp.mean(scaled * normed, -1, keepdims=True)
    return row_scale * (scaled - first_mean - normed * second_mean)


def forward(
    info, context, output_near, x, context_in, output_far, up_far, down_far, up_near, down_near, vectors,
    bias_near, bias_far, first_low, first_normed, first_scale, active_near, active_far, slope_near, slope_far,
    second_normed, second_scale, summary, total,
):
    length = total.shape[0]
    step = length // 2
    halves = (pl.ds(0, step), pl.ds(step, step))
    context, output_near, x, context_in, output_far = ready(context, output_near, x, context_in, output_far)
    for at in halves:
        heads = dot(context[at], output_near[...]) + dot(context_in[at], output_far[...])
        normed, scale = center(x[at].astype(f32) + (heads + vectors[OB : OB + 1]))
        out = normed * vectors[FG : FG + 1] + vectors[FS : FS + 1]
        first_normed[at] = normed.astype(bf16)
        first_scale[at] = scale
        first_low[at] = out.astype(bf16)
        total[at] = out + vectors[DB : DB + 1]
    first_low.send()
    first_normed.send()

    width = 3 * LANES
    for up, down, bias, active, slope in (
        (up_far, down_far, bias_far, active_far, slope_far),
        (up_near, down_near, bias_near, active_near, slope_near),
    ):
        up, down = ready(up, down)

        def body(index, _, up=up, down=down, bias=bias, active=active, slope=slope):
            units = rows_at(index, width)
            for at in halves:
                hidden = dot(first_low[at], up[:, units]) + bias[:, units]
                share = 0.5 * (1.0 + lax.erf(hidden * root_half))
                low = (hidden * share).astype(bf16)
                active[at, units] = low
                slope[at, units] = (
                    share + hidden * jnp.exp(-0.5 * hidden * hidden) * inv_root_tau
                ).astype(bf16)
                total[at] += dot(low, down[units])
            active.send(slice(None), units)
            slope.send(slice(None), units)
            return 0

        lax.fori_loop(0, up.shape[1] // width, body, 0)

    for at in halves:
        normed, scale = center(total[at])
        second_normed[at] = normed.astype(bf16)
        second_scale[at] = scale
        total[at] = normed * vectors[SG : SG + 1]
    second_normed.send()
    rows = [total[pl.ds(info[PLACES + k], 1)] for k in range(summary.shape[0])]
    summary[...] = jnp.concatenate(rows, 0).astype(bf16)


def loss_back(*refs, pieces):
    info, *sources = refs[: 1 + pieces]
    (
        upper, normed, scale, vectors, losses, query_gradient, second_delta, unit_delta, sums, all_rows, deltas,
        lost, out_delta,
    ) = refs[1 + pieces :]
    width = upper.shape[1]
    size = sources[0].shape[0]
    for step, source in enumerate(sources):
        all_rows[rows_at(info[BZ] ^ step, size) if pieces > 1 else pl.ds(0, size)] = source[...]
    count = all_rows.shape[0]
    block = min(256, count)
    score_scale = 1.0 / math.sqrt(width)
    own_passages = 4
    upper, normed = ready(upper, normed)
    out_delta[...] = upper[...].astype(f32)

    def body(index, sums_in):
        at = rows_at(index, block)
        rows = all_rows[at, :width]
        digits = all_rows[at, width:].astype(f32)
        scores = dot_t(rows, all_rows[:, :width]) * score_scale
        columns = lax.broadcasted_iota(jnp.int32, (block, count), 1)
        numbers = lax.broadcasted_iota(jnp.int32, (block, 1), 0)
        scores = jnp.where((columns & 15) < 8, scores, neg_large)
        peak = jnp.max(scores, -1, keepdims=True)
        raised = jnp.exp(scores - peak)
        total = jnp.sum(raised, -1, keepdims=True)
        target = (digits[:, 0:1] * 16.0 + digits[:, 1:2]).astype(jnp.int32)
        chosen = columns == target
        lost[at] = peak + jnp.log(total) - jnp.sum(jnp.where(chosen, scores, 0.0), -1, keepdims=True)
        delta = (raised / total - chosen.astype(f32)).astype(bf16)
        delta = jnp.where((numbers & 15) >= 8, delta, jnp.zeros_like(delta))
        deltas[at] = delta
        wide = delta.astype(f32)
        results = []
        for k in range(own_passages):
            column = info[BD] * 16 + info[BT] * own_passages + k
            share = jnp.sum(jnp.where(columns == column, wide, 0.0), -1, keepdims=True)
            results.append(sums_in[k] + jnp.sum(share * rows.astype(f32), 0, keepdims=True))
        return tuple(results)

    zero = jnp.zeros((1, width), f32)
    passage_delta = lax.fori_loop(0, count // block, body, (zero,) * own_passages)
    for k in range(own_passages):
        out_delta[pl.ds(info[PLACES + k], 1)] += passage_delta[k] * score_scale
    own = pl.multiple_of(info[BD] * 16, 16)
    own_delta = deltas[pl.ds(own, 16)]
    query_gradient[...] = (dot(own_delta, all_rows[:, :width]) * score_scale)[8:]
    losses[...] = lost[pl.ds(pl.multiple_of(own + 8, 8), 8)]

    length = upper.shape[0]
    step = length // 4
    bias_sum = gain_sum = zero
    for start in range(0, length, step):
        at = pl.ds(start, step)
        n = normed[at].astype(f32)
        delta = norm_back(out_delta[at], n, scale[at], vectors[SG : SG + 1])
        unit_delta[at] = delta.astype(bf16)
        second_delta[at] = delta
        unit_delta.send(at)
        second_delta.send(at)
        bias_sum += jnp.sum(delta, 0, keepdims=True)
        gain_sum += jnp.sum(out_delta[at] * n, 0, keepdims=True)
    sums[...] = jnp.concatenate(
        [jnp.zeros((DB, width), f32), bias_sum, gain_sum, jnp.zeros((7 - SG, width), f32)], 0
    )


def unit_back(info, unit_delta, down_weight, slope, hidden_delta):
    width = 3 * LANES
    unit_delta, down_weight, slope = ready(unit_delta, down_weight, slope)

    def body(index, _):
        units = rows_at(index, width)
        delta = dot_t(unit_delta[...], down_weight[units])
        hidden_delta[:, units] = (delta * slope[:, units].astype(f32)).astype(bf16)
        hidden_delta.send(slice(None), units)
        return 0

    lax.fori_loop(0, down_weight.shape[0] // width, body, 0)


def first_back(
    info, delta_far, up_far, delta_near, up_near, second_delta, normed, scale, vectors, sums_in, first_delta,
    branch, sums, total,
):
    length, width = total.shape
    delta_far, up_far = ready(delta_far, up_far)
    total[...] = dot_t(delta_far[...], up_far[...])
    delta_near, up_near = ready(delta_near, up_near)
    total[...] += dot_t(delta_near[...], up_near[...])
    second_delta, normed = ready(second_delta, normed)
    step = length // 4
    zero = jnp.zeros((1, width), f32)
    bias_sum = gain_sum = shift_sum = zero
    for start in range(0, length, step):
        at = pl.ds(start, step)
        out_delta = second_delta[at] + total[at]
        n = normed[at].astype(f32)
        delta = norm_back(out_delta, n, scale[at], vectors[FG : FG + 1])
        branch[at] = delta.astype(bf16)
        first_delta[at] = delta
        branch.send(at)
        first_delta.send(at)
        bias_sum += jnp.sum(delta, 0, keepdims=True)
        gain_sum += jnp.sum(out_delta * n, 0, keepdims=True)
        shift_sum += jnp.sum(out_delta, 0, keepdims=True)
    sums[...] = sums_in[...] + jnp.concatenate(
        [bias_sum, gain_sum, shift_sum, jnp.zeros((7 - FS, width), f32)], 0
    )


def shards(
    tokens,
    upper_delta,
    segments,
    summary_index,
    validity,
    queries,
    positives,
    query_weight,
    key_weight,
    value_weight,
    query_bias,
    value_bias,
    output_weight,
    output_bias,
    first_gain,
    first_shift,
    up_weight,
    up_bias,
    down_weight,
    down_bias,
    second_gain,
):
    row_count, length = segments.shape
    token_count = row_count * length
    members = lax.axis_size("tensor")
    place = lax.axis_index("tensor")
    own_count = token_count // members
    width_local = query_weight.shape[1]
    heads_local = width_local // HD
    at_dp = lax.axis_index("dp")
    half_rows = D // 2

    def own(value):
        part = value.shape[0] // members
        return lax.dynamic_slice_in_dim(value, place * part, part, 0)

    info = jnp.concatenate(
        [
            jnp.stack([at_dp & 1, (at_dp >> 1) & 1, (at_dp >> 2) & 3, place, at_dp]).astype(jnp.int32),
            own(summary_index).reshape(-1),
        ]
    )
    vectors = jnp.stack([output_bias, first_gain, first_shift, down_bias, second_gain]).astype(f32)
    vectors = jnp.concatenate([vectors, jnp.zeros((3, D), f32)], 0)
    output_far = swap(output_weight)
    up_far = swap(up_weight)
    bias_far = swap(up_bias.reshape(1, -1))
    down_far = swap(down_weight)

    context_shape = ((length, width_local), bf16)

    def near_rows(info, ref):
        return ref.at[rows_at(info[BT], length)]

    def far_rows(info, ref):
        return ref.at[rows_at(1 - info[BT], length)]

    def attention(far):
        return call(
            functools.partial(attend, far=far),
            "attend_far" if far else "attend_near",
            [context_shape] * 4 + [((heads_local, length, length), bf16)],
            info, tokens, query_weight, key_weight, value_weight, query_bias, value_bias, segments, validity,
            scratch=[pltpu.VMEM((length, length), f32)],
            late=(1, 2, 3, 4),
            early=(1, 2, 3, 4),
            parts={1: ((length, D), far_rows if far else near_rows)},
        )

    context_far, query_far, key_far, value_far, weights_far = attention(True)
    context_in = swap(context_far)
    context, query, key, value, weights = attention(False)

    row, units = ((length, D), bf16), ((length, up_weight.shape[1]), bf16)
    scale_shape = ((length, 1), f32)
    own_passages = summary_index.shape[1]
    (
        first_low, first_normed, first_scale, active, active_far, slope, slope_far, second_normed, second_scale,
        summary,
    ) = call(
        forward, "forward",
        [row, row, scale_shape, units, units, units, units, row, scale_shape, ((own_passages, D), bf16)],
        info, context, output_weight, tokens, context_in, output_far, up_far, down_far, up_weight, down_weight,
        vectors, up_bias.reshape(1, -1).astype(f32), bias_far.astype(f32),
        late=range(1, 10),
        early=(0, 1, 3, 4, 5, 6, 7),
        parts={3: ((length, D), near_rows)},
        scratch=[pltpu.VMEM((length, D), f32)],
    )
    first_in = swap(first_low)
    active_in = swap(active_far)

    pairs = jnp.concatenate([summary, swap(summary)], 0)
    pairs = jnp.where(place == 0, pairs, jnp.roll(pairs, own_passages, 0))
    column = (positives // 8) * 16 + positives % 8
    digits = jnp.stack([column // 16, column % 16], 1).astype(bf16)
    bundle = jnp.concatenate(
        [
            jnp.pad(pairs, ((0, 0), (0, LANES))),
            jnp.concatenate([queries, jnp.pad(digits, ((0, 0), (0, LANES - 2)))], 1),
        ],
        0,
    )
    for bit in (0, 1):
        bundle = join(bundle, flip_by(bundle, "dp", 1 << bit), own_bit("dp", bit))
    pieces = [bundle, *[flip_by(bundle, "dp", 4 * k) for k in (1, 2, 3)]]
    if bits_of("dp") > 4:
        place_z = (at_dp >> 2) & 3
        joined = jnp.zeros((4, *bundle.shape), bf16)
        for k, piece in enumerate(pieces):
            joined = lax.dynamic_update_slice(joined, piece[None], (place_z ^ k, 0, 0))
        bundle = joined.reshape(-1, bundle.shape[1])
        for bit in range(4, bits_of("dp")):
            bundle = join(bundle, flip_by(bundle, "dp", 1 << bit), own_bit("dp", bit))
        pieces = [bundle]
    gathered = 16 * lax.axis_size("dp")
    query_count = queries.shape[0]
    losses, query_gradient, second_delta, unit_delta, sums = call(
        functools.partial(loss_back, pieces=len(pieces)), "loss_back",
        [((query_count, 1), f32), ((query_count, D), f32), ((length, D), f32), row, ((8, D), f32)],
        info, *pieces, upper_delta, second_normed, second_scale, vectors,
        late=(len(pieces) + 1, len(pieces) + 2), early=(2, 3),
        scratch=[
            pltpu.VMEM((gathered, D + LANES), bf16),
            pltpu.VMEM((gathered, gathered), bf16),
            pltpu.VMEM((gathered, 1), f32),
            pltpu.VMEM((length, D), f32),
        ],
    )
    unit_in = swap(unit_delta)
    order = []

    def through_units(name, weight, slope):
        return call(
            unit_back, name, [units], info, unit_delta, weight, slope, late=(1, 2, 3), early=(0,), order=order
        )[0]

    delta_far = through_units("unit_back_far", down_far, slope_far)
    delta_in = swap(delta_far)
    half = ((half_rows, D), bf16)
    down = Reduction(
        info, order,
        call(
            down_gradient, "down_gradient", [half] * 4, info, unit_delta, active, unit_in, active_in,
            late=(1, 2, 3, 4), early=(0, 1, 2, 3), order=order,
        ),
    )
    hidden_delta = through_units("unit_back_near", down_weight, slope)
    *halves, up_bias_sum = call(
        up_gradient, "up_gradient", [half] * 4 + [((8, up_weight.shape[1]), f32)], info, hidden_delta, first_low,
        delta_in, first_in, late=(1, 2, 3, 4), early=(0, 1, 2, 3), order=order,
    )
    up = Reduction(info, order, halves)
    down.quarters()
    first_delta, branch, shared = call(
        first_back, "first_back", [((length, D), f32), row, ((8, D), f32)], info, delta_far, up_far,
        hidden_delta, up_weight, second_delta, first_normed, first_scale, vectors, sums,
        late=range(1, 7), early=(0, 1), scratch=[pltpu.VMEM((length, D), f32)], order=order,
    )
    branch_far = swap(branch)
    shared_in = swap(shared)

    def attention_back(name, branch, weights, query, key, value, context, kind):
        return call(
            attend_back,
            name,
            [context_shape] * 3 + [((length, D), kind)],
            info, branch, output_weight, value, context, weights, key, query, query_weight, key_weight, value_weight,
            scratch=[pltpu.VMEM((length, width_local), bf16)],
            late=range(1, 11),
            early=(0, 1, 2),
            order=order,
        )

    query_delta, key_delta, value_delta, part = attention_back(
        "attend_back_near", branch, weights, query, key, value, context, f32
    )
    down.chunks()
    up.quarters()
    query_delta_far, key_delta_far, value_delta_far, part_far = attention_back(
        "attend_back_far", branch_far, weights_far, query_far, key_far, value_far, context_far, bf16,
    )
    part_in = swap(part_far)
    down.total()
    up.chunks()

    tall = ((half_rows + SMALL, D), bf16)
    heads = Reduction(
        info, order,
        call(
            head_gradients, "head_gradients", [tall, half, tall, half], info, tokens, query_delta, query_delta_far,
            key_delta, key_delta_far, value_delta, value_delta_far, branch, branch_far, context, context_far,
            shared, shared_in, up_bias_sum, late=(1, 8, 9, 10, 11, 6, 7, 2, 3, 4, 5), early=(0, 1, 2, 3), order=order,
        ),
    )
    down.join_four()
    up.total()
    heads.quarters()
    down.join_two()
    heads.chunks()
    up.join_four()
    (down_total,) = down.finish(finish_down, [(down_weight.shape, f32)])
    heads.total()
    up.join_two()
    heads.join_four()
    (up_total,) = up.finish(finish_up, [(up_weight.shape, f32)])
    heads.join_two()
    wide = (query_weight.shape, f32)
    heads_total = heads.finish(finish_heads, [wide] * 3 + [(output_weight.shape, f32)])
    small_total = heads.small.astype(f32)
    token_gradient = (first_delta + part + part_in.astype(f32)).astype(bf16)

    return (
        losses.reshape(-1),
        query_gradient,
        token_gradient,
        heads_total[0],
        heads_total[1],
        heads_total[2],
        small_total[7, :width_local],
        small_total[7, width_local:],
        heads_total[3],
        small_total[OB],
        small_total[FG],
        small_total[FS],
        up_total,
        small_total[5:7].reshape(-1),
        down_total,
        small_total[DB],
        small_total[SG],
    )


def solution(mesh):
    in_specs = (
        P("dp", None),
        P(("dp", "tensor"), None),
        P("dp", None),
        P("dp", None),
        P("dp", None),
        P("dp", None),
        P("dp"),
        P(None, "tensor"),
        P(None, "tensor"),
        P(None, "tensor"),
        P("tensor"),
        P("tensor"),
        P("tensor", None),
        P(),
        P(),
        P(),
        P(None, "tensor"),
        P("tensor"),
        P("tensor", None),
        P(),
        P(),
    )
    out_specs = (
        P("dp"),
        P("dp", None),
        P(("dp", "tensor"), None),
        P(None, "tensor"),
        P(None, "tensor"),
        P(None, "tensor"),
        P("tensor"),
        P("tensor"),
        P("tensor", None),
        P(),
        P(),
        P(),
        P(None, "tensor"),
        P("tensor"),
        P("tensor", None),
        P(),
        P(),
    )
    return jax.shard_map(shards, mesh=mesh, in_specs=in_specs, out_specs=out_specs, check_vma=False)
```

time: 365 us -> 292 us (0.80)
  Pallas kernels: 0 us -> 160 us
  matrix products: 92.2 us -> 0 us
  waiting for transfers between devices: 124 us -> 49.2 us
  other arithmetic: 44.4 us -> 6.37 us
  local copies, waits for them, and re-layouts: 30.7 us -> 7.14 us
  starting transfers between devices: 66.5 us -> 62.6 us
    pallas_call x0 -> x30, Pallas kernels: none -> 160 us  [call(): pl.pallas_call(body, name=name, out_shape=[jax.ShapeDtypeStruct(s, t) for...]
    dot_general x38 -> x0, matrix products: 92.2 us -> none  [the longest x11 23.8 us: dot(): return jnp.dot(left, right, preferred_element_type=jnp.float32)]
    ppermute x77 -> x60, waiting for transfers between devices: 124 us -> 49.2 us  [flip_by(): return lax.ppermute(value, axis, [(i, i ^ mask) for i in range(size)])]
    convert_element_type x40 -> x4, other arithmetic: 25.4 us -> 4.27 us  [the longest x1 3.07 us: shards(): token_gradient = (first_delta + part + part_in.astype(f32)).astype(bf16)]
    reduce_sum x8 -> x0, other arithmetic: 7.94 us -> none  [the longest x1 1.86 us: shards(): row_total = jnp.sum(row_exp, -1, keepdims=True)]
    select_n x38 -> x2, other arithmetic: 7.91 us -> 0.04 us  [join(): jnp.where(high == 1, jnp.concatenate([other, value], 0), jnp.concatenate(...]
    convert_element_type x8 -> x1, local copies, waits for them, and re-layouts: 5.28 us -> 0.01 us  [shards(): up_bias.reshape(1, -1).astype(f32)]
    reshape x6 -> x2, local copies, waits for them, and re-layouts: 5.75 us -> 0.62 us  [the longest x1 0.61 us: shards(): small_total[5:7].reshape(-1)]
  transfers between devices with their start and end apart: 77 -> 60, of which waited for: 41 -> 17; matrix products, arithmetic and copies ran while one was open for 38% -> 3% of each run, Pallas kernels for 0% -> 45%
where the time goes in v2:
time: 292 us; the launch traced here: 287 us
  Pallas kernels  160 us (55%)
  starting transfers between devices  62.6 us (21%)
  waiting for transfers between devices  49.2 us (17%)
  local copies, waits for them, and re-layouts  7.14 us (2%)
  other arithmetic  6.37 us (2%)
    pallas_call x30, Pallas kernels, call(): pl.pallas_call(body, name=name, out_shape=[jax.ShapeDtypeStruct(s, t) for...  160 us
    ppermute x60, starting transfers between devices, flip_by(): return lax.ppermute(value, axis, [(i, i ^ mask) for i in range(size)])  62.6 us
    ppermute x60, waiting for transfers between devices, flip_by(): return lax.ppermute(value, axis, [(i, i ^ mask) for i in range(size)])  49.2 us
  transfers between devices with their start and end apart: 60, of which 17 were waited for; matrix products, arithmetic and copies ran while one was open for 3% of the time, Pallas kernels for 45%

profile of v2, /device:TPU:0, one launch (start us, length us, event | category | flops | bytes accessed | tf_op | source)
XLA Modules:
  0.0 286.9 jit_solution(16651015112836642376)
XLA Ops:
  2.0 9.2 %attend_far.1 = (bf16[512,384]{1,0:T(8,128)(2,1)}, bf16[512,384]{1,0:T(8,128)(2,1)}, bf16[512,384]{1,0:T(8,128)(2,1)}, bf16[512,384]{1,0:T(8,128)(2,1)}, bf16[6,512,512]{2,1,0:T(8,128)(2,1)}) custom-call(s32[9]{0:T(128)} %concatenate.35.refs_0_, bf16[1024,768]{1,0:T(8,128)(2,1)} %refs_1_.5, bf16[768,384]{1,0:T(8,128)(2,1)} %refs_8_.9, ...), custom_call_target="tpu_custom_call" | custom-call | flops 20700000256 | bytes 1 | tf_op jit(solution)/shard_map/attend_far/pallas_call | solution.py:146
  12.9 9.2 %attend_near.1 = (bf16[512,384]{1,0:T(8,128)(2,1)}, bf16[512,384]{1,0:T(8,128)(2,1)}, bf16[512,384]{1,0:T(8,128)(2,1)}, bf16[512,384]{1,0:T(8,128)(2,1)}, bf16[6,512,512]{2,1,0:T(8,128)(2,1)}) custom-call(s32[9]{0:T(128)} %concatenate.35.refs_0_, bf16[1024,768]{1,0:T(8,128)(2,1)} %refs_1_.5, bf16[768,384]{1,0:T(8,128)(2,1)} %refs_8_.9, ...), custom_call_target="tpu_custom_call" | custom-call | flops 20700000256 | bytes 1 | tf_op jit(solution)/shard_map/attend_near/pallas_call | solution.py:146
  24.1 16.4 %forward.1 = (bf16[512,768]{1,0:T(8,128)(2,1)}, bf16[512,768]{1,0:T(8,128)(2,1)}, f32[512,1]{1,0:T(8,128)}, bf16[512,1536]{1,0:T(8,128)(2,1)}, bf16[512,1536]{1,...) custom-call(s32[9]{0:T(128)} %concatenate.35.refs_0_, ...), custom_call_target="tpu_custom_call" | custom-call | flops 39099998208 | bytes 1 | tf_op jit(solution)/shard_map/forward/pallas_call | solution.py:146
  42.8 2.7 collective-permute-start.6
  45.5 1.9 collective-permute-done.6
  47.4 2.1 collective-permute-start.7
  49.5 2.2 collective-permute-done.7
  51.7 2.1 collective-permute-start.8
  53.9 2.6 collective-permute-start.9
  57.5 6.2 %collective-permute-done.9.refs_3_ = bf16[64,896]{1,0:T(8,128)(2,1)S(1)} collective-permute-done((bf16[64,896]{1,0:T(8,128)(2,1)S(1)}, bf16[64,896]{1,0:T(8,128)(2,1)S(1)}, u32[]{:S(2)}, u32[]{:S(2)}) %collective-permute-start.9) | collective-permute-done | bytes 114720 | tf_op jit(solution)/shard_map/ppermute | solution.py:38
  64.4 6.0 %loss_back.1 = (f32[8,1]{1,0:T(8,128)}, f32[8,768]{1,0:T(8,128)}, f32[512,768]{1,0:T(8,128)}, bf16[512,768]{1,0:T(8,128)(2,1)}, f32[8,768]{1,0:T(8,128)}) custom-call(s32[9]{0:T(128)} %concatenate.35.refs_0_, bf16[64,896]{1,0:T(8,128)(2,1)} %copy-done.4, bf16[64,896]{1,0:T(8,128)(2,1)} %copy-done.28, bf16[64,896]{1,0:T(8,128)(2,1)} %copy-done.29, ...), custom_call_target="tpu_custom_call" | custom-call | flops 13799999488 | bytes 1 | tf_op jit(solution)/shard_map/loss_back/pallas_call | solution.py:146
  70.5 6.2 %unit_back_far.1.refs_5_.refs_1_ = bf16[512,1536]{1,0:T(8,128)(2,1)} custom-call(s32[9]{0:T(128)} %concatenate.35.refs_0_, bf16[512,768]{1,0:T(8,128)(2,1)} %get-tuple-element.113.refs_1_, bf16[1536,768]{1,0:T(8,128)(2,1)} %collective-permute-done.3.refs_7_.refs_2_, bf16[512,1536]{1,0:T(8,128)(2,1)} %get-tuple-element.114.refs_3_), custom_call_target="tpu_custom_call" | custom-call | flops 13799999488 | bytes 1 | tf_op jit(solution)/shard_map/unit_back_far/pallas_call | solution.py:146
  77.4 6.6 %down_gradient.1 = (bf16[384,768]{1,0:T(8,128)(2,1)}, bf16[384,768]{1,0:T(8,128)(2,1)}, bf16[384,768]{1,0:T(8,128)(2,1)}, bf16[384,768]{1,0:T(8,128)(2,1)}) custom-call(s32[9]{0:T(128)} %concatenate.35.refs_0_, bf16[512,768]{1,0:T(8,128)(2,1)} %get-tuple-element.113.refs_1_, bf16[512,1536]{1,0:T(8,128)(2,1)} %get-tuple-element.116.refs_2_, ...), custom_call_target="tpu_custom_call" | custom-call | flops 16099999744 | bytes 1 | tf_op jit(solution)/shard_map/down_gradient/pallas_call | solution.py:146
  84.0 1.5 collective-permute-start.13
  85.5 1.5 collective-permute-start.14
  87.0 6.3 %unit_back_near.1.refs_1_.refs_5_.refs_3_ = bf16[512,1536]{1,0:T(8,128)(2,1)} custom-call(s32[9]{0:T(128)} %concatenate.35.refs_0_, bf16[512,768]{1,0:T(8,128)(2,1)} %get-tuple-element.113.refs_1_, bf16[1536,768]{1,0:T(8,128)(2,1)} %refs_2_.9, bf16[512,1536]{1,0:T(8,128)(2,1)} %get-tuple-element.115.refs_3_, bf16[384,768]{1,0:T(8,128)(2,1)} %get-tuple-element.118.refs_4_.refs_3_), custom_call_target="tpu_custom_call" | custom-call | flops 13799999488 | bytes 1 | tf_op jit(solution)/shard_map/unit_back_near/pallas_call | solution.py:146
  94.2 7.1 %up_gradient.1 = (bf16[384,768]{1,0:T(8,128)(2,1)}, bf16[384,768]{1,0:T(8,128)(2,1)}, bf16[384,768]{1,0:T(8,128)(2,1)}, bf16[384,768]{1,0:T(8,128)(2,1)}, f32[8,1536]{1,0:T(8,128)}) custom-call(s32[9]{0:T(128)} %concatenate.35.refs_0_, bf16[512,1536]{1,0:T(8,128)(2,1)} %unit_back_near.1.refs_1_.refs_5_.refs_3_, bf16[512,768]{1,0:T(8,128)(2,1)} %get-tuple-element.126.refs_2_, ...), custom_call_target="tpu_custom_call" | custom-call | flops 16099999744 | bytes 1 | tf_op jit(solution)/shard_map/up_gradient/pallas_call | solution.py:146
  102.4 2.8 add_halves.3
  105.3 9.4 %first_back.1 = (f32[512,768]{1,0:T(8,128)}, bf16[512,768]{1,0:T(8,128)(2,1)}, f32[8,768]{1,0:T(8,128)}) custom-call(s32[9]{0:T(128)} %concatenate.35.refs_0_, bf16[512,1536]{1,0:T(8,128)(2,1)} %unit_back_far.1.refs_5_.refs_1_, bf16[768,1536]{1,0:T(8,128)(2,1)} %collective-permute-done.2.refs_6_.refs_2_, ...), custom_call_target="tpu_custom_call" | custom-call | flops 20700000256 | bytes 1 | tf_op jit(solution)/shard_map/first_back/pallas_call | solution.py:146
  114.7 1.6 collective-permute-start.20
  116.3 1.5 collective-permute-start.21
  117.8 19.9 %attend_back_near.1 = (bf16[512,384]{1,0:T(8,128)(2,1)}, bf16[512,384]{1,0:T(8,128)(2,1)}, bf16[512,384]{1,0:T(8,128)(2,1)}, f32[512,768]{1,0:T(8,128)}) custom-call(s32[9]{0:T(128)} %concatenate.35.refs_0_, bf16[512,768]{1,0:T(8,128)(2,1)} %get-tuple-element.130.refs_1_.refs_8_, bf16[384,768]{1,0:T(8,128)(2,1)} %refs_2_.11, ...), custom_call_target="tpu_custom_call" | custom-call | flops 23000000512 | bytes 1 | tf_op jit(solution)/shard_map/attend_back_near/pallas_call | solution.py:146
  137.8 2.1 add_chunks.3
  139.9 2.5 collective-permute-start.28
  142.4 2.8 add_halves.4
  147.7 10.0 %attend_back_far.1 = (bf16[512,384]{1,0:T(8,128)(2,1)}, bf16[512,384]{1,0:T(8,128)(2,1)}, bf16[512,384]{1,0:T(8,128)(2,1)}, bf16[512,768]{1,0:T(8,128)(2,1)}) custom-call(s32[9]{0:T(128)} %concatenate.35.refs_0_, bf16[512,768]{1,0:T(8,128)(2,1)} %copy-done.13, bf16[384,768]{1,0:T(8,128)(2,1)} %refs_2_.11, bf16[512,384]{1,0:T(8,128)(2,1)} %get-tuple-element.137.refs_3_, ...), custom_call_target="tpu_custom_call" | custom-call | flops 23000000512 | bytes 1 | tf_op jit(solution)/shard_map/attend_back_far/pallas_call | solution.py:146
  158.3 1.9 add_four.3.refs_5_.refs_1_
  161.2 2.1 collective-permute-start.35
  164.6 1.8 collective-permute-done.25.refs_4_
  167.1 2.1 add_chunks.4
  169.2 2.4 collective-permute-start.33
  171.6 8.0 %head_gradients.1 = (bf16[400,768]{1,0:T(8,128)(2,1)}, bf16[384,768]{1,0:T(8,128)(2,1)}, bf16[400,768]{1,0:T(8,128)(2,1)}, bf16[384,768]{1,0:T(8,128)(2,1)}) custom-call(s32[9]{0:T(128)} %concatenate.35.refs_0_, bf16[1024,768]{1,0:T(8,128)(2,1)} %refs_1_.5, bf16[512,384]{1,0:T(8,128)(2,1)} %get-tuple-element.151.refs_2_, ...), custom_call_target="tpu_custom_call" | custom-call | flops 18400000000 | bytes 1 | tf_op jit(solution)/shard_map/head_gradients/pallas_call | solution.py:146
  180.3 1.5 collective-permute-start.30
  181.8 1.9 collective-permute-start.32
  183.8 2.0 join_chunks.3
  185.8 3.2 %collective-permute-done.31.refs_2_ = bf16[96,768]{1,0:T(8,128)(2,1)} collective-permute-done((bf16[96,768]{1,0:T(8,128)(2,1)}, bf16[96,768]{1,0:T(8,128)(2,1)}, u32[]{:S(2)}, u32[]{:S(2)}) %collective-permute-start.31) | collective-permute-done | bytes 147488 | tf_op jit(solution)/shard_map/ppermute | solution.py:38
  189.0 1.5 collective-permute-start.40
  190.5 1.9 add_four.4.refs_5_.refs_1_
  192.5 2.0 collective-permute-start.47
  194.5 2.4 collective-permute-start.48
  198.3 2.8 add_halves.5
  201.1 5.4 %collective-permute-done.39.refs_2_ = bf16[192,768]{1,0:T(8,128)(2,1)} collective-permute-done((bf16[192,768]{1,0:T(8,128)(2,1)S(1)}, bf16[192,768]{1,0:T(8,128)(2,1)}, u32[]{:S(2)}, u32[]{:S(2)}) %collective-permute-start.39) | collective-permute-done | bytes 294944 | tf_op jit(solution)/shard_map/ppermute | solution.py:38
  207.4 2.3 join_quarters.3
  209.7 7.8 %collective-permute-done.38.refs_4_ = bf16[192,768]{1,0:T(8,128)(2,1)S(1)} collective-permute-done((bf16[192,768]{1,0:T(8,128)(2,1)}, bf16[192,768]{1,0:T(8,128)(2,1)S(1)}, u32[]{:S(2)}, u32[]{:S(2)}) %collective-permute-start.38) | collective-permute-done | bytes 294944 | tf_op jit(solution)/shard_map/ppermute | solution.py:38
  219.5 2.2 add_chunks.5
  221.8 4.3 %collective-permute-start.43 = (bf16[112,768]{1,0:T(8,128)(2,1)}, bf16[112,768]{1,0:T(8,128)(2,1)}, u32[]{:S(2)}, u32[]{:S(2)}) collective-permute-start(bf16[112,768]{1,0:T(8,128)(2,1)} %get-tuple-element.181.refs_5_), channel_id=1, source_target_pairs={{0,24},{2,26},{4,28},{6,30},{8,16},{10,18},{12,20},{14,22},{16,8},... | collective-permute-start | bytes 516104 | tf_op jit(solution)/shard_map/ppermute | solution.py:38
  226.0 2.0 join_chunks.4
  228.0 3.5 %collective-permute-done.44.refs_2_ = bf16[384,768]{1,0:T(8,128)(2,1)S(1)} collective-permute-done((bf16[384,768]{1,0:T(8,128)(2,1)}, bf16[384,768]{1,0:T(8,128)(2,1)S(1)}, u32[]{:S(2)}, u32[]{:S(2)}) %collective-permute-start.44) | collective-permute-done | bytes 589856 | tf_op jit(solution)/shard_map/ppermute | solution.py:38
  232.7 4.1 %finish_down.1.refs_5_ = f32[1536,768]{1,0:T(8,128)} custom-call(s32[9]{0:T(128)} %concatenate.35.refs_0_, bf16[384,768]{1,0:T(8,128)(2,1)} %get-tuple-element.182.refs_1_, bf16[384,768]{1,0:T(8,128)(2,1)} %copy-done.17, bf16[384,768]{1,0:T(8,128)(2,1)} %get-tuple-element.177.refs_5_.refs_3_, bf16[384,768]{1,0:T(8,128)(2,1)} %collective-permute-done.45.refs_4_, ...), custom_call_target="tpu_custom_call" | custom-call | flops 9200000000 | bytes 1 | tf_op jit(solution)/shard_map/finish_down/pallas_call | solution.py:146
  236.8 1.9 add_four.5.refs_5_
  238.8 2.8 collective-permute-done.52.refs_2_
  242.9 2.3 join_quarters.4
  246.3 4.3 %collective-permute-start.51 = (bf16[96,768]{1,0:T(8,128)(2,1)S(1)}, bf16[96,768]{1,0:T(8,128)(2,1)}, u32[]{:S(2)}, u32[]{:S(2)}) collective-permute-start(bf16[96,768]{1,0:T(8,128)(2,1)S(1)} %slice.44.refs_1_), channel_id=1, source_target_pairs={{0,24},{2,26},{4,28},{6,30},{8,16},{10,18},{12,20},{14,22},{16,8},... | collective-permute-start | bytes 442376 | tf_op jit(solution)/shard_map/ppermute | solution.py:38
  251.3 1.6 collective-permute-done.49.refs_2_
  252.8 2.7 collective-permute-done.50.refs_3_
  256.2 2.0 join_chunks.5
  259.4 2.0 collective-permute-start.55
  261.4 4.1 %finish_up.1.refs_5_ = f32[768,1536]{1,0:T(8,128)} custom-call(s32[9]{0:T(128)} %concatenate.35.refs_0_, bf16[384,768]{1,0:T(8,128)(2,1)} %get-tuple-element.188.refs_1_, bf16[384,768]{1,0:T(8,128)(2,1)} %collective-permute-done.56.refs_2_, bf16[384,768]{1,0:T(8,128)(2,1)} %get-tuple-element.185.refs_5_.refs_3_, ...), custom_call_target="tpu_custom_call" | custom-call | flops 9200000000 | bytes 1 | tf_op jit(solution)/shard_map/finish_up/pallas_call | solution.py:146
  266.5 2.3 join_quarters.5
  268.8 2.0 collective-permute-start.58
  271.7 3.1 %add_convert_fusion = bf16[512,768]{1,0:T(8,128)(2,1)} fusion(bf16[512,768]{1,0:T(8,128)(2,1)S(1)} %collective-permute-done.22, f32[512,768]{1,0:T(8,128)} %get-tuple-element.129, f32[512,768]{1,0:T(8,128)} %get-tuple-element.136.refs_5_), kind=kLoop, calls=%fused_computation | loop fusion | flops 1572864 | bytes 4718592 | tf_op jit(solution)/shard_map/convert_element_type | solution.py:854
  276.6 4.6 %collective-permute-done.58.refs_2_ = bf16[384,768]{1,0:T(8,128)(2,1)} collective-permute-done((bf16[384,768]{1,0:T(8,128)(2,1)}, bf16[384,768]{1,0:T(8,128)(2,1)}, u32[]{:S(2)}, u32[]{:S(2)}) %collective-permute-start.58) | collective-permute-done | bytes 589856 | tf_op jit(solution)/shard_map/ppermute | solution.py:38
  281.2 1.5 collective-permute-done.59.refs_4_
  282.7 4.1 %finish_heads.1 = (f32[768,384]{1,0:T(8,128)}, f32[768,384]{1,0:T(8,128)}, f32[768,384]{1,0:T(8,128)}, f32[384,768]{1,0:T(8,128)}) custom-call(s32[9]{0:T(128)} %concatenate.35.refs_0_, bf16[384,768]{1,0:T(8,128)(2,1)} %get-tuple-element.189.refs_1_, bf16[384,768]{1,0:T(8,128)(2,1)} %collective-permute-done.58.refs_2_, ...), custom_call_target="tpu_custom_call" | custom-call | flops 9200000000 | bytes 1 | tf_op jit(solution)/shard_map/finish_heads/pallas_call | solution.py:146
  (182 shorter events, 32.5 us)
Async XLA Ops:
  11.2 12.9 %collective-permute-start = (bf16[512,384]{1,0:T(8,128)(2,1)}, bf16[512,384]{1,0:T(8,128)(2,1)}, u32[]{:S(2)}, u32[]{:S(2)}) collective-permute-start(bf16[512,384]{1,0:T(8,128)(2,1)} %get-tuple-element.107.refs_4_.refs_11_), channel_id=1, source_target_pairs={{0,1},{1,0},{2,3},{3,2},{4,5},{5,4},{6,7},{7,6},{8,9},{9,8},{10,11... | collective-permute-start | bytes 1179656 | tf_op jit(solution)/shard_map/ppermute | solution.py:38
  11.7 12.4 %collective-permute-start.1 = (bf16[384,768]{1,0:T(8,128)(2,1)S(1)}, bf16[384,768]{1,0:T(8,128)(2,1)}, u32[]{:S(2)}, u32[]{:S(2)}) collective-permute-start(bf16[384,768]{1,0:T(8,128)(2,1)S(1)} %copy-done.16), channel_id=1, source_target_pairs={{0,1},{1,0},{2,3},{3,2},{4,5},{5,4},{6,7},{7,6},{8,9},{9,8},{10,11... | collective-permute-start | bytes 1769480 | tf_op jit(solution)/shard_map/ppermute | solution.py:38
  11.8 12.3 %collective-permute-start.2 = (bf16[768,1536]{1,0:T(8,128)(2,1)}, bf16[768,1536]{1,0:T(8,128)(2,1)}, u32[]{:S(2)}, u32[]{:S(2)}) collective-permute-start(bf16[768,1536]{1,0:T(8,128)(2,1)} %refs_4_.5), channel_id=1, source_target_pairs={{0,1},{1,0},{2,3},{3,2},{4,5},{5,4},{6,7},{7,6},{8,9},{9,8},{10,11... | collective-permute-start | bytes 7077896 | tf_op jit(solution)/shard_map/ppermute | solution.py:38
  12.2 11.9 %collective-permute-start.3 = (bf16[1536,768]{1,0:T(8,128)(2,1)}, bf16[1536,768]{1,0:T(8,128)(2,1)}, u32[]{:S(2)}, u32[]{:S(2)}) collective-permute-start(bf16[1536,768]{1,0:T(8,128)(2,1)} %refs_2_.9), channel_id=1, source_target_pairs={{0,1},{1,0},{2,3},{3,2},{4,5},{5,4},{6,7},{7,6},{8,9},{9,8},{10,11... | collective-permute-start | bytes 7077896 | tf_op jit(solution)/shard_map/ppermute | solution.py:38
  12.4 11.1 %collective-permute-start.4 = (bf16[1,1536]{1,0:T(2,128)(2,1)S(1)}, bf16[1,1536]{1,0:T(2,128)(2,1)S(1)}, u32[]{:S(2)}, u32[]{:S(2)}) collective-permute-start(bf16[1,1536]{1,0:T(2,128)(2,1)S(1)} %convert_element_type.23), channel_id=1, source_target_pairs={{0,1},{1,0},{2,3},{3,2},{4,5},{5,4},{6,7},{7,6},{8,9},{9,8},{10,11... | collective-permute-start | bytes 9224 | tf_op jit(solution)/shard_map/ppermute | solution.py:38
  24.1 18.7 %copy-start.5 = (bf16[8,768]{1,0:T(8,128)(2,1)S(1)}, bf16[8,768]{1,0:T(8,128)(2,1)}, u32[]{:S(2)}) copy-start(bf16[8,768]{1,0:T(8,128)(2,1)} %param.26) | copy-start | bytes 36868
  40.6 1.4 collective-permute-start.5
  42.8 4.6 %collective-permute-start.6 = (bf16[16,896]{1,0:T(8,128)(2,1)S(1)}, bf16[16,896]{1,0:T(8,128)(2,1)S(1)}, u32[]{:S(2)}, u32[]{:S(2)}) collective-permute-start(bf16[16,896]{1,0:T(8,128)(2,1)S(1)} %maximum_maximum_fusion), channel_id=1, source_target_pairs={{0,2},{2,0},{4,6},{6,4},{8,10},{10,8},{12,14},{14,12},{16,18},{18,... | collective-permute-start | bytes 86024 | tf_op jit(solution)/shard_map/ppermute | solution.py:38
  47.4 4.3 %collective-permute-start.7 = (bf16[32,896]{1,0:T(8,128)(2,1)S(1)}, bf16[32,896]{1,0:T(8,128)(2,1)S(1)}, u32[]{:S(2)}, u32[]{:S(2)}) collective-permute-start(bf16[32,896]{1,0:T(8,128)(2,1)S(1)} %maximum_select_fusion.1), channel_id=1, source_target_pairs={{0,4},{2,6},{4,0},{6,2},{8,12},{10,14},{12,8},{14,10},{16,20},{18,... | collective-permute-start | bytes 172040 | tf_op jit(solution)/shard_map/ppermute | solution.py:38
  51.7 12.7 %copy-start.4 = (bf16[64,896]{1,0:T(8,128)(2,1)}, bf16[64,896]{1,0:T(8,128)(2,1)S(1)}, u32[]{:S(2)}) copy-start(bf16[64,896]{1,0:T(8,128)(2,1)S(1)} %maximum_select_fusion.refs_1_) | copy-start | bytes 344068
  51.7 5.8 %collective-permute-start.8 = (bf16[64,896]{1,0:T(8,128)(2,1)S(1)}, bf16[64,896]{1,0:T(8,128)(2,1)S(1)}, u32[]{:S(2)}, u32[]{:S(2)}) collective-permute-start(bf16[64,896]{1,0:T(8,128)(2,1)S(1)} %maximum_select_fusion.refs_1_), channel_id=1, source_target_pairs={{0,8},{2,10},{4,12},{6,14},{8,0},{10,2},{12,4},{14,6},{16,24},{18,... | collective-permute-start | bytes 344072 | tf_op jit(solution)/shard_map/ppermute | solution.py:38
  53.9 9.9 %collective-permute-start.9 = (bf16[64,896]{1,0:T(8,128)(2,1)S(1)}, bf16[64,896]{1,0:T(8,128)(2,1)S(1)}, u32[]{:S(2)}, u32[]{:S(2)}) collective-permute-start(bf16[64,896]{1,0:T(8,128)(2,1)S(1)} %maximum_select_fusion.refs_1_), channel_id=1, source_target_pairs={{0,16},{2,18},{4,20},{6,22},{8,24},{10,26},{12,28},{14,30},{16,0},... | collective-permute-start | bytes 344072 | tf_op jit(solution)/shard_map/ppermute | solution.py:38
  56.4 7.3 %collective-permute-start.10 = (bf16[64,896]{1,0:T(8,128)(2,1)S(1)}, bf16[64,896]{1,0:T(8,128)(2,1)S(1)}, u32[]{:S(2)}, u32[]{:S(2)}) collective-permute-start(bf16[64,896]{1,0:T(8,128)(2,1)S(1)} %maximum_select_fusion.refs_1_), channel_id=1, source_target_pairs={{0,24},{2,26},{4,28},{6,30},{8,16},{10,18},{12,20},{14,22},{16,8},... | collective-permute-start | bytes 344072 | tf_op jit(solution)/shard_map/ppermute | solution.py:38
  56.4 20.9 %collective-permute-start.12 = (bf16[512,1536]{1,0:T(8,128)(2,1)}, bf16[512,1536]{1,0:T(8,128)(2,1)}, u32[]{:S(2)}, u32[]{:S(2)}) collective-permute-start(bf16[512,1536]{1,0:T(8,128)(2,1)} %get-tuple-element.117), channel_id=1, source_target_pairs={{0,1},{1,0},{2,3},{3,2},{4,5},{5,4},{6,7},{7,6},{8,9},{9,8},{10,11... | collective-permute-start | bytes 4718600 | tf_op jit(solution)/shard_map/ppermute | solution.py:38
  56.4 36.8 %collective-permute-start.16 = (bf16[512,768]{1,0:T(8,128)(2,1)}, bf16[512,768]{1,0:T(8,128)(2,1)S(1)}, u32[]{:S(2)}, u32[]{:S(2)}) collective-permute-start(bf16[512,768]{1,0:T(8,128)(2,1)} %get-tuple-element.126.refs_2_), channel_id=1, source_target_pairs={{0,1},{1,0},{2,3},{3,2},{4,5},{5,4},{6,7},{7,6},{8,9},{9,8},{10,11... | collective-permute-start | bytes 2359304 | tf_op jit(solution)/shard_map/ppermute | solution.py:38
  70.5 6.9 %collective-permute-start.11 = (bf16[512,768]{1,0:T(8,128)(2,1)}, bf16[512,768]{1,0:T(8,128)(2,1)}, u32[]{:S(2)}, u32[]{:S(2)}) collective-permute-start(bf16[512,768]{1,0:T(8,128)(2,1)} %get-tuple-element.113.refs_1_), channel_id=1, source_target_pairs={{0,1},{1,0},{2,3},{3,2},{4,5},{5,4},{6,7},{7,6},{8,9},{9,8},{10,11... | collective-permute-start | bytes 2359304 | tf_op jit(solution)/shard_map/ppermute | solution.py:38
  76.8 16.5 %collective-permute-start.15 = (bf16[512,1536]{1,0:T(8,128)(2,1)}, bf16[512,1536]{1,0:T(8,128)(2,1)}, u32[]{:S(2)}, u32[]{:S(2)}) collective-permute-start(bf16[512,1536]{1,0:T(8,128)(2,1)} %unit_back_far.1.refs_5_.refs_1_), channel_id=1, source_target_pairs={{0,1},{1,0},{2,3},{3,2},{4,5},{5,4},{6,7},{7,6},{8,9},{9,8},{10,11... | collective-permute-start | bytes 4718600 | tf_op jit(solution)/shard_map/ppermute | solution.py:38
  84.0 18.5 %collective-permute-start.13 = (bf16[384,768]{1,0:T(8,128)(2,1)}, bf16[384,768]{1,0:T(8,128)(2,1)}, u32[]{:S(2)}, u32[]{:S(2)}) collective-permute-start(bf16[384,768]{1,0:T(8,128)(2,1)} %get-tuple-element.124), channel_id=1, source_target_pairs={{0,2},{2,0},{4,6},{6,4},{8,10},{10,8},{12,14},{14,12},{16,18},{18,... | collective-permute-start | bytes 1769480 | tf_op jit(solution)/shard_map/ppermute | solution.py:38
  85.5 16.9 %collective-permute-start.14 = (bf16[384,768]{1,0:T(8,128)(2,1)}, bf16[384,768]{1,0:T(8,128)(2,1)}, u32[]{:S(2)}, u32[]{:S(2)}) collective-permute-start(bf16[384,768]{1,0:T(8,128)(2,1)} %get-tuple-element.125), channel_id=1, source_target_pairs={{0,4},{2,6},{4,0},{6,2},{8,12},{10,14},{12,8},{14,10},{16,20},{18,... | collective-permute-start | bytes 1769480 | tf_op jit(solution)/shard_map/ppermute | solution.py:38
  101.3 41.1 %collective-permute-start.18 = (bf16[384,768]{1,0:T(8,128)(2,1)}, bf16[384,768]{1,0:T(8,128)(2,1)}, u32[]{:S(2)}, u32[]{:S(2)}) collective-permute-start(bf16[384,768]{1,0:T(8,128)(2,1)} %get-tuple-element.142), channel_id=1, source_target_pairs={{0,2},{2,0},{4,6},{6,4},{8,10},{10,8},{12,14},{14,12},{16,18},{18,... | collective-permute-start | bytes 1769480 | tf_op jit(solution)/shard_map/ppermute | solution.py:38
  101.9 40.5 %collective-permute-start.19 = (bf16[384,768]{1,0:T(8,128)(2,1)}, bf16[384,768]{1,0:T(8,128)(2,1)}, u32[]{:S(2)}, u32[]{:S(2)}) collective-permute-start(bf16[384,768]{1,0:T(8,128)(2,1)} %get-tuple-element.144), channel_id=1, source_target_pairs={{0,4},{2,6},{4,0},{6,2},{8,12},{10,14},{12,8},{14,10},{16,20},{18,... | collective-permute-start | bytes 1769480 | tf_op jit(solution)/shard_map/ppermute | solution.py:38
  114.7 32.0 %collective-permute-start.17 = (bf16[512,768]{1,0:T(8,128)(2,1)}, bf16[512,768]{1,0:T(8,128)(2,1)S(1)}, u32[]{:S(2)}, u32[]{:S(2)}) collective-permute-start(bf16[512,768]{1,0:T(8,128)(2,1)} %get-tuple-element.130.refs_1_.refs_8_), channel_id=1, source_target_pairs={{0,1},{1,0},{2,3},{3,2},{4,5},{5,4},{6,7},{7,6},{8,9},{9,8},{10,11... | collective-permute-start | bytes 2359304 | tf_op jit(solution)/shard_map/ppermute | solution.py:38
  114.7 22.9 %collective-permute-start.20 = (bf16[192,768]{1,0:T(8,128)(2,1)}, bf16[192,768]{1,0:T(8,128)(2,1)}, u32[]{:S(2)}, u32[]{:S(2)}) collective-permute-start(bf16[192,768]{1,0:T(8,128)(2,1)} %get-tuple-element.146), channel_id=1, source_target_pairs={{0,4},{2,6},{4,0},{6,2},{8,12},{10,14},{12,8},{14,10},{16,20},{18,... | collective-permute-start | bytes 884744 | tf_op jit(solution)/shard_map/ppermute | solution.py:38
  116.3 21.5 %collective-permute-start.21 = (bf16[192,768]{1,0:T(8,128)(2,1)}, bf16[192,768]{1,0:T(8,128)(2,1)}, u32[]{:S(2)}, u32[]{:S(2)}) collective-permute-start(bf16[192,768]{1,0:T(8,128)(2,1)} %get-tuple-element.147), channel_id=1, source_target_pairs={{0,2},{2,0},{4,6},{6,4},{8,10},{10,8},{12,14},{14,12},{16,18},{18,... | collective-permute-start | bytes 884744 | tf_op jit(solution)/shard_map/ppermute | solution.py:38
  117.8 19.9 %copy-start.31 = (f32[8,768]{1,0:T(8,128)S(1)}, f32[8,768]{1,0:T(8,128)}, u32[]{:S(2)}) copy-start(f32[8,768]{1,0:T(8,128)} %get-tuple-element.135.refs_11_.refs_12_) | copy-start | bytes 73732
  137.7 33.9 %collective-permute-start.23 = (f32[8,768]{1,0:T(8,128)S(1)}, f32[8,768]{1,0:T(8,128)}, u32[]{:S(2)}, u32[]{:S(2)}) collective-permute-start(f32[8,768]{1,0:T(8,128)S(1)} %copy-done.31), channel_id=1, source_target_pairs={{0,1},{1,0},{2,3},{3,2},{4,5},{5,4},{6,7},{7,6},{8,9},{9,8},{10,11... | collective-permute-start | bytes 73736 | tf_op jit(solution)/shard_map/ppermute | solution.py:38
  139.9 18.4 %collective-permute-start.28 = (bf16[96,768]{1,0:T(8,128)(2,1)}, bf16[96,768]{1,0:T(8,128)(2,1)}, u32[]{:S(2)}, u32[]{:S(2)}) collective-permute-start(bf16[96,768]{1,0:T(8,128)(2,1)} %get-tuple-element.148.refs_5_), channel_id=1, source_target_pairs={{0,24},{2,26},{4,28},{6,30},{8,16},{10,18},{12,20},{14,22},{16,8},... | collective-permute-start | bytes 442376 | tf_op jit(solution)/shard_map/ppermute | solution.py:38
  145.3 18.0 %collective-permute-start.24 = (bf16[192,768]{1,0:T(8,128)(2,1)}, bf16[192,768]{1,0:T(8,128)(2,1)}, u32[]{:S(2)}, u32[]{:S(2)}) collective-permute-start(bf16[192,768]{1,0:T(8,128)(2,1)} %get-tuple-element.158), channel_id=1, source_target_pairs={{0,4},{2,6},{4,0},{6,2},{8,12},{10,14},{12,8},{14,10},{16,20},{18,... | collective-permute-start | bytes 884744 | tf_op jit(solution)/shard_map/ppermute | solution.py:38
  145.8 11.9 %collective-permute-start.26 = (bf16[96,768]{1,0:T(8,128)(2,1)}, bf16[96,768]{1,0:T(8,128)(2,1)}, u32[]{:S(2)}, u32[]{:S(2)}) collective-permute-start(bf16[96,768]{1,0:T(8,128)(2,1)} %get-tuple-element.161), channel_id=1, source_target_pairs={{0,8},{2,10},{4,12},{6,14},{8,0},{10,2},{12,4},{14,6},{16,24},{18,... | collective-permute-start | bytes 442376 | tf_op jit(solution)/shard_map/ppermute | solution.py:38
  146.6 11.7 %collective-permute-start.27 = (bf16[96,768]{1,0:T(8,128)(2,1)S(1)}, bf16[96,768]{1,0:T(8,128)(2,1)}, u32[]{:S(2)}, u32[]{:S(2)}) collective-permute-start(bf16[96,768]{1,0:T(8,128)(2,1)S(1)} %copy-done.25), channel_id=1, source_target_pairs={{0,16},{2,18},{4,20},{6,22},{8,24},{10,26},{12,28},{14,30},{16,0},... | collective-permute-start | bytes 442376 | tf_op jit(solution)/shard_map/ppermute | solution.py:38
  157.7 8.6 %collective-permute-start.25 = (bf16[192,768]{1,0:T(8,128)(2,1)}, bf16[192,768]{1,0:T(8,128)(2,1)S(1)}, u32[]{:S(2)}, u32[]{:S(2)}) collective-permute-start(bf16[192,768]{1,0:T(8,128)(2,1)} %get-tuple-element.159), channel_id=1, source_target_pairs={{0,2},{2,0},{4,6},{6,4},{8,10},{10,8},{12,14},{14,12},{16,18},{18,... | collective-permute-start | bytes 884744 | tf_op jit(solution)/shard_map/ppermute | solution.py:38
  160.2 20.1 %collective-permute-start.34 = (bf16[96,768]{1,0:T(8,128)(2,1)}, bf16[96,768]{1,0:T(8,128)(2,1)S(1)}, u32[]{:S(2)}, u32[]{:S(2)}) collective-permute-start(bf16[96,768]{1,0:T(8,128)(2,1)} %add_four.3.refs_5_.refs_1_), channel_id=1, source_target_pairs={{0,8},{2,10},{4,12},{6,14},{8,0},{10,2},{12,4},{14,6},{16,24},{18,... | collective-permute-start | bytes 442376 | tf_op jit(solution)/shard_map/ppermute | solution.py:38
  161.2 20.6 %collective-permute-start.35 = (bf16[96,768]{1,0:T(8,128)(2,1)}, bf16[96,768]{1,0:T(8,128)(2,1)S(1)}, u32[]{:S(2)}, u32[]{:S(2)}) collective-permute-start(bf16[96,768]{1,0:T(8,128)(2,1)} %add_four.3.refs_5_.refs_1_), channel_id=1, source_target_pairs={{0,16},{2,18},{4,20},{6,22},{8,24},{10,26},{12,28},{14,30},{16,0},... | collective-permute-start | bytes 442376 | tf_op jit(solution)/shard_map/ppermute | solution.py:38
  163.3 18.5 %collective-permute-start.36 = (bf16[96,768]{1,0:T(8,128)(2,1)}, bf16[96,768]{1,0:T(8,128)(2,1)}, u32[]{:S(2)}, u32[]{:S(2)}) collective-permute-start(bf16[96,768]{1,0:T(8,128)(2,1)} %add_four.3.refs_5_.refs_1_), channel_id=1, source_target_pairs={{0,24},{2,26},{4,28},{6,30},{8,16},{10,18},{12,20},{14,22},{16,8},... | collective-permute-start | bytes 442376 | tf_op jit(solution)/shard_map/ppermute | solution.py:38
  169.2 21.3 %collective-permute-start.33 = (bf16[96,768]{1,0:T(8,128)(2,1)}, bf16[96,768]{1,0:T(8,128)(2,1)}, u32[]{:S(2)}, u32[]{:S(2)}) collective-permute-start(bf16[96,768]{1,0:T(8,128)(2,1)} %get-tuple-element.163.refs_15_), channel_id=1, source_target_pairs={{0,24},{2,26},{4,28},{6,30},{8,16},{10,18},{12,20},{14,22},{16,8},... | collective-permute-start | bytes 442376 | tf_op jit(solution)/shard_map/ppermute | solution.py:38
  179.7 17.2 %collective-permute-start.29 = (bf16[400,768]{1,0:T(8,128)(2,1)}, bf16[400,768]{1,0:T(8,128)(2,1)S(1)}, u32[]{:S(2)}, u32[]{:S(2)}) collective-permute-start(bf16[400,768]{1,0:T(8,128)(2,1)} %get-tuple-element.165), channel_id=1, source_target_pairs={{0,2},{2,0},{4,6},{6,4},{8,10},{10,8},{12,14},{14,12},{16,18},{18,... | collective-permute-start | bytes 1843208 | tf_op jit(solution)/shard_map/ppermute | solution.py:38
  180.3 14.2 %collective-permute-start.30 = (bf16[384,768]{1,0:T(8,128)(2,1)}, bf16[384,768]{1,0:T(8,128)(2,1)}, u32[]{:S(2)}, u32[]{:S(2)}) collective-permute-start(bf16[384,768]{1,0:T(8,128)(2,1)} %get-tuple-element.167), channel_id=1, source_target_pairs={{0,4},{2,6},{4,0},{6,2},{8,12},{10,14},{12,8},{14,10},{16,20},{18,... | collective-permute-start | bytes 1769480 | tf_op jit(solution)/shard_map/ppermute | solution.py:38
  181.8 7.2 %collective-permute-start.31 = (bf16[96,768]{1,0:T(8,128)(2,1)}, bf16[96,768]{1,0:T(8,128)(2,1)}, u32[]{:S(2)}, u32[]{:S(2)}) collective-permute-start(bf16[96,768]{1,0:T(8,128)(2,1)} %get-tuple-element.169), channel_id=1, source_target_pairs={{0,8},{2,10},{4,12},{6,14},{8,0},{10,2},{12,4},{14,6},{16,24},{18,... | collective-permute-start | bytes 442376 | tf_op jit(solution)/shard_map/ppermute | solution.py:38
  181.8 8.7 %collective-permute-start.32 = (bf16[96,768]{1,0:T(8,128)(2,1)}, bf16[96,768]{1,0:T(8,128)(2,1)}, u32[]{:S(2)}, u32[]{:S(2)}) collective-permute-start(bf16[96,768]{1,0:T(8,128)(2,1)} %get-tuple-element.170), channel_id=1, source_target_pairs={{0,16},{2,18},{4,20},{6,22},{8,24},{10,26},{12,28},{14,30},{16,0},... | collective-permute-start | bytes 442376 | tf_op jit(solution)/shard_map/ppermute | solution.py:38
  189.0 18.4 %collective-permute-start.40 = (bf16[192,768]{1,0:T(8,128)(2,1)}, bf16[192,768]{1,0:T(8,128)(2,1)}, u32[]{:S(2)}, u32[]{:S(2)}) collective-permute-start(bf16[192,768]{1,0:T(8,128)(2,1)} %get-tuple-element.171.refs_5_.refs_3_), channel_id=1, source_target_pairs={{0,2},{2,0},{4,6},{6,4},{8,10},{10,8},{12,14},{14,12},{16,18},{18,... | collective-permute-start | bytes 884744 | tf_op jit(solution)/shard_map/ppermute | solution.py:38
  192.5 29.2 %collective-permute-start.46 = (bf16[96,768]{1,0:T(8,128)(2,1)}, bf16[96,768]{1,0:T(8,128)(2,1)}, u32[]{:S(2)}, u32[]{:S(2)}) collective-permute-start(bf16[96,768]{1,0:T(8,128)(2,1)} %add_four.4.refs_5_.refs_1_), channel_id=1, source_target_pairs={{0,8},{2,10},{4,12},{6,14},{8,0},{10,2},{12,4},{14,6},{16,24},{18,... | collective-permute-start | bytes 442376 | tf_op jit(solution)/shard_map/ppermute | solution.py:38
  192.5 29.2 %collective-permute-start.47 = (bf16[96,768]{1,0:T(8,128)(2,1)}, bf16[96,768]{1,0:T(8,128)(2,1)}, u32[]{:S(2)}, u32[]{:S(2)}) collective-permute-start(bf16[96,768]{1,0:T(8,128)(2,1)} %add_four.4.refs_5_.refs_1_), channel_id=1, source_target_pairs={{0,16},{2,18},{4,20},{6,22},{8,24},{10,26},{12,28},{14,30},{16,0},... | collective-permute-start | bytes 442376 | tf_op jit(solution)/shard_map/ppermute | solution.py:38
  194.5 27.3 %collective-permute-start.48 = (bf16[96,768]{1,0:T(8,128)(2,1)}, bf16[96,768]{1,0:T(8,128)(2,1)}, u32[]{:S(2)}, u32[]{:S(2)}) collective-permute-start(bf16[96,768]{1,0:T(8,128)(2,1)} %add_four.4.refs_5_.refs_1_), channel_id=1, source_target_pairs={{0,24},{2,26},{4,28},{6,30},{8,16},{10,18},{12,20},{14,22},{16,8},... | collective-permute-start | bytes 442376 | tf_op jit(solution)/shard_map/ppermute | solution.py:38
  196.9 9.6 %collective-permute-start.39 = (bf16[192,768]{1,0:T(8,128)(2,1)S(1)}, bf16[192,768]{1,0:T(8,128)(2,1)}, u32[]{:S(2)}, u32[]{:S(2)}) collective-permute-start(bf16[192,768]{1,0:T(8,128)(2,1)S(1)} %copy-done.19), channel_id=1, source_target_pairs={{0,4},{2,6},{4,0},{6,2},{8,12},{10,14},{12,8},{14,10},{16,20},{18,... | collective-permute-start | bytes 884744 | tf_op jit(solution)/shard_map/ppermute | solution.py:38
  206.5 11.8 %collective-permute-start.37 = (bf16[208,768]{1,0:T(8,128)(2,1)}, bf16[208,768]{1,0:T(8,128)(2,1)S(1)}, u32[]{:S(2)}, u32[]{:S(2)}) collective-permute-start(bf16[208,768]{1,0:T(8,128)(2,1)} %get-tuple-element.173), channel_id=1, source_target_pairs={{0,4},{2,6},{4,0},{6,2},{8,12},{10,14},{12,8},{14,10},{16,20},{18,... | collective-permute-start | bytes 958472 | tf_op jit(solution)/shard_map/ppermute | solution.py:38
  207.4 10.2 %collective-permute-start.38 = (bf16[192,768]{1,0:T(8,128)(2,1)}, bf16[192,768]{1,0:T(8,128)(2,1)S(1)}, u32[]{:S(2)}, u32[]{:S(2)}) collective-permute-start(bf16[192,768]{1,0:T(8,128)(2,1)} %get-tuple-element.175), channel_id=1, source_target_pairs={{0,2},{2,0},{4,6},{6,4},{8,10},{10,8},{12,14},{14,12},{16,18},{18,... | collective-permute-start | bytes 884744 | tf_op jit(solution)/shard_map/ppermute | solution.py:38
  218.3 13.3 %collective-permute-start.44 = (bf16[384,768]{1,0:T(8,128)(2,1)}, bf16[384,768]{1,0:T(8,128)(2,1)S(1)}, u32[]{:S(2)}, u32[]{:S(2)}) collective-permute-start(bf16[384,768]{1,0:T(8,128)(2,1)} %get-tuple-element.182.refs_1_), channel_id=1, source_target_pairs={{0,2},{2,0},{4,6},{6,4},{8,10},{10,8},{12,14},{14,12},{16,18},{18,... | collective-permute-start | bytes 1769480 | tf_op jit(solution)/shard_map/ppermute | solution.py:38
  218.3 14.4 %collective-permute-start.45 = (bf16[384,768]{1,0:T(8,128)(2,1)}, bf16[384,768]{1,0:T(8,128)(2,1)}, u32[]{:S(2)}, u32[]{:S(2)}) collective-permute-start(bf16[384,768]{1,0:T(8,128)(2,1)} %get-tuple-element.177.refs_5_.refs_3_), channel_id=1, source_target_pairs={{0,4},{2,6},{4,0},{6,2},{8,12},{10,14},{12,8},{14,10},{16,20},{18,... | collective-permute-start | bytes 1769480 | tf_op jit(solution)/shard_map/ppermute | solution.py:38
  221.7 15.2 %collective-permute-start.41 = (bf16[112,768]{1,0:T(8,128)(2,1)}, bf16[112,768]{1,0:T(8,128)(2,1)}, u32[]{:S(2)}, u32[]{:S(2)}) collective-permute-start(bf16[112,768]{1,0:T(8,128)(2,1)} %get-tuple-element.179), channel_id=1, source_target_pairs={{0,8},{2,10},{4,12},{6,14},{8,0},{10,2},{12,4},{14,6},{16,24},{18,... | collective-permute-start | bytes 516104 | tf_op jit(solution)/shard_map/ppermute | solution.py:38
  221.7 15.2 %collective-permute-start.42 = (bf16[112,768]{1,0:T(8,128)(2,1)}, bf16[112,768]{1,0:T(8,128)(2,1)}, u32[]{:S(2)}, u32[]{:S(2)}) collective-permute-start(bf16[112,768]{1,0:T(8,128)(2,1)} %get-tuple-element.180), channel_id=1, source_target_pairs={{0,16},{2,18},{4,20},{6,22},{8,24},{10,26},{12,28},{14,30},{16,0},... | collective-permute-start | bytes 516104 | tf_op jit(solution)/shard_map/ppermute | solution.py:38
  221.8 15.1 %collective-permute-start.43 = (bf16[112,768]{1,0:T(8,128)(2,1)}, bf16[112,768]{1,0:T(8,128)(2,1)}, u32[]{:S(2)}, u32[]{:S(2)}) collective-permute-start(bf16[112,768]{1,0:T(8,128)(2,1)} %get-tuple-element.181.refs_5_), channel_id=1, source_target_pairs={{0,24},{2,26},{4,28},{6,30},{8,16},{10,18},{12,20},{14,22},{16,8},... | collective-permute-start | bytes 516104 | tf_op jit(solution)/shard_map/ppermute | solution.py:38
  231.5 10.1 %collective-permute-start.52 = (bf16[192,768]{1,0:T(8,128)(2,1)}, bf16[192,768]{1,0:T(8,128)(2,1)S(1)}, u32[]{:S(2)}, u32[]{:S(2)}) collective-permute-start(bf16[192,768]{1,0:T(8,128)(2,1)} %get-tuple-element.184.refs_1_), channel_id=1, source_target_pairs={{0,4},{2,6},{4,0},{6,2},{8,12},{10,14},{12,8},{14,10},{16,20},{18,... | collective-permute-start | bytes 884744 | tf_op jit(solution)/shard_map/ppermute | solution.py:38
  232.7 10.3 %collective-permute-start.53 = (bf16[192,768]{1,0:T(8,128)(2,1)}, bf16[192,768]{1,0:T(8,128)(2,1)}, u32[]{:S(2)}, u32[]{:S(2)}) collective-permute-start(bf16[192,768]{1,0:T(8,128)(2,1)} %get-tuple-element.183.refs_5_.refs_3_), channel_id=1, source_target_pairs={{0,2},{2,0},{4,6},{6,4},{8,10},{10,8},{12,14},{14,12},{16,18},{18,... | collective-permute-start | bytes 884744 | tf_op jit(solution)/shard_map/ppermute | solution.py:38
  238.8 11.8 %copy-start.7 = (f32[8,1]{1,0:T(8,128)S(1)}, f32[8,1]{1,0:T(8,128)}, u32[]{:S(2)}) copy-start(f32[8,1]{1,0:T(8,128)} %get-tuple-element.111) | copy-start | bytes 100
  245.2 16.1 %collective-permute-start.56 = (bf16[384,768]{1,0:T(8,128)(2,1)}, bf16[384,768]{1,0:T(8,128)(2,1)}, u32[]{:S(2)}, u32[]{:S(2)}) collective-permute-start(bf16[384,768]{1,0:T(8,128)(2,1)} %get-tuple-element.188.refs_1_), channel_id=1, source_target_pairs={{0,2},{2,0},{4,6},{6,4},{8,10},{10,8},{12,14},{14,12},{16,18},{18,... | collective-permute-start | bytes 1769480 | tf_op jit(solution)/shard_map/ppermute | solution.py:38
  245.3 16.1 %collective-permute-start.57 = (bf16[384,768]{1,0:T(8,128)(2,1)}, bf16[384,768]{1,0:T(8,128)(2,1)}, u32[]{:S(2)}, u32[]{:S(2)}) collective-permute-start(bf16[384,768]{1,0:T(8,128)(2,1)} %get-tuple-element.185.refs_5_.refs_3_), channel_id=1, source_target_pairs={{0,4},{2,6},{4,0},{6,2},{8,12},{10,14},{12,8},{14,10},{16,20},{18,... | collective-permute-start | bytes 1769480 | tf_op jit(solution)/shard_map/ppermute | solution.py:38
  246.2 6.6 %collective-permute-start.49 = (bf16[96,768]{1,0:T(8,128)(2,1)S(1)}, bf16[96,768]{1,0:T(8,128)(2,1)S(1)}, u32[]{:S(2)}, u32[]{:S(2)}) collective-permute-start(bf16[96,768]{1,0:T(8,128)(2,1)S(1)} %slice.44.refs_1_), channel_id=1, source_target_pairs={{0,8},{2,10},{4,12},{6,14},{8,0},{10,2},{12,4},{14,6},{16,24},{18,... | collective-permute-start | bytes 442376 | tf_op jit(solution)/shard_map/ppermute | solution.py:38
  246.3 9.3 %collective-permute-start.50 = (bf16[96,768]{1,0:T(8,128)(2,1)S(1)}, bf16[96,768]{1,0:T(8,128)(2,1)S(1)}, u32[]{:S(2)}, u32[]{:S(2)}) collective-permute-start(bf16[96,768]{1,0:T(8,128)(2,1)S(1)} %slice.44.refs_1_), channel_id=1, source_target_pairs={{0,16},{2,18},{4,20},{6,22},{8,24},{10,26},{12,28},{14,30},{16,0},... | collective-permute-start | bytes 442376 | tf_op jit(solution)/shard_map/ppermute | solution.py:38
  246.3 9.9 %collective-permute-start.51 = (bf16[96,768]{1,0:T(8,128)(2,1)S(1)}, bf16[96,768]{1,0:T(8,128)(2,1)}, u32[]{:S(2)}, u32[]{:S(2)}) collective-permute-start(bf16[96,768]{1,0:T(8,128)(2,1)S(1)} %slice.44.refs_1_), channel_id=1, source_target_pairs={{0,24},{2,26},{4,28},{6,30},{8,16},{10,18},{12,20},{14,22},{16,8},... | collective-permute-start | bytes 442376 | tf_op jit(solution)/shard_map/ppermute | solution.py:38
  252.8 18.8 %collective-permute-start.22 = (bf16[512,768]{1,0:T(8,128)(2,1)}, bf16[512,768]{1,0:T(8,128)(2,1)S(1)}, u32[]{:S(2)}, u32[]{:S(2)}) collective-permute-start(bf16[512,768]{1,0:T(8,128)(2,1)} %get-tuple-element.150.refs_5_), channel_id=1, source_target_pairs={{0,1},{1,0},{2,3},{3,2},{4,5},{5,4},{6,7},{7,6},{8,9},{9,8},{10,11... | collective-permute-start | bytes 2359304 | tf_op jit(solution)/shard_map/ppermute | solution.py:38
  258.2 7.3 %collective-permute-start.54 = (bf16[192,768]{1,0:T(8,128)(2,1)}, bf16[192,768]{1,0:T(8,128)(2,1)}, u32[]{:S(2)}, u32[]{:S(2)}) collective-permute-start(bf16[192,768]{1,0:T(8,128)(2,1)} %get-tuple-element.186.refs_1_), channel_id=1, source_target_pairs={{0,4},{2,6},{4,0},{6,2},{8,12},{10,14},{12,8},{14,10},{16,20},{18,... | collective-permute-start | bytes 884744 | tf_op jit(solution)/shard_map/ppermute | solution.py:38
  259.4 7.0 %collective-permute-start.55 = (bf16[192,768]{1,0:T(8,128)(2,1)}, bf16[192,768]{1,0:T(8,128)(2,1)}, u32[]{:S(2)}, u32[]{:S(2)}) collective-permute-start(bf16[192,768]{1,0:T(8,128)(2,1)} %get-tuple-element.187.refs_5_.refs_3_), channel_id=1, source_target_pairs={{0,2},{2,0},{4,6},{6,4},{8,10},{10,8},{12,14},{14,12},{16,18},{18,... | collective-permute-start | bytes 884744 | tf_op jit(solution)/shard_map/ppermute | solution.py:38
  268.8 12.4 %collective-permute-start.58 = (bf16[384,768]{1,0:T(8,128)(2,1)}, bf16[384,768]{1,0:T(8,128)(2,1)}, u32[]{:S(2)}, u32[]{:S(2)}) collective-permute-start(bf16[384,768]{1,0:T(8,128)(2,1)} %get-tuple-element.189.refs_1_), channel_id=1, source_target_pairs={{0,2},{2,0},{4,6},{6,4},{8,10},{10,8},{12,14},{14,12},{16,18},{18,... | collective-permute-start | bytes 1769480 | tf_op jit(solution)/shard_map/ppermute | solution.py:38
  270.8 11.9 %collective-permute-start.59 = (bf16[384,768]{1,0:T(8,128)(2,1)}, bf16[384,768]{1,0:T(8,128)(2,1)}, u32[]{:S(2)}, u32[]{:S(2)}) collective-permute-start(bf16[384,768]{1,0:T(8,128)(2,1)} %get-tuple-element.190.refs_3_.refs_5_), channel_id=1, source_target_pairs={{0,4},{2,6},{4,0},{6,2},{8,12},{10,14},{12,8},{14,10},{16,20},{18,... | collective-permute-start | bytes 1769480 | tf_op jit(solution)/shard_map/ppermute | solution.py:38
  (29 other events, 131.4 us)

commit v3 on v2

--- a/solution.py
+++ b/solution.py
@@ -22,10 +22,9 @@
 COSTS = dict(
     attend_far=9, attend_near=9, forward=17, loss_back=6, unit_back_far=6, unit_back_near=6, down_gradient=7,
     up_gradient=7, first_back=9, attend_back_near=10, attend_back_far=10, head_gradients=8, add_halves=3,
-    add_chunks=2, add_four=2, join_chunks=2, join_quarters=2, finish_down=4, finish_up=4, finish_heads=4,
+    add_quarters=2, add_eighths=2, add_last=2, join_pieces=2, join_eighths=2, join_quarters=2, finish_down=4, finish_up=4, finish_heads=4,
 )
 FLOPS = int(2.3e9)
-VMEM_GRANT = 63 << 20
 SMALL = 16
 
 
@@ -115,12 +114,11 @@
     return [value.wait() if isinstance(value, Late) else value for value in values]
 
 
-def call(kernel, name, outs, *args, scratch=(), late=(), early=(), order=None, parts=None):
-    parts, after = parts or {}, order or []
+def call(kernel, name, outs, *args, scratch=(), late=(), early=(), order=None, grant=20, final=()):
+    after = order or []
     count, waits, made = len(args), len(after), len(outs)
-    held = [
-        pltpu.VMEM(parts[i][0] if i in parts else args[i].shape, args[i].dtype) for i in late
-    ] + [pltpu.VMEM(*outs[i]) for i in early]
+    held = [pltpu.VMEM(args[i].shape, args[i].dtype) for i in late] + [pltpu.VMEM(*outs[i]) for i in early]
+    args = [pltpu.with_memory_space_constraint(a, pltpu.HBM) if i in late else a for i, a in enumerate(args)]
 
     def body(*refs):
         inputs = list(refs[:count])
@@ -128,29 +126,28 @@
         rest = refs[count + waits + made :]
         scratches, rest = rest[: len(scratch)], rest[len(scratch) :]
         for k, i in enumerate(late):
-            source = parts[i][1](inputs[0], inputs[i]) if i in parts else inputs[i]
-            inputs[i] = Late(source, rest[k], rest[-1].at[k])
-        for k, i in enumerate(early):
-            k += len(late)
+            inputs[i] = Late(inputs[i], rest[k], rest[-1].at[k])
+        for k, i in enumerate(early, len(late)):
             results[i] = Early(rest[k], results[i], rest[-1].at[k])
         kernel(*inputs, *results, *scratches)
-        for i in late:
-            inputs[i].wait()
         for i in early:
             results[i].finish()
 
     specs = [pl.BlockSpec(memory_space=pltpu.SMEM)]
-    specs += [pl.BlockSpec(memory_space=pl.ANY if i in late else pltpu.VMEM) for i in range(1, count)]
+    specs += [pl.BlockSpec(memory_space=pltpu.HBM if i in late else pltpu.VMEM) for i in range(1, count)]
     specs += [pl.BlockSpec(memory_space=pl.ANY)] * waits
     own = [pltpu.SemaphoreType.DMA((len(held),))] if held else []
     made_by = pl.pallas_call(
         body,
         name=name,
-        out_shape=[jax.ShapeDtypeStruct(s, t) for s, t in outs],
+        out_shape=[
+            jax.ShapeDtypeStruct(*out) if i in final else (pltpu.HBM if i in early else pltpu.VMEM)(*out)
+            for i, out in enumerate(outs)
+        ],
         in_specs=specs,
-        out_specs=[pl.BlockSpec(memory_space=pl.ANY if i in early else pltpu.VMEM) for i in range(made)],
+        out_specs=[pl.BlockSpec(memory_space=pltpu.HBM if i in early else pltpu.VMEM) for i in range(made)],
         scratch_shapes=[*scratch, *held, *own],
-        compiler_params=pltpu.CompilerParams(vmem_limit_bytes=VMEM_GRANT),
+        compiler_params=pltpu.CompilerParams(vmem_limit_bytes=grant << 20),
         cost_estimate=pl.CostEstimate(
             flops=int(COSTS[name] * FLOPS), bytes_accessed=1, transcendentals=0
         ),
@@ -186,30 +183,50 @@
             kept[quarter:] = extra
 
 
-def add_chunks(info, keep_a, came_a, keep_b, came_b, own, one, two, three):
+def add_quarters(info, keep_a, came_a, keep_b, came_b, send, kept):
     quarter = keep_b.shape[0]
-    chunk = quarter // 4
-    for step, out in enumerate((own, one, two, three)):
-        at = rows_at(info[BZ] ^ step, chunk)
-        out[:chunk] = add_low(keep_a[at], came_a[at])
-        out[chunk : 2 * chunk] = add_low(keep_b[at], came_b[at])
+    half = quarter // 2
+    bit = info[BZ] & 1
+    for out, side in ((send, 1 - bit), (kept, bit)):
+        at = rows_at(side, half)
+        out[:half] = add_low(keep_a[at], came_a[at])
+        out[half:quarter] = add_low(keep_b[at], came_b[at])
         if keep_a.shape[0] > quarter:
-            out[2 * chunk :] = add_low(keep_a[quarter:], came_a[quarter:])
-
-
-def add_four(info, own, one, two, three, total):
-    total[...] = (
-        (own[...].astype(f32) + one[...].astype(f32))
-        + (two[...].astype(f32) + three[...].astype(f32))
-    ).astype(bf16)
-
-
-def join_chunks(info, own, one, two, three, quarter_a, quarter_b):
-    chunk = quarter_a.shape[0] // 4
-    for step, part in enumerate((own, one, two, three)):
-        at = rows_at(info[BZ] ^ step, chunk)
-        quarter_a[at] = part[:chunk]
-        quarter_b[at] = part[chunk : 2 * chunk]
+            out[quarter:] = add_low(keep_a[quarter:], came_a[quarter:])
+
+
+def add_eighths(info, keep, came, send, kept):
+    half = kept.shape[0] // 32 * 16
+    bit = info[BZ] >> 1
+    for out, side in ((send, 1 - bit), (kept, bit)):
+        for part in range(2):
+            at = rows_at(2 * part + side, half)
+            out[part * half : part * half + half] = add_low(keep[at], came[at])
+        if kept.shape[0] > 2 * half:
+            out[2 * half :] = add_low(keep[4 * half :], came[4 * half :])
+
+
+def add_last(info, keep, came, total, *small):
+    size = total.shape[0]
+    total[...] = add_low(keep[:size], came[:size])
+    if small:
+        small[0][...] = add_low(keep[size:], came[size:])
+
+
+def join_pieces(info, own, came, eighth):
+    half = own.shape[0] // 2
+    bit = info[BZ] >> 1
+    for source, side in ((own, bit), (came, 1 - bit)):
+        for part in range(2):
+            eighth[rows_at(2 * part + side, half)] = source[part * half : part * half + half]
+
+
+def join_eighths(info, own, came, quarter_a, quarter_b):
+    half = own.shape[0] // 2
+    bit = info[BZ] & 1
+    for source, side in ((own, bit), (came, 1 - bit)):
+        quarter_a[rows_at(side, half)] = source[:half]
+        quarter_b[rows_at(side, half)] = source[half:]
 
 
 def join_quarters(info, own_a, came_a, own_b, came_b, half_a, half_b):
@@ -222,32 +239,38 @@
         half[rows_at(1 - bit, size)] = came[...]
 
 
-def finish_down(info, own_a, came_a, own_b, came_b, out):
+def finish_down(info, own_a, came_a, own_b, came_b, out, mark):
+    mark[...] = jnp.zeros_like(mark)
     size = own_a.shape[0]
     for part, bit, own, came in ((0, info[BX], own_a, came_a), (1, info[BY], own_b, came_b)):
-        out[rows_at(2 * part + bit, size)] = own[...].astype(f32)
-        out[rows_at(2 * part + 1 - bit, size)] = came[...].astype(f32)
-
-
-def finish_up(info, own_a, came_a, own_b, came_b, out):
+        for side, source in ((bit, own), (1 - bit, came)):
+            at = rows_at(2 * part + side, size)
+            out[at] = source[...].astype(f32)
+            out.send(at)
+
+
+def finish_up(info, own_a, came_a, own_b, came_b, out, mark):
+    mark[...] = jnp.zeros_like(mark)
     size, width = own_a.shape
     for part, bit, own, came in ((0, info[BX], own_a, came_a), (1, info[BY], own_b, came_b)):
-        columns = pl.ds(part * width, width)
-        out[rows_at(bit, size), columns] = own[...].astype(f32)
-        out[rows_at(1 - bit, size), columns] = came[...].astype(f32)
+        for side, source in ((bit, own), (1 - bit, came)):
+            at = rows_at(side, size), pl.ds(part * width, width)
+            out[at] = source[...].astype(f32)
+            out.send(*at)
 
 
 def finish_heads(info, own_a, came_a, own_b, came_b, query, key, value, output):
     size, width = own_a.shape
     half = width // 2
     for part, bit, own, came in ((0, info[BX], own_a, came_a), (1, info[BY], own_b, came_b)):
-        left, right = ((query, key), (value, None))[part]
-        for at, source in ((bit, own), (1 - bit, came)):
-            left[rows_at(at, size)] = source[:, :half].astype(f32)
-            if right is None:
-                output[:, rows_at(at, size)] = source[:, half:].astype(f32).T
-            else:
-                right[rows_at(at, size)] = source[:, half:].astype(f32)
+        left, right = ((query, key), (value, output))[part]
+        for side, source in ((bit, own), (1 - bit, came)):
+            at = rows_at(side, size)
+            left[at] = source[:, :half].astype(f32)
+            left.send(at)
+            at = (slice(None), at) if right is output else (at,)
+            right[at] = source[:, half:].astype(f32)
+            right.send(*at)
 
 
 class Reduction:
@@ -257,8 +280,8 @@
         send_a, send_b, self.keep_a, self.keep_b = halves
         self.came = [flip_by(send_a, "dp", 1), flip_by(send_b, "dp", 2)]
 
-    def staged(self, kernel, outs, *args):
-        self.made = call(kernel, kernel.__name__, outs, self.info, *args, order=self.order)
+    def staged(self, kernel, outs, *args, early=()):
+        self.made = call(kernel, kernel.__name__, outs, self.info, *args, order=self.order, early=early)
         return self.made
 
     def quarters(self):
@@ -271,25 +294,39 @@
         self.keep_a, self.keep_b, self.width = keep_a, keep_b, width
         self.came = [flip_by(send_a, "dp", 2), flip_by(send_b, "dp", 1)]
 
-    def chunks(self):
-        self.piece = ((self.quarter // 2 + self.extra, self.width), bf16)
-        self.own, *sent = self.staged(
-            add_chunks, [self.piece] * 4, self.keep_a, self.came[0], self.keep_b, self.came[1]
+    def eighths(self):
+        piece = ((self.quarter + self.extra, self.width), bf16)
+        send, self.own = self.staged(
+            add_quarters, [piece] * 2, self.keep_a, self.came[0], self.keep_b, self.came[1]
         )
-        self.came = [flip_by(s, "dp", 4 * (k + 1)) for k, s in enumerate(sent)]
+        self.came = flip_by(send, "dp", 4)
+
+    def pieces(self):
+        piece = ((self.quarter // 2 + self.extra, self.width), bf16)
+        send, self.own = self.staged(add_eighths, [piece] * 2, self.own, self.came)
+        self.came = flip_by(send, "dp", 8)
 
     def total(self):
-        (total,) = self.staged(add_four, [self.piece], self.own, *self.came)
-        for bit in range(4, bits_of("dp")):
-            total = add_low(total, flip_by(total, "dp", 1 << bit))
-        rows = self.quarter // 2
-        self.small = total[rows:] if self.extra else None
-        self.own = total[:rows] if self.extra else total
-        self.came = [flip_by(self.own, "dp", 4 * (k + 1)) for k in range(3)]
-
-    def join_four(self):
+        outs = [((self.quarter // 2, self.width), bf16)]
+        outs += [((self.extra, self.width), bf16)] if self.extra else []
+        self.own, *small = [
+            functools.reduce(
+                lambda value, bit: add_low(value, flip_by(value, "dp", 1 << bit)),
+                range(4, bits_of("dp")),
+                made,
+            )
+            for made in self.staged(add_last, outs, self.own, self.came)
+        ]
+        self.small = small[0] if small else None
+        self.came = flip_by(self.own, "dp", 8)
+
+    def join_two_z(self):
+        (self.own,) = self.staged(join_pieces, [((self.quarter, self.width), bf16)], self.own, self.came)
+        self.came = flip_by(self.own, "dp", 4)
+
+    def join_z(self):
         whole = ((self.quarter, self.width), bf16)
-        self.keep_a, self.keep_b = self.staged(join_chunks, [whole] * 2, self.own, *self.came)
+        self.keep_a, self.keep_b = self.staged(join_eighths, [whole] * 2, self.own, self.came)
         self.came = [flip_by(self.keep_a, "dp", 2), flip_by(self.keep_b, "dp", 1)]
 
     def join_two(self):
@@ -300,7 +337,10 @@
         self.came = [flip_by(self.keep_a, "dp", 1), flip_by(self.keep_b, "dp", 2)]
 
     def finish(self, kernel, outs):
-        return self.staged(kernel, outs, self.keep_a, self.came[0], self.keep_b, self.came[1])
+        return self.staged(
+            kernel, outs, self.keep_a, self.came[0], self.keep_b, self.came[1],
+            early=[i for i, out in enumerate(outs) if out[0][0] > 8],
+        )
 
 
 def down_gradient(info, unit, active, unit_in, active_in, send_a, send_b, keep_a, keep_b):
@@ -312,7 +352,6 @@
             outs[side][...] = (
                 t_dot(active[:, at], unit[...]) + t_dot(active_in[:, at], unit_in[...])
             ).astype(bf16)
-            outs[side].send()
 
 
 def up_gradient(info, delta, first, delta_in, first_in, send_a, send_b, keep_a, keep_b, bias):
@@ -325,7 +364,6 @@
             outs[side][...] = (
                 t_dot(first[:, at], delta[:, columns]) + t_dot(first_in[:, at], delta_in[:, columns])
             ).astype(bf16)
-            outs[side].send()
     ones = jnp.ones((8, delta.shape[0]), bf16)
     bias[...] = dot(ones, delta[...]) + dot(ones, delta_in[...])
 
@@ -350,10 +388,9 @@
                 right = t_dot(tokens_near, key[...]) + t_dot(tokens_far, key_far[...])
             else:
                 left = t_dot(tokens_near, value[...]) + t_dot(tokens_far, value_far[...])
-                right = t_dot(branch[:, at], context[...]) + t_dot(branch_far[:, at], context_far[...])
+                right = dot(context[...], branch[:, at]) + dot(context_far[...], branch_far[:, at])
             out[:half, :narrow] = left.astype(bf16)
             out[:half, narrow:] = right.astype(bf16)
-            out.send(pl.ds(0, half))
     ones = jnp.ones((8, length), bf16)
     query_sum = dot(ones, query[...]) + dot(ones, query_far[...])
     value_sum = dot(ones, value[...]) + dot(ones, value_far[...])
@@ -365,7 +402,6 @@
     block = jnp.concatenate([block, jnp.zeros_like(block)], 0).astype(bf16)
     for out in (send_a, keep_a):
         out[half:] = block
-        out.send(pl.ds(half, SMALL))
 
 
 def pair_columns(pair):
@@ -374,80 +410,85 @@
 
 def attend(
     info, tokens, query_weight, key_weight, value_weight, query_bias, value_bias, segments, validity,
-    context, query, key, value, weights, shade, *, far,
+    context, query, key, value, raised, shares, shade, *, far,
 ):
-    length = context.shape[0]
+    length = context.shape[1]
     row = 1 - info[BT] if far else info[BT]
+    segments, validity = ready(segments, validity)
     mark = segments[pl.ds(row, 1)]
     seen = jnp.where(validity[pl.ds(row, 1)] > 0, mark, -1)
-    column = jnp.broadcast_to(mark.astype(f32), (8, length)).T[:, :1]
-    shade[...] = jnp.where(column == seen.astype(f32), 0.0, neg_large)
-    x, query_weight = ready(tokens, query_weight)
-    query[...] = (dot(x[...], query_weight[...]) + query_bias[...].astype(f32)[None]).astype(bf16)
+    column = jnp.broadcast_to(seen.astype(f32), (8, length)).T[:, :1]
+    shade[...] = jnp.where(column == mark.astype(f32), 0.0, neg_large)
+    tokens, query_weight, query_bias, value_bias = ready(tokens, query_weight, query_bias, value_bias)
+    x = tokens[rows_at(row, length)]
+    scale = 1.0 / math.sqrt(HD)
+    query[...] = (
+        (dot(x, query_weight[...]) + query_bias[...].astype(f32)[None]).astype(bf16) * bf16(scale)
+    )
     query.send()
     (key_weight,) = ready(key_weight)
-    key[...] = dot(x[...], key_weight[...]).astype(bf16)
+    key[...] = dot(x, key_weight[...]).astype(bf16)
     key.send()
     (value_weight,) = ready(value_weight)
-    value[...] = (dot(x[...], value_weight[...]) + value_bias[...].astype(f32)[None]).astype(bf16)
+    value[...] = (dot(x, value_weight[...]) + value_bias[...].astype(f32)[None]).astype(bf16)
     value.send()
     low = lax.broadcasted_iota(jnp.int32, (length, LANES), 1) < HD
-    scale = log2_e / math.sqrt(HD)
 
     def body(pair, _):
         at = pair_columns(pair)
         q, k, v = query[:, at], key[:, at], value[:, at]
-        parts = []
         for member in range(2):
-            side = jnp.where(low if member == 0 else ~low, q, jnp.zeros_like(q))
-            logits = dot_t(side, k) * scale + shade[...]
-            peak = jnp.max(logits, -1, keepdims=True)
-            raised = jnp.exp2(logits - peak)
-            total = jnp.sum(raised, -1, keepdims=True)
-            share = (raised * (1.0 / total)).astype(bf16)
-            weights[2 * pair + member] = share
-            weights.send(2 * pair + member)
-            parts.append(dot(share, v))
-        context[:, at] = jnp.where(low, parts[0], parts[1]).astype(bf16)
+            mine = low if member == 0 else ~low
+            logits = dot_t(k, jnp.where(mine, q, jnp.zeros_like(q))) + shade[...]
+            peak = jnp.max(logits, 0, keepdims=True)
+            lifted = jnp.exp(logits - peak).astype(bf16)
+            raised[2 * pair + member] = lifted
+            raised.send(2 * pair + member)
+            sums = t_dot(jnp.where(mine, v, jnp.ones_like(v)), lifted)
+            own, other = pl.ds(member * HD, HD), (1 - member) * HD
+            share = 1.0 / sums[other : other + 1]
+            shares[pl.ds(2 * pair + member, 1)] = share
+            context[pl.ds(pl.multiple_of(pair * LANES + member * HD, HD), HD)] = (
+                sums[member * HD : member * HD + HD] * share
+            ).astype(bf16)
         return 0
 
-    lax.fori_loop(0, context.shape[1] // LANES, body, 0)
+    lax.fori_loop(0, context.shape[0] // LANES, body, 0)
 
 
 def attend_back(
-    info, branch, output_weight, value, context, weights, key, query, query_weight, key_weight, value_weight,
+    info, branch, output_weight, shares, value, context, raised, key, query, query_weight, key_weight, value_weight,
     query_delta, key_delta, value_delta, part, context_delta,
 ):
     length = part.shape[0]
     branch, output_weight = ready(branch, output_weight)
-    context_delta[...] = dot_t(branch[...], output_weight[...]).astype(bf16)
-    value, context, weights, key, query = ready(value, context, weights, key, query)
+    context_delta[...] = dot_t(output_weight[...], branch[...]).astype(bf16)
+    value, context, raised, key, query = ready(value, context, raised, key, query)
     low = lax.broadcasted_iota(jnp.int32, (length, LANES), 1) < HD
     scale = 1.0 / math.sqrt(HD)
 
     def body(pair, _):
         at = pair_columns(pair)
-        q, k, v, delta = query[:, at], key[:, at], value[:, at], context_delta[:, at]
-        product = delta.astype(f32) * context[:, at].astype(f32)
+        q, k, v = query[:, at], key[:, at], value[:, at]
         queries, keys, values = [], [], []
         for member in range(2):
-            mine = low if member == 0 else ~low
-            inner = jnp.sum(jnp.where(mine, product, 0.0), -1, keepdims=True)
-            side = jnp.where(mine, delta, jnp.zeros_like(delta))
-            share = weights[2 * pair + member]
-            logit_delta = (share.astype(f32) * (dot_t(side, v) - inner)).astype(bf16)
-            queries.append(dot(logit_delta, k))
-            keys.append(t_dot(logit_delta, q))
-            values.append(t_dot(share, delta))
-        query_delta[:, at] = (jnp.where(low, queries[0], queries[1]) * scale).astype(bf16)
-        key_delta[:, at] = (jnp.where(low, keys[0], keys[1]) * scale).astype(bf16)
-        value_delta[:, at] = jnp.where(low, values[0], values[1]).astype(bf16)
+            rows = pl.ds(pl.multiple_of(pair * LANES + member * HD, HD), HD)
+            delta = context_delta[rows].astype(f32) * shares[pl.ds(2 * pair + member, 1)]
+            inner = jnp.sum(delta * context[rows].astype(f32), 0, keepdims=True)
+            delta = delta.astype(bf16)
+            none = jnp.zeros_like(delta)
+            delta = jnp.concatenate([none, delta] if member else [delta, none], 0)
+            lifted = raised[2 * pair + member]
+            logit_delta = (lifted.astype(f32) * (dot(v, delta) - inner)).astype(bf16)
+            values.append(dot_t(lifted, delta))
+            keys.append(dot(logit_delta, q))
+            queries.append(t_dot(k, logit_delta)[member * HD : member * HD + HD])
+        query_delta[:, at] = (jnp.concatenate(queries, 0) * scale).T.astype(bf16)
+        key_delta[:, at] = jnp.where(low, keys[0], keys[1]).astype(bf16)
+        value_delta[:, at] = (values[0] + values[1]).astype(bf16)
         return 0
 
     lax.fori_loop(0, query.shape[1] // LANES, body, 0)
-    query_delta.send()
-    key_delta.send()
-    value_delta.send()
     query_weight, key_weight, value_weight = ready(query_weight, key_weight, value_weight)
     part[...] = (
         dot_t(query_delta[...], query_weight[...])
@@ -474,17 +515,18 @@
 
 
 def forward(
-    info, context, output_near, x, context_in, output_far, up_far, down_far, up_near, down_near, vectors,
+    info, context, output_near, tokens, context_in, output_far, up_far, down_far, up_near, down_near, vectors,
     bias_near, bias_far, first_low, first_normed, first_scale, active_near, active_far, slope_near, slope_far,
     second_normed, second_scale, summary, total,
 ):
     length = total.shape[0]
     step = length // 2
     halves = (pl.ds(0, step), pl.ds(step, step))
-    context, output_near, x, context_in, output_far = ready(context, output_near, x, context_in, output_far)
+    base = info[BT] * length
     for at in halves:
-        heads = dot(context[at], output_near[...]) + dot(context_in[at], output_far[...])
-        normed, scale = center(x[at].astype(f32) + (heads + vectors[OB : OB + 1]))
+        heads = t_dot(context[:, at], output_near[...]) + t_dot(context_in[:, at], output_far[...])
+        x = tokens[pl.ds(pl.multiple_of(base + at.start, step), step)].astype(f32)
+        normed, scale = center(x + (heads + vectors[OB : OB + 1]))
         out = normed * vectors[FG : FG + 1] + vectors[FS : FS + 1]
         first_normed[at] = normed.astype(bf16)
         first_scale[at] = scale
@@ -492,8 +534,9 @@
         total[at] = out + vectors[DB : DB + 1]
     first_low.send()
     first_normed.send()
-
-    width = 3 * LANES
+    first_scale.send()
+
+    width = 4 * LANES
     for up, down, bias, active, slope in (
         (up_far, down_far, bias_far, active_far, slope_far),
         (up_near, down_near, bias_near, active_near, slope_near),
@@ -522,7 +565,6 @@
         second_normed[at] = normed.astype(bf16)
         second_scale[at] = scale
         total[at] = normed * vectors[SG : SG + 1]
-    second_normed.send()
     rows = [total[pl.ds(info[PLACES + k], 1)] for k in range(summary.shape[0])]
     summary[...] = jnp.concatenate(rows, 0).astype(bf16)
 
@@ -541,7 +583,7 @@
     block = min(256, count)
     score_scale = 1.0 / math.sqrt(width)
     own_passages = 4
-    upper, normed = ready(upper, normed)
+    upper, normed, scale = ready(upper, normed, scale)
     out_delta[...] = upper[...].astype(f32)
 
     def body(index, sums_in):
@@ -587,8 +629,6 @@
         delta = norm_back(out_delta[at], n, scale[at], vectors[SG : SG + 1])
         unit_delta[at] = delta.astype(bf16)
         second_delta[at] = delta
-        unit_delta.send(at)
-        second_delta.send(at)
         bias_sum += jnp.sum(delta, 0, keepdims=True)
         gain_sum += jnp.sum(out_delta[at] * n, 0, keepdims=True)
     sums[...] = jnp.concatenate(
@@ -597,14 +637,13 @@
 
 
 def unit_back(info, unit_delta, down_weight, slope, hidden_delta):
-    width = 3 * LANES
+    width = 4 * LANES
     unit_delta, down_weight, slope = ready(unit_delta, down_weight, slope)
 
     def body(index, _):
         units = rows_at(index, width)
         delta = dot_t(unit_delta[...], down_weight[units])
         hidden_delta[:, units] = (delta * slope[:, units].astype(f32)).astype(bf16)
-        hidden_delta.send(slice(None), units)
         return 0
 
     lax.fori_loop(0, down_weight.shape[0] // width, body, 0)
@@ -630,8 +669,6 @@
         delta = norm_back(out_delta, n, scale[at], vectors[FG : FG + 1])
         branch[at] = delta.astype(bf16)
         first_delta[at] = delta
-        branch.send(at)
-        first_delta.send(at)
         bias_sum += jnp.sum(delta, 0, keepdims=True)
         gain_sum += jnp.sum(out_delta * n, 0, keepdims=True)
         shift_sum += jnp.sum(out_delta, 0, keepdims=True)
@@ -692,27 +729,21 @@
 
     context_shape = ((length, width_local), bf16)
 
-    def near_rows(info, ref):
-        return ref.at[rows_at(info[BT], length)]
-
-    def far_rows(info, ref):
-        return ref.at[rows_at(1 - info[BT], length)]
-
     def attention(far):
         return call(
             functools.partial(attend, far=far),
             "attend_far" if far else "attend_near",
-            [context_shape] * 4 + [((heads_local, length, length), bf16)],
+            [((width_local, length), bf16)] + [context_shape] * 3
+            + [((heads_local, length, length), bf16), ((heads_local + -heads_local % 8, length), f32)],
             info, tokens, query_weight, key_weight, value_weight, query_bias, value_bias, segments, validity,
             scratch=[pltpu.VMEM((length, length), f32)],
-            late=(1, 2, 3, 4),
-            early=(1, 2, 3, 4),
-            parts={1: ((length, D), far_rows if far else near_rows)},
+            late=(1, 2, 3, 4, 5, 6, 7, 8) if far else (),
+            early=(1, 2, 3, 4, 5),
         )
 
-    context_far, query_far, key_far, value_far, weights_far = attention(True)
+    context_far, query_far, key_far, value_far, raised_far, shares_far = attention(True)
     context_in = swap(context_far)
-    context, query, key, value, weights = attention(False)
+    context, query, key, value, raised, shares = attention(False)
 
     row, units = ((length, D), bf16), ((length, up_weight.shape[1]), bf16)
     scale_shape = ((length, 1), f32)
@@ -725,9 +756,7 @@
         [row, row, scale_shape, units, units, units, units, row, scale_shape, ((own_passages, D), bf16)],
         info, context, output_weight, tokens, context_in, output_far, up_far, down_far, up_weight, down_weight,
         vectors, up_bias.reshape(1, -1).astype(f32), bias_far.astype(f32),
-        late=range(1, 10),
-        early=(0, 1, 3, 4, 5, 6, 7),
-        parts={3: ((length, D), near_rows)},
+        late=(8, 9), early=(0, 1, 2, 3, 4, 5, 6, 7, 8), grant=30,
         scratch=[pltpu.VMEM((length, D), f32)],
     )
     first_in = swap(first_low)
@@ -762,7 +791,8 @@
         functools.partial(loss_back, pieces=len(pieces)), "loss_back",
         [((query_count, 1), f32), ((query_count, D), f32), ((length, D), f32), row, ((8, D), f32)],
         info, *pieces, upper_delta, second_normed, second_scale, vectors,
-        late=(len(pieces) + 1, len(pieces) + 2), early=(2, 3),
+
+        late=range(len(pieces) + 1, len(pieces) + 4), final=(0, 1), grant=20 if gathered <= 256 else 40,
         scratch=[
             pltpu.VMEM((gathered, D + LANES), bf16),
             pltpu.VMEM((gathered, gathered), bf16),
@@ -775,7 +805,7 @@
 
     def through_units(name, weight, slope):
         return call(
-            unit_back, name, [units], info, unit_delta, weight, slope, late=(1, 2, 3), early=(0,), order=order
+            unit_back, name, [units], info, unit_delta, weight, slope, order=order
         )[0]
 
     delta_far = through_units("unit_back_far", down_far, slope_far)
@@ -785,47 +815,46 @@
         info, order,
         call(
             down_gradient, "down_gradient", [half] * 4, info, unit_delta, active, unit_in, active_in,
-            late=(1, 2, 3, 4), early=(0, 1, 2, 3), order=order,
+            order=order,
         ),
     )
     hidden_delta = through_units("unit_back_near", down_weight, slope)
     *halves, up_bias_sum = call(
         up_gradient, "up_gradient", [half] * 4 + [((8, up_weight.shape[1]), f32)], info, hidden_delta, first_low,
-        delta_in, first_in, late=(1, 2, 3, 4), early=(0, 1, 2, 3), order=order,
+        delta_in, first_in, order=order,
     )
     up = Reduction(info, order, halves)
     down.quarters()
     first_delta, branch, shared = call(
         first_back, "first_back", [((length, D), f32), row, ((8, D), f32)], info, delta_far, up_far,
         hidden_delta, up_weight, second_delta, first_normed, first_scale, vectors, sums,
-        late=range(1, 7), early=(0, 1), scratch=[pltpu.VMEM((length, D), f32)], order=order,
+        scratch=[pltpu.VMEM((length, D), f32)], order=order,
     )
     branch_far = swap(branch)
     shared_in = swap(shared)
 
-    def attention_back(name, branch, weights, query, key, value, context, kind):
+    def attention_back(name, branch, shares, raised, query, key, value, context, kind):
         return call(
             attend_back,
             name,
             [context_shape] * 3 + [((length, D), kind)],
-            info, branch, output_weight, value, context, weights, key, query, query_weight, key_weight, value_weight,
-            scratch=[pltpu.VMEM((length, width_local), bf16)],
-            late=range(1, 11),
-            early=(0, 1, 2),
+            info, branch, output_weight, shares, value, context, raised, key, query, query_weight, key_weight,
+            value_weight,
+            scratch=[pltpu.VMEM((width_local, length), bf16)],
             order=order,
         )
 
     query_delta, key_delta, value_delta, part = attention_back(
-        "attend_back_near", branch, weights, query, key, value, context, f32
-    )
-    down.chunks()
+        "attend_back_near", branch, shares, raised, query, key, value, context, f32
+    )
+    down.eighths()
     up.quarters()
     query_delta_far, key_delta_far, value_delta_far, part_far = attention_back(
-        "attend_back_far", branch_far, weights_far, query_far, key_far, value_far, context_far, bf16,
+        "attend_back_far", branch_far, shares_far, raised_far, query_far, key_far, value_far, context_far, bf16,
     )
     part_in = swap(part_far)
-    down.total()
-    up.chunks()
+    down.pieces()
+    up.eighths()
 
     tall = ((half_rows + SMALL, D), bf16)
     heads = Reduction(
@@ -833,20 +862,27 @@
         call(
             head_gradients, "head_gradients", [tall, half, tall, half], info, tokens, query_delta, query_delta_far,
             key_delta, key_delta_far, value_delta, value_delta_far, branch, branch_far, context, context_far,
-            shared, shared_in, up_bias_sum, late=(1, 8, 9, 10, 11, 6, 7, 2, 3, 4, 5), early=(0, 1, 2, 3), order=order,
+            shared, shared_in, up_bias_sum, order=order,
         ),
     )
-    down.join_four()
+    mark = ((8, LANES), f32)
+    down.total()
+    up.pieces()
+    heads.quarters()
+    down.join_two_z()
     up.total()
-    heads.quarters()
+    heads.eighths()
+    down.join_z()
+    up.join_two_z()
+    heads.pieces()
     down.join_two()
-    heads.chunks()
-    up.join_four()
-    (down_total,) = down.finish(finish_down, [(down_weight.shape, f32)])
+    up.join_z()
     heads.total()
+    down_total = down.finish(finish_down, [(down_weight.shape, f32), mark])[0]
     up.join_two()
-    heads.join_four()
-    (up_total,) = up.finish(finish_up, [(up_weight.shape, f32)])
+    heads.join_two_z()
+    up_total = up.finish(finish_up, [(up_weight.shape, f32), mark])[0]
+    heads.join_z()
     heads.join_two()
     wide = (query_weight.shape, f32)
     heads_total = heads.finish(finish_heads, [wide] * 3 + [(output_weight.shape, f32)])

time: 292 us -> 234 us (0.80); the launches traced: 287 us -> 234 us
  Pallas kernels: 160 us -> 98.2 us
  waiting for transfers between devices: 49.2 us -> 69.1 us
  starting transfers between devices: 62.6 us -> 56.3 us
  other arithmetic: 6.37 us -> 3.02 us
    pallas_call x30 -> x36, Pallas kernels: 160 us -> 98.2 us  [call(): pl.pallas_call(body, name=name, out_shape=[jax.ShapeDtypeStruct(*out) if...]
    ppermute x60 -> x54, waiting for transfers between devices: 49.2 us -> 69.1 us  [flip_by(): return lax.ppermute(value, axis, [(i, i ^ mask) for i in range(size)])]
    ppermute x60 -> x54, starting transfers between devices: 62.6 us -> 56.3 us  [flip_by(): return lax.ppermute(value, axis, [(i, i ^ mask) for i in range(size)])]
  transfers between devices with their start and end apart: 60 -> 54, of which waited for: 17 -> 27; matrix products, arithmetic and copies ran while one was open for 3% -> 2% of each run, Pallas kernels for 45% -> 29%
where the time goes in v3:
time: 234 us
  Pallas kernels  98.2 us (42%)
  waiting for transfers between devices  69.1 us (30%)
  starting transfers between devices  56.3 us (24%)
  local copies, waits for them, and re-layouts  5.09 us (2%)
  other arithmetic  3.02 us (1%)
    pallas_call x36, Pallas kernels, call(): pl.pallas_call(body, name=name, out_shape=[jax.ShapeDtypeStruct(*out) if...  98.2 us
    ppermute x54, waiting for transfers between devices, flip_by(): return lax.ppermute(value, axis, [(i, i ^ mask) for i in range(size)])  69.1 us
    ppermute x54, starting transfers between devices, flip_by(): return lax.ppermute(value, axis, [(i, i ^ mask) for i in range(size)])  56.3 us
  transfers between devices with their start and end apart: 54, of which 27 were waited for; matrix products, arithmetic and copies ran while one was open for 2% of the time, Pallas kernels for 29%

profile of v3, /device:TPU:0, one launch (start us, length us, event | category | flops | bytes accessed | tf_op | source)
XLA Modules:
  0.0 233.6 jit_solution(7193452184154261319)
XLA Ops:
  1.5 10.3 %attend_far.1 = (bf16[384,512]{1,0:T(8,128)(2,1)}, bf16[512,384]{1,0:T(8,128)(2,1)}, bf16[512,384]{1,0:T(8,128)(2,1)}, bf16[512,384]{1,0:T(8,128)(2,1)}, bf16[6,512,512]{2,1,0:T(8,128)(2,1)}, /*index=5*/f32[8,512]{1,0:T(8,128)}) custom-call(s32[9]{0:T(128)S(1)} %concatenate.35.refs_0_, bf16[1024,768]{1,0:T(8,128)(2,1)} %refs_1_.5, bf16[768,384]{1,0:T(8,128)(2,1)} %refs_9_.5, ...), custom_call_target="tpu_custom_call" | custom-call | flops 20700000256 | bytes 1 | tf_op jit(solution)/shard_map/attend_far/pallas_call | solution.py:140
  13.6 6.9 %attend_near.1 = (bf16[384,512]{1,0:T(8,128)(2,1)S(1)}, bf16[512,384]{1,0:T(8,128)(2,1)}, bf16[512,384]{1,0:T(8,128)(2,1)}, bf16[512,384]{1,0:T(8,128)(2,1)}, bf...) custom-call(s32[9]{0:T(128)S(1)} %concatenate.35.refs_0_, bf16[1024,768]{1,0:T(8,128)(2,1)S(1)} %copy-done.4, ...), custom_call_target="tpu_custom_call" | custom-call | flops 20700000256 | bytes 1 | tf_op jit(solution)/shard_map/attend_near/pallas_call | solution.py:140
  22.7 14.6 %forward.1 = (bf16[512,768]{1,0:T(8,128)(2,1)}, bf16[512,768]{1,0:T(8,128)(2,1)}, f32[512,1]{1,0:T(8,128)}, bf16[512,1536]{1,0:T(8,128)(2,1)}, bf16[512,1536]{1,...) custom-call(s32[9]{0:T(128)S(1)} %concatenate.35.refs_0_, ...), custom_call_target="tpu_custom_call" | custom-call | flops 39099998208 | bytes 1 | tf_op jit(solution)/shard_map/forward/pallas_call | solution.py:140
  38.6 2.9 %collective-permute-start.6 = (bf16[16,896]{1,0:T(8,128)(2,1)S(1)}, bf16[16,896]{1,0:T(8,128)(2,1)S(1)}, u32[]{:S(2)}, u32[]{:S(2)}) collective-permute-start(bf16[16,896]{1,0:T(8,128)(2,1)S(1)} %maximum_maximum_fusion), channel_id=1, source_target_pairs={{0,2},{2,0},{4,6},{6,4},{8,10},{10,8},{12,14},{14,12},{16,18},{18,... | collective-permute-start | bytes 86024 | tf_op jit(solution)/shard_map/ppermute | solution.py:37
  41.5 1.9 collective-permute-done.6
  43.4 2.1 collective-permute-start.7
  45.5 2.2 collective-permute-done.7
  47.6 2.1 collective-permute-start.8
  49.8 2.6 %collective-permute-start.9 = (bf16[64,896]{1,0:T(8,128)(2,1)S(1)}, bf16[64,896]{1,0:T(8,128)(2,1)S(1)}, u32[]{:S(2)}, u32[]{:S(2)}) collective-permute-start(bf16[64,896]{1,0:T(8,128)(2,1)S(1)} %maximum_select_fusion.refs_1_), channel_id=1, source_target_pairs={{0,16},{2,18},{4,20},{6,22},{8,24},{10,26},{12,28},{14,30},{16,0},... | collective-permute-start | bytes 344072 | tf_op jit(solution)/shard_map/ppermute | solution.py:37
  53.3 6.2 %collective-permute-done.9.refs_3_ = bf16[64,896]{1,0:T(8,128)(2,1)S(1)} collective-permute-done((bf16[64,896]{1,0:T(8,128)(2,1)S(1)}, bf16[64,896]{1,0:T(8,128)(2,1)S(1)}, u32[]{:S(2)}, u32[]{:S(2)}) %collective-permute-start.9) | collective-permute-done | bytes 114720 | tf_op jit(solution)/shard_map/ppermute | solution.py:37
  59.5 3.7 %loss_back.1 = (f32[8,1]{1,0:T(8,128)S(1)}, f32[8,768]{1,0:T(8,128)}, f32[512,768]{1,0:T(8,128)S(1)}, bf16[512,768]{1,0:T(8,128)(2,1)S(1)}, f32[8,768]{1,0:T(8,128)S(1)}) custom-call(s32[9]{0:T(128)S(1)} %concatenate.35.refs_0_, bf16[64,896]{1,0:T(8,128)(2,1)S(1)} %maximum_select_fusion.refs_1_, bf16[64,896]{1,0:T(8,128)(2,1)S(1)} %collective-permute-done.8.refs_2_, ...), custom_call_target="tpu_custom_call" | custom-call | flops 13799999488 | bytes 1 | tf_op jit(solution)/shard_map/loss_back/pallas_call | solution.py:140
  63.3 3.8 %unit_back_far.1.refs_5_.refs_1_ = bf16[512,1536]{1,0:T(8,128)(2,1)S(1)} custom-call(s32[9]{0:T(128)S(1)} %concatenate.35.refs_0_, bf16[512,768]{1,0:T(8,128)(2,1)S(1)} %get-tuple-element.121.refs_1_, bf16[1536,768]{1,0:T(8,128)(2,1)} %collective-permute-done.3.refs_7_.refs_2_, bf16[512,1536]{1,0:T(8,128)(2,1)S(1)} %copy-done.19), custom_call_target="tpu_custom_call" | custom-call | flops 13799999488 | bytes 1 | tf_op jit(solution)/shard_map/unit_back_far/pallas_call | solution.py:140
  67.7 3.2 %down_gradient.1 = (bf16[384,768]{1,0:T(8,128)(2,1)S(1)}, bf16[384,768]{1,0:T(8,128)(2,1)S(1)}, bf16[384,768]{1,0:T(8,128)(2,1)S(1)}, bf16[384,768]{1,0:T(8,128)(2,1)S(1)}) custom-call(s32[9]{0:T(128)S(1)} %concatenate.35.refs_0_, bf16[512,768]{1,0:T(8,128)(2,1)S(1)} %get-tuple-element.121.refs_1_, bf16[512,1536]{1,0:T(8,128)(2,1)S(1)} %copy-done.22, ...), custom_call_target="tpu_custom_call" | custom-call | flops 16099999744 | bytes 1 | tf_op jit(solution)/shard_map/down_gradient/pallas_call | solution.py:140
  70.9 1.6 collective-permute-start.13
  72.5 1.5 collective-permute-start.14
  74.0 3.6 %unit_back_near.1.refs_1_.refs_5_.refs_3_ = bf16[512,1536]{1,0:T(8,128)(2,1)S(1)} custom-call(s32[9]{0:T(128)S(1)} %concatenate.35.refs_0_, bf16[512,768]{1,0:T(8,128)(2,1)S(1)} %get-tuple-element.121.refs_1_, bf16[1536,768]{1,0:T(8,128)(2,1)} %refs_2_.9, bf16[512,1536]{1,0:T(8,128)(2,1)S(1)} %copy-done.18, ...), custom_call_target="tpu_custom_call" | custom-call | flops 13799999488 | bytes 1 | tf_op jit(solution)/shard_map/unit_back_near/pallas_call | solution.py:140
  77.6 3.6 %up_gradient.1 = (bf16[384,768]{1,0:T(8,128)(2,1)S(1)}, bf16[384,768]{1,0:T(8,128)(2,1)S(1)}, bf16[384,768]{1,0:T(8,128)(2,1)S(1)}, bf16[384,768]{1,0:T(8,128)(2,1)S(1)}, f32[8,1536]{1,0:T(8,128)S(1)}) custom-call(s32[9]{0:T(128)S(1)} %concatenate.35.refs_0_, bf16[512,1536]{1,0:T(8,128)(2,1)S(1)} %unit_back_near.1.refs_1_.refs_5_.refs_3_, ...), custom_call_target="tpu_custom_call" | custom-call | flops 16099999744 | bytes 1 | tf_op jit(solution)/shard_map/up_gradient/pallas_call | solution.py:140
  82.3 4.9 %collective-permute-done.13.refs_2_ = bf16[384,768]{1,0:T(8,128)(2,1)S(1)} collective-permute-done((bf16[384,768]{1,0:T(8,128)(2,1)S(1)}, bf16[384,768]{1,0:T(8,128)(2,1)S(1)}, u32[]{:S(2)}, u32[]{:S(2)}) %collective-permute-start.13) | collective-permute-done | bytes 589856 | tf_op jit(solution)/shard_map/ppermute | solution.py:37
  87.2 1.5 collective-permute-done.14.refs_4_
  90.0 5.9 %first_back.1 = (f32[512,768]{1,0:T(8,128)S(1)}, bf16[512,768]{1,0:T(8,128)(2,1)S(1)}, f32[8,768]{1,0:T(8,128)S(1)}) custom-call(s32[9]{0:T(128)S(1)} %concatenate.35.refs_0_, bf16[512,1536]{1,0:T(8,128)(2,1)S(1)} %unit_back_far.1.refs_5_.refs_1_, bf16[768,1536]{1,0:T(8,128)(2,1)} %collective-permute-done.2.refs_6_.refs_2_, ...), custom_call_target="tpu_custom_call" | custom-call | flops 20700000256 | bytes 1 | tf_op jit(solution)/shard_map/first_back/pallas_call | solution.py:140
  95.9 1.6 collective-permute-start.20
  98.1 6.2 %attend_back_near.1 = (bf16[512,384]{1,0:T(8,128)(2,1)S(1)}, bf16[512,384]{1,0:T(8,128)(2,1)S(1)}, bf16[512,384]{1,0:T(8,128)(2,1)S(1)}, f32[512,768]{1,0:T(8,128)S(1)}) custom-call(s32[9]{0:T(128)S(1)} %concatenate.35.refs_0_, bf16[512,768]{1,0:T(8,128)(2,1)S(1)} %get-tuple-element.138.refs_1_.refs_8_, bf16[384,768]{1,0:T(8,128)(2,1)S(1)} %copy-done.13, ...), custom_call_target="tpu_custom_call" | custom-call | flops 23000000512 | bytes 1 | tf_op jit(solution)/shard_map/attend_back_near/pallas_call | solution.py:140
  104.3 2.1 collective-permute-done.20.refs_2_
  108.2 1.4 collective-permute-start.24
  110.1 1.8 collective-permute-start.26
  112.0 7.8 %attend_back_far.1 = (bf16[512,384]{1,0:T(8,128)(2,1)S(1)}, bf16[512,384]{1,0:T(8,128)(2,1)S(1)}, bf16[512,384]{1,0:T(8,128)(2,1)S(1)}, bf16[512,768]{1,0:T(8,128)(2,1)}) custom-call(s32[9]{0:T(128)S(1)} %concatenate.35.refs_0_, bf16[512,768]{1,0:T(8,128)(2,1)S(1)} %collective-permute-done.17.refs_1_.refs_9_, bf16[384,768]{1,0:T(8,128)(2,1)S(1)} %copy-done.13, ...), custom_call_target="tpu_custom_call" | custom-call | flops 23000000512 | bytes 1 | tf_op jit(solution)/shard_map/attend_back_far/pallas_call | solution.py:140
  120.4 2.2 collective-permute-start.30
  123.2 4.7 %head_gradients.1 = (bf16[400,768]{1,0:T(8,128)(2,1)S(1)}, bf16[384,768]{1,0:T(8,128)(2,1)S(1)}, bf16[400,768]{1,0:T(8,128)(2,1)S(1)}, bf16[384,768]{1,0:T(8,128)(2,1)S(1)}) custom-call(s32[9]{0:T(128)S(1)} %concatenate.35.refs_0_, bf16[1024,768]{1,0:T(8,128)(2,1)S(1)} %copy-done.4, bf16[512,384]{1,0:T(8,128)(2,1)S(1)} %get-tuple-element.161.refs_2_, ...), custom_call_target="tpu_custom_call" | custom-call | flops 18400000000 | bytes 1 | tf_op jit(solution)/shard_map/head_gradients/pallas_call | solution.py:140
  127.9 1.5 collective-permute-start.27
  130.0 1.1 collective-permute-start.29
  132.5 8.2 %collective-permute-done.29.refs_2_ = bf16[192,768]{1,0:T(8,128)(2,1)S(1)} collective-permute-done((bf16[192,768]{1,0:T(8,128)(2,1)S(1)}, bf16[192,768]{1,0:T(8,128)(2,1)S(1)}, u32[]{:S(2)}, u32[]{:S(2)}) %collective-permute-start.29) | collective-permute-done | bytes 294944 | tf_op jit(solution)/shard_map/ppermute | solution.py:37
  141.4 1.8 collective-permute-done.28.refs_4_
  144.5 1.2 collective-permute-start.32
  146.3 1.4 collective-permute-start.37
  147.7 1.1 collective-permute-done.33.refs_2_
  149.5 2.1 collective-permute-done.32.refs_4_
  152.3 1.9 collective-permute-start.35
  154.1 4.8 %collective-permute-done.37.refs_2_ = bf16[192,768]{1,0:T(8,128)(2,1)S(1)} collective-permute-done((bf16[192,768]{1,0:T(8,128)(2,1)S(1)}, bf16[192,768]{1,0:T(8,128)(2,1)S(1)}, u32[]{:S(2)}, u32[]{:S(2)}) %collective-permute-start.37) | collective-permute-done | bytes 294944 | tf_op jit(solution)/shard_map/ppermute | solution.py:37
  159.6 1.0 collective-permute-start.41
  161.3 1.6 collective-permute-start.40
  162.9 2.9 %collective-permute-done.35.refs_2_ = bf16[208,768]{1,0:T(8,128)(2,1)S(1)} collective-permute-done((bf16[208,768]{1,0:T(8,128)(2,1)S(1)}, bf16[208,768]{1,0:T(8,128)(2,1)S(1)}, u32[]{:S(2)}, u32[]{:S(2)}) %collective-permute-start.35) | collective-permute-done | bytes 319520 | tf_op jit(solution)/shard_map/ppermute | solution.py:37
  166.4 1.3 collective-permute-start.38
  168.7 1.3 collective-permute-start.45
  170.0 1.9 collective-permute-start.46
  171.8 2.1 collective-permute-done.39.refs_2_
  174.5 1.3 collective-permute-start.43
  175.8 1.2 collective-permute-start.44
  177.6 5.3 %collective-permute-done.45.refs_2_ = bf16[384,768]{1,0:T(8,128)(2,1)S(1)} collective-permute-done((bf16[384,768]{1,0:T(8,128)(2,1)S(1)}, bf16[384,768]{1,0:T(8,128)(2,1)S(1)}, u32[]{:S(2)}, u32[]{:S(2)}) %collective-permute-start.45) | collective-permute-done | bytes 589856 | tf_op jit(solution)/shard_map/ppermute | solution.py:37
  182.9 1.1 collective-permute-done.46.refs_4_
  184.0 2.8 %finish_down.1 = (f32[1536,768]{1,0:T(8,128)}, f32[8,128]{1,0:T(8,128)S(1)}) custom-call(s32[9]{0:T(128)S(1)} %concatenate.35.refs_0_, bf16[384,768]{1,0:T(8,128)(2,1)S(1)} %get-tuple-element.195.refs_1_, bf16[384,768]{1,0:T(8,128)(2,1)S(1)} %collective-permute-done.45.refs_2_, bf16[384,768]{1,0:T(8,128)(2,1)S(1)} %get-tuple-element.191.refs_3_, ...), custom_call_target="tpu_custom_call" | custom-call | flops 9200000000 | bytes 1 | tf_op jit(solution)/shard_map/finish_down/pallas_call | solution.py:140
  186.8 1.6 collective-permute-done.43.refs_2_
  189.4 1.5 collective-permute-start.49
  190.9 2.6 %collective-permute-start.42 = (bf16[96,768]{1,0:T(8,128)(2,1)S(1)}, bf16[96,768]{1,0:T(8,128)(2,1)S(1)}, u32[]{:S(2)}, u32[]{:S(2)}) collective-permute-start(bf16[96,768]{1,0:T(8,128)(2,1)S(1)} %get-tuple-element.193.refs_1_), channel_id=1, source_target_pairs={{0,16},{2,18},{4,20},{6,22},{8,24},{10,26},{12,28},{14,30},{16,0},... | collective-permute-start | bytes 442376 | tf_op jit(solution)/shard_map/ppermute | solution.py:37
  193.5 3.4 %collective-permute-done.42.refs_2_ = bf16[96,768]{1,0:T(8,128)(2,1)S(1)} collective-permute-done((bf16[96,768]{1,0:T(8,128)(2,1)S(1)}, bf16[96,768]{1,0:T(8,128)(2,1)S(1)}, u32[]{:S(2)}, u32[]{:S(2)}) %collective-permute-start.42) | collective-permute-done | bytes 147488 | tf_op jit(solution)/shard_map/ppermute | solution.py:37
  197.5 4.6 %collective-permute-start.47 = (bf16[192,768]{1,0:T(8,128)(2,1)S(1)}, bf16[192,768]{1,0:T(8,128)(2,1)S(1)}, u32[]{:S(2)}, u32[]{:S(2)}) collective-permute-start(bf16[192,768]{1,0:T(8,128)(2,1)S(1)} %join_pieces.5.refs_5_.refs_1_), channel_id=1, source_target_pairs={{0,8},{2,10},{4,12},{6,14},{8,0},{10,2},{12,4},{14,6},{16,24},{18,... | collective-permute-start | bytes 884744 | tf_op jit(solution)/shard_map/ppermute | solution.py:37
  202.1 2.8 %finish_up.1 = (f32[768,1536]{1,0:T(8,128)}, f32[8,128]{1,0:T(8,128)S(1)}) custom-call(s32[9]{0:T(128)S(1)} %concatenate.35.refs_0_, bf16[384,768]{1,0:T(8,128)(2,1)S(1)} %get-tuple-element.199.refs_1_, bf16[384,768]{1,0:T(8,128)(2,1)S(1)} %collective-permute-done.48.refs_2_, bf16[384,768]{1,0:T(8,128)(2,1)S(1)} %get-tuple-element.198.refs_3_, ...), custom_call_target="tpu_custom_call" | custom-call | flops 9200000000 | bytes 1 | tf_op jit(solution)/shard_map/finish_up/pallas_call | solution.py:140
  205.0 1.9 collective-permute-done.47.refs_2_
  208.3 7.5 %collective-permute-done.50.refs_2_ = bf16[192,768]{1,0:T(8,128)(2,1)S(1)} collective-permute-done((bf16[192,768]{1,0:T(8,128)(2,1)S(1)}, bf16[192,768]{1,0:T(8,128)(2,1)S(1)}, u32[]{:S(2)}, u32[]{:S(2)}) %collective-permute-start.50) | collective-permute-done | bytes 294944 | tf_op jit(solution)/shard_map/ppermute | solution.py:37
  215.8 1.4 collective-permute-done.51.refs_4_
  217.2 1.6 join_quarters.5
  218.9 2.4 %collective-permute-start.53 = (bf16[384,768]{1,0:T(8,128)(2,1)}, bf16[384,768]{1,0:T(8,128)(2,1)}, u32[]{:S(2)}, u32[]{:S(2)}) collective-permute-start(bf16[384,768]{1,0:T(8,128)(2,1)} %get-tuple-element.204.refs_3_.refs_5_), channel_id=1, source_target_pairs={{0,4},{2,6},{4,0},{6,2},{8,12},{10,14},{12,8},{14,10},{16,20},{18,... | collective-permute-start | bytes 1769480 | tf_op jit(solution)/shard_map/ppermute | solution.py:37
  222.0 2.3 add_convert_fusion
  226.1 3.0 %collective-permute-done.52.refs_2_ = bf16[384,768]{1,0:T(8,128)(2,1)} collective-permute-done((bf16[384,768]{1,0:T(8,128)(2,1)}, bf16[384,768]{1,0:T(8,128)(2,1)}, u32[]{:S(2)}, u32[]{:S(2)}) %collective-permute-start.52) | collective-permute-done | bytes 589856 | tf_op jit(solution)/shard_map/ppermute | solution.py:37
  229.5 3.9 %finish_heads.1 = (f32[768,384]{1,0:T(8,128)}, f32[768,384]{1,0:T(8,128)}, f32[768,384]{1,0:T(8,128)}, f32[384,768]{1,0:T(8,128)}) custom-call(s32[9]{0:T(128)S(1)} %concatenate.35.refs_0_, bf16[384,768]{1,0:T(8,128)(2,1)} %get-tuple-element.203.refs_1_, bf16[384,768]{1,0:T(8,128)(2,1)} %collective-permute-done.52.refs_2_, ...), custom_call_target="tpu_custom_call" | custom-call | flops 9200000000 | bytes 1 | tf_op jit(solution)/shard_map/finish_heads/pallas_call | solution.py:140
  (197 shorter events, 29.4 us)
Async XLA Ops:
  1.4 12.1 %copy-start.4 = (bf16[1024,768]{1,0:T(8,128)(2,1)S(1)}, bf16[1024,768]{1,0:T(8,128)(2,1)}, u32[]{:S(2)}) copy-start(bf16[1024,768]{1,0:T(8,128)(2,1)} %refs_1_.5) | copy-start | bytes 4718596
  1.4 12.1 %copy-start.6 = (bf16[768,384]{1,0:T(8,128)(2,1)S(1)}, bf16[768,384]{1,0:T(8,128)(2,1)}, u32[]{:S(2)}) copy-start(bf16[768,384]{1,0:T(8,128)(2,1)} %refs_9_.5) | copy-start | bytes 1769476
  1.5 12.1 %copy-start.8 = (bf16[768,384]{1,0:T(8,128)(2,1)S(1)}, bf16[768,384]{1,0:T(8,128)(2,1)}, u32[]{:S(2)}) copy-start(bf16[768,384]{1,0:T(8,128)(2,1)} %refs_10_.3) | copy-start | bytes 1769476
  1.5 12.1 %copy-start.10 = (bf16[768,384]{1,0:T(8,128)(2,1)S(1)}, bf16[768,384]{1,0:T(8,128)(2,1)}, u32[]{:S(2)}) copy-start(bf16[768,384]{1,0:T(8,128)(2,1)} %refs_11_.3) | copy-start | bytes 1769476
  1.5 12.1 %copy-start.14 = (s32[2,512]{1,0:T(2,128)S(1)}, s32[2,512]{1,0:T(2,128)}, u32[]{:S(2)}) copy-start(s32[2,512]{1,0:T(2,128)} %refs_7_.3) | copy-start | bytes 12292
  1.5 12.1 %copy-start.15 = (s32[2,512]{1,0:T(2,128)S(1)}, s32[2,512]{1,0:T(2,128)}, u32[]{:S(2)}) copy-start(s32[2,512]{1,0:T(2,128)} %refs_8_.4) | copy-start | bytes 12292
  1.5 12.1 %copy-start.16 = (bf16[384]{0:T(512)(128)(2,1)S(1)}, bf16[384]{0:T(512)(128)(2,1)}, u32[]{:S(2)}) copy-start(bf16[384]{0:T(512)(128)(2,1)} %refs_5_.4) | copy-start | bytes 2308
  1.5 12.1 %copy-start.17 = (bf16[384]{0:T(512)(128)(2,1)S(1)}, bf16[384]{0:T(512)(128)(2,1)}, u32[]{:S(2)}) copy-start(bf16[384]{0:T(512)(128)(2,1)} %refs_6_.3) | copy-start | bytes 2308
  11.8 9.7 %collective-permute-start = (bf16[384,512]{1,0:T(8,128)(2,1)}, bf16[384,512]{1,0:T(8,128)(2,1)}, u32[]{:S(2)}, u32[]{:S(2)}) collective-permute-start(bf16[384,512]{1,0:T(8,128)(2,1)} %get-tuple-element.115.refs_5_.refs_11_), channel_id=1, source_target_pairs={{0,1},{1,0},{2,3},{3,2},{4,5},{5,4},{6,7},{7,6},{8,9},{9,8},{10,11... | collective-permute-start | bytes 1179656 | tf_op jit(solution)/shard_map/ppermute | solution.py:37
  12.4 9.2 %collective-permute-start.1 = (bf16[384,768]{1,0:T(8,128)(2,1)S(1)}, bf16[384,768]{1,0:T(8,128)(2,1)S(1)}, u32[]{:S(2)}, u32[]{:S(2)}) collective-permute-start(bf16[384,768]{1,0:T(8,128)(2,1)S(1)} %copy-done.12), channel_id=1, source_target_pairs={{0,1},{1,0},{2,3},{3,2},{4,5},{5,4},{6,7},{7,6},{8,9},{9,8},{10,11... | collective-permute-start | bytes 1769480 | tf_op jit(solution)/shard_map/ppermute | solution.py:37
  12.5 9.1 %collective-permute-start.2 = (bf16[768,1536]{1,0:T(8,128)(2,1)}, bf16[768,1536]{1,0:T(8,128)(2,1)}, u32[]{:S(2)}, u32[]{:S(2)}) collective-permute-start(bf16[768,1536]{1,0:T(8,128)(2,1)} %refs_4_.5), channel_id=1, source_target_pairs={{0,1},{1,0},{2,3},{3,2},{4,5},{5,4},{6,7},{7,6},{8,9},{9,8},{10,11... | collective-permute-start | bytes 7077896 | tf_op jit(solution)/shard_map/ppermute | solution.py:37
  12.9 8.8 %collective-permute-start.3 = (bf16[1536,768]{1,0:T(8,128)(2,1)}, bf16[1536,768]{1,0:T(8,128)(2,1)}, u32[]{:S(2)}, u32[]{:S(2)}) collective-permute-start(bf16[1536,768]{1,0:T(8,128)(2,1)} %refs_2_.9), channel_id=1, source_target_pairs={{0,1},{1,0},{2,3},{3,2},{4,5},{5,4},{6,7},{7,6},{8,9},{9,8},{10,11... | collective-permute-start | bytes 7077896 | tf_op jit(solution)/shard_map/ppermute | solution.py:37
  13.1 8.4 %collective-permute-start.4 = (bf16[1,1536]{1,0:T(2,128)(2,1)S(1)}, bf16[1,1536]{1,0:T(2,128)(2,1)S(1)}, u32[]{:S(2)}, u32[]{:S(2)}) collective-permute-start(bf16[1,1536]{1,0:T(2,128)(2,1)S(1)} %convert_element_type.23), channel_id=1, source_target_pairs={{0,1},{1,0},{2,3},{3,2},{4,5},{5,4},{6,7},{7,6},{8,9},{9,8},{10,11... | collective-permute-start | bytes 9224 | tf_op jit(solution)/shard_map/ppermute | solution.py:37
  22.7 15.9 %copy-start.36 = (bf16[8,768]{1,0:T(8,128)(2,1)S(1)}, bf16[8,768]{1,0:T(8,128)(2,1)}, u32[]{:S(2)}) copy-start(bf16[8,768]{1,0:T(8,128)(2,1)} %param.26) | copy-start | bytes 36868
  37.3 1.3 collective-permute-start.5
  38.6 4.7 %collective-permute-start.6 = (bf16[16,896]{1,0:T(8,128)(2,1)S(1)}, bf16[16,896]{1,0:T(8,128)(2,1)S(1)}, u32[]{:S(2)}, u32[]{:S(2)}) collective-permute-start(bf16[16,896]{1,0:T(8,128)(2,1)S(1)} %maximum_maximum_fusion), channel_id=1, source_target_pairs={{0,2},{2,0},{4,6},{6,4},{8,10},{10,8},{12,14},{14,12},{16,18},{18,... | collective-permute-start | bytes 86024 | tf_op jit(solution)/shard_map/ppermute | solution.py:37
  43.4 4.3 %collective-permute-start.7 = (bf16[32,896]{1,0:T(8,128)(2,1)S(1)}, bf16[32,896]{1,0:T(8,128)(2,1)S(1)}, u32[]{:S(2)}, u32[]{:S(2)}) collective-permute-start(bf16[32,896]{1,0:T(8,128)(2,1)S(1)} %maximum_select_fusion.1), channel_id=1, source_target_pairs={{0,4},{2,6},{4,0},{6,2},{8,12},{10,14},{12,8},{14,10},{16,20},{18,... | collective-permute-start | bytes 172040 | tf_op jit(solution)/shard_map/ppermute | solution.py:37
  47.6 5.7 %collective-permute-start.8 = (bf16[64,896]{1,0:T(8,128)(2,1)S(1)}, bf16[64,896]{1,0:T(8,128)(2,1)S(1)}, u32[]{:S(2)}, u32[]{:S(2)}) collective-permute-start(bf16[64,896]{1,0:T(8,128)(2,1)S(1)} %maximum_select_fusion.refs_1_), channel_id=1, source_target_pairs={{0,8},{2,10},{4,12},{6,14},{8,0},{10,2},{12,4},{14,6},{16,24},{18,... | collective-permute-start | bytes 344072 | tf_op jit(solution)/shard_map/ppermute | solution.py:37
  49.8 9.7 %collective-permute-start.9 = (bf16[64,896]{1,0:T(8,128)(2,1)S(1)}, bf16[64,896]{1,0:T(8,128)(2,1)S(1)}, u32[]{:S(2)}, u32[]{:S(2)}) collective-permute-start(bf16[64,896]{1,0:T(8,128)(2,1)S(1)} %maximum_select_fusion.refs_1_), channel_id=1, source_target_pairs={{0,16},{2,18},{4,20},{6,22},{8,24},{10,26},{12,28},{14,30},{16,0},... | collective-permute-start | bytes 344072 | tf_op jit(solution)/shard_map/ppermute | solution.py:37
  52.4 7.1 %collective-permute-start.10 = (bf16[64,896]{1,0:T(8,128)(2,1)S(1)}, bf16[64,896]{1,0:T(8,128)(2,1)S(1)}, u32[]{:S(2)}, u32[]{:S(2)}) collective-permute-start(bf16[64,896]{1,0:T(8,128)(2,1)S(1)} %maximum_select_fusion.refs_1_), channel_id=1, source_target_pairs={{0,24},{2,26},{4,28},{6,30},{8,16},{10,18},{12,20},{14,22},{16,8},... | collective-permute-start | bytes 344072 | tf_op jit(solution)/shard_map/ppermute | solution.py:37
  52.4 15.3 %collective-permute-start.12 = (bf16[512,1536]{1,0:T(8,128)(2,1)}, bf16[512,1536]{1,0:T(8,128)(2,1)S(1)}, u32[]{:S(2)}, u32[]{:S(2)}) collective-permute-start(bf16[512,1536]{1,0:T(8,128)(2,1)} %get-tuple-element.125), channel_id=1, source_target_pairs={{0,1},{1,0},{2,3},{3,2},{4,5},{5,4},{6,7},{7,6},{8,9},{9,8},{10,11... | collective-permute-start | bytes 4718600 | tf_op jit(solution)/shard_map/ppermute | solution.py:37
  52.4 25.2 %collective-permute-start.16 = (bf16[512,768]{1,0:T(8,128)(2,1)}, bf16[512,768]{1,0:T(8,128)(2,1)S(1)}, u32[]{:S(2)}, u32[]{:S(2)}) collective-permute-start(bf16[512,768]{1,0:T(8,128)(2,1)} %get-tuple-element.134.refs_2_), channel_id=1, source_target_pairs={{0,1},{1,0},{2,3},{3,2},{4,5},{5,4},{6,7},{7,6},{8,9},{9,8},{10,11... | collective-permute-start | bytes 2359304 | tf_op jit(solution)/shard_map/ppermute | solution.py:37
  63.2 4.5 %collective-permute-start.11 = (bf16[512,768]{1,0:T(8,128)(2,1)S(1)}, bf16[512,768]{1,0:T(8,128)(2,1)S(1)}, u32[]{:S(2)}, u32[]{:S(2)}) collective-permute-start(bf16[512,768]{1,0:T(8,128)(2,1)S(1)} %get-tuple-element.121.refs_1_), channel_id=1, source_target_pairs={{0,1},{1,0},{2,3},{3,2},{4,5},{5,4},{6,7},{7,6},{8,9},{9,8},{10,11... | collective-permute-start | bytes 2359304 | tf_op jit(solution)/shard_map/ppermute | solution.py:37
  67.1 10.5 %collective-permute-start.15 = (bf16[512,1536]{1,0:T(8,128)(2,1)S(1)}, bf16[512,1536]{1,0:T(8,128)(2,1)S(1)}, u32[]{:S(2)}, u32[]{:S(2)}) collective-permute-start(bf16[512,1536]{1,0:T(8,128)(2,1)S(1)} %unit_back_far.1.refs_5_.refs_1_), channel_id=1, source_target_pairs={{0,1},{1,0},{2,3},{3,2},{4,5},{5,4},{6,7},{7,6},{8,9},{9,8},{10,11... | collective-permute-start | bytes 4718600 | tf_op jit(solution)/shard_map/ppermute | solution.py:37
  70.9 16.3 %collective-permute-start.13 = (bf16[384,768]{1,0:T(8,128)(2,1)S(1)}, bf16[384,768]{1,0:T(8,128)(2,1)S(1)}, u32[]{:S(2)}, u32[]{:S(2)}) collective-permute-start(bf16[384,768]{1,0:T(8,128)(2,1)S(1)} %get-tuple-element.132), channel_id=1, source_target_pairs={{0,2},{2,0},{4,6},{6,4},{8,10},{10,8},{12,14},{14,12},{16,18},{18,... | collective-permute-start | bytes 1769480 | tf_op jit(solution)/shard_map/ppermute | solution.py:37
  72.5 16.2 %collective-permute-start.14 = (bf16[384,768]{1,0:T(8,128)(2,1)S(1)}, bf16[384,768]{1,0:T(8,128)(2,1)S(1)}, u32[]{:S(2)}, u32[]{:S(2)}) collective-permute-start(bf16[384,768]{1,0:T(8,128)(2,1)S(1)} %get-tuple-element.133), channel_id=1, source_target_pairs={{0,4},{2,6},{4,0},{6,2},{8,12},{10,14},{12,8},{14,10},{16,20},{18,... | collective-permute-start | bytes 1769480 | tf_op jit(solution)/shard_map/ppermute | solution.py:37
  81.2 26.1 %collective-permute-start.18 = (bf16[384,768]{1,0:T(8,128)(2,1)S(1)}, bf16[384,768]{1,0:T(8,128)(2,1)S(1)}, u32[]{:S(2)}, u32[]{:S(2)}) collective-permute-start(bf16[384,768]{1,0:T(8,128)(2,1)S(1)} %get-tuple-element.152), channel_id=1, source_target_pairs={{0,2},{2,0},{4,6},{6,4},{8,10},{10,8},{12,14},{14,12},{16,18},{18,... | collective-permute-start | bytes 1769480 | tf_op jit(solution)/shard_map/ppermute | solution.py:37
  81.7 25.6 %collective-permute-start.19 = (bf16[384,768]{1,0:T(8,128)(2,1)S(1)}, bf16[384,768]{1,0:T(8,128)(2,1)S(1)}, u32[]{:S(2)}, u32[]{:S(2)}) collective-permute-start(bf16[384,768]{1,0:T(8,128)(2,1)S(1)} %get-tuple-element.154), channel_id=1, source_target_pairs={{0,4},{2,6},{4,0},{6,2},{8,12},{10,14},{12,8},{14,10},{16,20},{18,... | collective-permute-start | bytes 1769480 | tf_op jit(solution)/shard_map/ppermute | solution.py:37
  95.8 16.1 %collective-permute-start.17 = (bf16[512,768]{1,0:T(8,128)(2,1)S(1)}, bf16[512,768]{1,0:T(8,128)(2,1)S(1)}, u32[]{:S(2)}, u32[]{:S(2)}) collective-permute-start(bf16[512,768]{1,0:T(8,128)(2,1)S(1)} %get-tuple-element.138.refs_1_.refs_8_), channel_id=1, source_target_pairs={{0,1},{1,0},{2,3},{3,2},{4,5},{5,4},{6,7},{7,6},{8,9},{9,8},{10,11... | collective-permute-start | bytes 2359304 | tf_op jit(solution)/shard_map/ppermute | solution.py:37
  95.9 10.5 %collective-permute-start.20 = (bf16[192,768]{1,0:T(8,128)(2,1)S(1)}, bf16[192,768]{1,0:T(8,128)(2,1)S(1)}, u32[]{:S(2)}, u32[]{:S(2)}) collective-permute-start(bf16[192,768]{1,0:T(8,128)(2,1)S(1)} %get-tuple-element.156), channel_id=1, source_target_pairs={{0,4},{2,6},{4,0},{6,2},{8,12},{10,14},{12,8},{14,10},{16,20},{18,... | collective-permute-start | bytes 884744 | tf_op jit(solution)/shard_map/ppermute | solution.py:37
  97.5 9.1 %collective-permute-start.21 = (bf16[192,768]{1,0:T(8,128)(2,1)S(1)}, bf16[192,768]{1,0:T(8,128)(2,1)S(1)}, u32[]{:S(2)}, u32[]{:S(2)}) collective-permute-start(bf16[192,768]{1,0:T(8,128)(2,1)S(1)} %get-tuple-element.157), channel_id=1, source_target_pairs={{0,2},{2,0},{4,6},{6,4},{8,10},{10,8},{12,14},{14,12},{16,18},{18,... | collective-permute-start | bytes 884744 | tf_op jit(solution)/shard_map/ppermute | solution.py:37
  106.4 16.8 %collective-permute-start.23 = (f32[8,768]{1,0:T(8,128)S(1)}, f32[8,768]{1,0:T(8,128)S(1)}, u32[]{:S(2)}, u32[]{:S(2)}) collective-permute-start(f32[8,768]{1,0:T(8,128)S(1)} %get-tuple-element.144.refs_12_), channel_id=1, source_target_pairs={{0,1},{1,0},{2,3},{3,2},{4,5},{5,4},{6,7},{7,6},{8,9},{9,8},{10,11... | collective-permute-start | bytes 73736 | tf_op jit(solution)/shard_map/ppermute | solution.py:37
  108.2 14.4 %collective-permute-start.24 = (bf16[192,768]{1,0:T(8,128)(2,1)S(1)}, bf16[192,768]{1,0:T(8,128)(2,1)S(1)}, u32[]{:S(2)}, u32[]{:S(2)}) collective-permute-start(bf16[192,768]{1,0:T(8,128)(2,1)S(1)} %get-tuple-element.168), channel_id=1, source_target_pairs={{0,4},{2,6},{4,0},{6,2},{8,12},{10,14},{12,8},{14,10},{16,20},{18,... | collective-permute-start | bytes 884744 | tf_op jit(solution)/shard_map/ppermute | solution.py:37
  109.6 12.9 %collective-permute-start.25 = (bf16[192,768]{1,0:T(8,128)(2,1)S(1)}, bf16[192,768]{1,0:T(8,128)(2,1)S(1)}, u32[]{:S(2)}, u32[]{:S(2)}) collective-permute-start(bf16[192,768]{1,0:T(8,128)(2,1)S(1)} %get-tuple-element.169), channel_id=1, source_target_pairs={{0,2},{2,0},{4,6},{6,4},{8,10},{10,8},{12,14},{14,12},{16,18},{18,... | collective-permute-start | bytes 884744 | tf_op jit(solution)/shard_map/ppermute | solution.py:37
  110.1 9.6 %collective-permute-start.26 = (bf16[192,768]{1,0:T(8,128)(2,1)S(1)}, bf16[192,768]{1,0:T(8,128)(2,1)S(1)}, u32[]{:S(2)}, u32[]{:S(2)}) collective-permute-start(bf16[192,768]{1,0:T(8,128)(2,1)S(1)} %get-tuple-element.170), channel_id=1, source_target_pairs={{0,8},{2,10},{4,12},{6,14},{8,0},{10,2},{12,4},{14,6},{16,24},{18,... | collective-permute-start | bytes 884744 | tf_op jit(solution)/shard_map/ppermute | solution.py:37
  120.4 10.8 %collective-permute-start.30 = (bf16[96,768]{1,0:T(8,128)(2,1)S(1)}, bf16[96,768]{1,0:T(8,128)(2,1)S(1)}, u32[]{:S(2)}, u32[]{:S(2)}) collective-permute-start(bf16[96,768]{1,0:T(8,128)(2,1)S(1)} %get-tuple-element.178), channel_id=1, source_target_pairs={{0,16},{2,18},{4,20},{6,22},{8,24},{10,26},{12,28},{14,30},{16,0},... | collective-permute-start | bytes 442376 | tf_op jit(solution)/shard_map/ppermute | solution.py:37
  127.9 15.3 %collective-permute-start.27 = (bf16[400,768]{1,0:T(8,128)(2,1)S(1)}, bf16[400,768]{1,0:T(8,128)(2,1)S(1)}, u32[]{:S(2)}, u32[]{:S(2)}) collective-permute-start(bf16[400,768]{1,0:T(8,128)(2,1)S(1)} %get-tuple-element.174), channel_id=1, source_target_pairs={{0,2},{2,0},{4,6},{6,4},{8,10},{10,8},{12,14},{14,12},{16,18},{18,... | collective-permute-start | bytes 1843208 | tf_op jit(solution)/shard_map/ppermute | solution.py:37
  129.5 13.8 %collective-permute-start.28 = (bf16[384,768]{1,0:T(8,128)(2,1)S(1)}, bf16[384,768]{1,0:T(8,128)(2,1)S(1)}, u32[]{:S(2)}, u32[]{:S(2)}) collective-permute-start(bf16[384,768]{1,0:T(8,128)(2,1)S(1)} %get-tuple-element.176), channel_id=1, source_target_pairs={{0,4},{2,6},{4,0},{6,2},{8,12},{10,14},{12,8},{14,10},{16,20},{18,... | collective-permute-start | bytes 1769480 | tf_op jit(solution)/shard_map/ppermute | solution.py:37
  130.0 10.7 %collective-permute-start.29 = (bf16[192,768]{1,0:T(8,128)(2,1)S(1)}, bf16[192,768]{1,0:T(8,128)(2,1)S(1)}, u32[]{:S(2)}, u32[]{:S(2)}) collective-permute-start(bf16[192,768]{1,0:T(8,128)(2,1)S(1)} %get-tuple-element.177), channel_id=1, source_target_pairs={{0,8},{2,10},{4,12},{6,14},{8,0},{10,2},{12,4},{14,6},{16,24},{18,... | collective-permute-start | bytes 884744 | tf_op jit(solution)/shard_map/ppermute | solution.py:37
  131.7 14.0 %collective-permute-start.34 = (bf16[96,768]{1,0:T(8,128)(2,1)S(1)}, bf16[96,768]{1,0:T(8,128)(2,1)S(1)}, u32[]{:S(2)}, u32[]{:S(2)}) collective-permute-start(bf16[96,768]{1,0:T(8,128)(2,1)S(1)} %add_last.3.refs_3_.refs_1_), channel_id=1, source_target_pairs={{0,16},{2,18},{4,20},{6,22},{8,24},{10,26},{12,28},{14,30},{16,0},... | collective-permute-start | bytes 442376 | tf_op jit(solution)/shard_map/ppermute | solution.py:37
  141.4 7.4 %collective-permute-start.33 = (bf16[96,768]{1,0:T(8,128)(2,1)S(1)}, bf16[96,768]{1,0:T(8,128)(2,1)S(1)}, u32[]{:S(2)}, u32[]{:S(2)}) collective-permute-start(bf16[96,768]{1,0:T(8,128)(2,1)S(1)} %get-tuple-element.184), channel_id=1, source_target_pairs={{0,16},{2,18},{4,20},{6,22},{8,24},{10,26},{12,28},{14,30},{16,0},... | collective-permute-start | bytes 442376 | tf_op jit(solution)/shard_map/ppermute | solution.py:37
  144.1 7.5 %collective-permute-start.31 = (bf16[208,768]{1,0:T(8,128)(2,1)S(1)}, bf16[208,768]{1,0:T(8,128)(2,1)S(1)}, u32[]{:S(2)}, u32[]{:S(2)}) collective-permute-start(bf16[208,768]{1,0:T(8,128)(2,1)S(1)} %get-tuple-element.181), channel_id=1, source_target_pairs={{0,4},{2,6},{4,0},{6,2},{8,12},{10,14},{12,8},{14,10},{16,20},{18,... | collective-permute-start | bytes 958472 | tf_op jit(solution)/shard_map/ppermute | solution.py:37
  144.5 7.0 %collective-permute-start.32 = (bf16[192,768]{1,0:T(8,128)(2,1)S(1)}, bf16[192,768]{1,0:T(8,128)(2,1)S(1)}, u32[]{:S(2)}, u32[]{:S(2)}) collective-permute-start(bf16[192,768]{1,0:T(8,128)(2,1)S(1)} %get-tuple-element.183), channel_id=1, source_target_pairs={{0,2},{2,0},{4,6},{6,4},{8,10},{10,8},{12,14},{14,12},{16,18},{18,... | collective-permute-start | bytes 884744 | tf_op jit(solution)/shard_map/ppermute | solution.py:37
  146.3 12.6 %collective-permute-start.37 = (bf16[192,768]{1,0:T(8,128)(2,1)S(1)}, bf16[192,768]{1,0:T(8,128)(2,1)S(1)}, u32[]{:S(2)}, u32[]{:S(2)}) collective-permute-start(bf16[192,768]{1,0:T(8,128)(2,1)S(1)} %join_pieces.3.refs_3_.refs_1_), channel_id=1, source_target_pairs={{0,8},{2,10},{4,12},{6,14},{8,0},{10,2},{12,4},{14,6},{16,24},{18,... | collective-permute-start | bytes 884744 | tf_op jit(solution)/shard_map/ppermute | solution.py:37
  149.4 11.2 %collective-permute-start.36 = (bf16[96,768]{1,0:T(8,128)(2,1)S(1)}, bf16[96,768]{1,0:T(8,128)(2,1)S(1)}, u32[]{:S(2)}, u32[]{:S(2)}) collective-permute-start(bf16[96,768]{1,0:T(8,128)(2,1)S(1)} %add_last.4.refs_5_.refs_1_), channel_id=1, source_target_pairs={{0,16},{2,18},{4,20},{6,22},{8,24},{10,26},{12,28},{14,30},{16,0},... | collective-permute-start | bytes 442376 | tf_op jit(solution)/shard_map/ppermute | solution.py:37
  152.3 13.6 %collective-permute-start.35 = (bf16[208,768]{1,0:T(8,128)(2,1)S(1)}, bf16[208,768]{1,0:T(8,128)(2,1)S(1)}, u32[]{:S(2)}, u32[]{:S(2)}) collective-permute-start(bf16[208,768]{1,0:T(8,128)(2,1)S(1)} %get-tuple-element.186), channel_id=1, source_target_pairs={{0,8},{2,10},{4,12},{6,14},{8,0},{10,2},{12,4},{14,6},{16,24},{18,... | collective-permute-start | bytes 958472 | tf_op jit(solution)/shard_map/ppermute | solution.py:37
  159.6 8.5 %collective-permute-start.41 = (bf16[192,768]{1,0:T(8,128)(2,1)S(1)}, bf16[192,768]{1,0:T(8,128)(2,1)S(1)}, u32[]{:S(2)}, u32[]{:S(2)}) collective-permute-start(bf16[192,768]{1,0:T(8,128)(2,1)S(1)} %get-tuple-element.187.refs_3_), channel_id=1, source_target_pairs={{0,2},{2,0},{4,6},{6,4},{8,10},{10,8},{12,14},{14,12},{16,18},{18,... | collective-permute-start | bytes 884744 | tf_op jit(solution)/shard_map/ppermute | solution.py:37
  161.1 12.8 %collective-permute-start.39 = (bf16[192,768]{1,0:T(8,128)(2,1)S(1)}, bf16[192,768]{1,0:T(8,128)(2,1)S(1)}, u32[]{:S(2)}, u32[]{:S(2)}) collective-permute-start(bf16[192,768]{1,0:T(8,128)(2,1)S(1)} %join_pieces.4.refs_3_.refs_1_), channel_id=1, source_target_pairs={{0,8},{2,10},{4,12},{6,14},{8,0},{10,2},{12,4},{14,6},{16,24},{18,... | collective-permute-start | bytes 884744 | tf_op jit(solution)/shard_map/ppermute | solution.py:37
  161.3 6.7 %collective-permute-start.40 = (bf16[192,768]{1,0:T(8,128)(2,1)S(1)}, bf16[192,768]{1,0:T(8,128)(2,1)S(1)}, u32[]{:S(2)}, u32[]{:S(2)}) collective-permute-start(bf16[192,768]{1,0:T(8,128)(2,1)S(1)} %get-tuple-element.190.refs_1_), channel_id=1, source_target_pairs={{0,4},{2,6},{4,0},{6,2},{8,12},{10,14},{12,8},{14,10},{16,20},{18,... | collective-permute-start | bytes 884744 | tf_op jit(solution)/shard_map/ppermute | solution.py:37
  166.4 10.6 %collective-permute-start.38 = (bf16[112,768]{1,0:T(8,128)(2,1)S(1)}, bf16[112,768]{1,0:T(8,128)(2,1)S(1)}, u32[]{:S(2)}, u32[]{:S(2)}) collective-permute-start(bf16[112,768]{1,0:T(8,128)(2,1)S(1)} %get-tuple-element.189), channel_id=1, source_target_pairs={{0,16},{2,18},{4,20},{6,22},{8,24},{10,26},{12,28},{14,30},{16,0},... | collective-permute-start | bytes 516104 | tf_op jit(solution)/shard_map/ppermute | solution.py:37
  168.7 14.2 %collective-permute-start.45 = (bf16[384,768]{1,0:T(8,128)(2,1)S(1)}, bf16[384,768]{1,0:T(8,128)(2,1)S(1)}, u32[]{:S(2)}, u32[]{:S(2)}) collective-permute-start(bf16[384,768]{1,0:T(8,128)(2,1)S(1)} %get-tuple-element.195.refs_1_), channel_id=1, source_target_pairs={{0,2},{2,0},{4,6},{6,4},{8,10},{10,8},{12,14},{14,12},{16,18},{18,... | collective-permute-start | bytes 1769480 | tf_op jit(solution)/shard_map/ppermute | solution.py:37
  170.0 14.1 %collective-permute-start.46 = (bf16[384,768]{1,0:T(8,128)(2,1)S(1)}, bf16[384,768]{1,0:T(8,128)(2,1)S(1)}, u32[]{:S(2)}, u32[]{:S(2)}) collective-permute-start(bf16[384,768]{1,0:T(8,128)(2,1)S(1)} %get-tuple-element.191.refs_3_), channel_id=1, source_target_pairs={{0,4},{2,6},{4,0},{6,2},{8,12},{10,14},{12,8},{14,10},{16,20},{18,... | collective-permute-start | bytes 1769480 | tf_op jit(solution)/shard_map/ppermute | solution.py:37
  174.5 13.9 %collective-permute-start.43 = (bf16[192,768]{1,0:T(8,128)(2,1)S(1)}, bf16[192,768]{1,0:T(8,128)(2,1)S(1)}, u32[]{:S(2)}, u32[]{:S(2)}) collective-permute-start(bf16[192,768]{1,0:T(8,128)(2,1)S(1)} %get-tuple-element.194.refs_1_), channel_id=1, source_target_pairs={{0,4},{2,6},{4,0},{6,2},{8,12},{10,14},{12,8},{14,10},{16,20},{18,... | collective-permute-start | bytes 884744 | tf_op jit(solution)/shard_map/ppermute | solution.py:37
  175.8 12.7 %collective-permute-start.44 = (bf16[192,768]{1,0:T(8,128)(2,1)S(1)}, bf16[192,768]{1,0:T(8,128)(2,1)S(1)}, u32[]{:S(2)}, u32[]{:S(2)}) collective-permute-start(bf16[192,768]{1,0:T(8,128)(2,1)S(1)} %get-tuple-element.192.refs_3_), channel_id=1, source_target_pairs={{0,2},{2,0},{4,6},{6,4},{8,10},{10,8},{12,14},{14,12},{16,18},{18,... | collective-permute-start | bytes 884744 | tf_op jit(solution)/shard_map/ppermute | solution.py:37
  189.1 13.1 %collective-permute-start.48 = (bf16[384,768]{1,0:T(8,128)(2,1)S(1)}, bf16[384,768]{1,0:T(8,128)(2,1)S(1)}, u32[]{:S(2)}, u32[]{:S(2)}) collective-permute-start(bf16[384,768]{1,0:T(8,128)(2,1)S(1)} %get-tuple-element.199.refs_1_), channel_id=1, source_target_pairs={{0,2},{2,0},{4,6},{6,4},{8,10},{10,8},{12,14},{14,12},{16,18},{18,... | collective-permute-start | bytes 1769480 | tf_op jit(solution)/shard_map/ppermute | solution.py:37
  189.4 12.7 %collective-permute-start.49 = (bf16[384,768]{1,0:T(8,128)(2,1)S(1)}, bf16[384,768]{1,0:T(8,128)(2,1)S(1)}, u32[]{:S(2)}, u32[]{:S(2)}) collective-permute-start(bf16[384,768]{1,0:T(8,128)(2,1)S(1)} %get-tuple-element.198.refs_3_), channel_id=1, source_target_pairs={{0,4},{2,6},{4,0},{6,2},{8,12},{10,14},{12,8},{14,10},{16,20},{18,... | collective-permute-start | bytes 1769480 | tf_op jit(solution)/shard_map/ppermute | solution.py:37
  190.9 6.0 %collective-permute-start.42 = (bf16[96,768]{1,0:T(8,128)(2,1)S(1)}, bf16[96,768]{1,0:T(8,128)(2,1)S(1)}, u32[]{:S(2)}, u32[]{:S(2)}) collective-permute-start(bf16[96,768]{1,0:T(8,128)(2,1)S(1)} %get-tuple-element.193.refs_1_), channel_id=1, source_target_pairs={{0,16},{2,18},{4,20},{6,22},{8,24},{10,26},{12,28},{14,30},{16,0},... | collective-permute-start | bytes 442376 | tf_op jit(solution)/shard_map/ppermute | solution.py:37
  193.5 28.5 %collective-permute-start.22 = (bf16[512,768]{1,0:T(8,128)(2,1)}, bf16[512,768]{1,0:T(8,128)(2,1)}, u32[]{:S(2)}, u32[]{:S(2)}) collective-permute-start(bf16[512,768]{1,0:T(8,128)(2,1)} %get-tuple-element.160.refs_3_), channel_id=1, source_target_pairs={{0,1},{1,0},{2,3},{3,2},{4,5},{5,4},{6,7},{7,6},{8,9},{9,8},{10,11... | collective-permute-start | bytes 2359304 | tf_op jit(solution)/shard_map/ppermute | solution.py:37
  197.5 9.3 %collective-permute-start.47 = (bf16[192,768]{1,0:T(8,128)(2,1)S(1)}, bf16[192,768]{1,0:T(8,128)(2,1)S(1)}, u32[]{:S(2)}, u32[]{:S(2)}) collective-permute-start(bf16[192,768]{1,0:T(8,128)(2,1)S(1)} %join_pieces.5.refs_5_.refs_1_), channel_id=1, source_target_pairs={{0,8},{2,10},{4,12},{6,14},{8,0},{10,2},{12,4},{14,6},{16,24},{18,... | collective-permute-start | bytes 884744 | tf_op jit(solution)/shard_map/ppermute | solution.py:37
  207.4 8.4 %collective-permute-start.50 = (bf16[192,768]{1,0:T(8,128)(2,1)S(1)}, bf16[192,768]{1,0:T(8,128)(2,1)S(1)}, u32[]{:S(2)}, u32[]{:S(2)}) collective-permute-start(bf16[192,768]{1,0:T(8,128)(2,1)S(1)} %get-tuple-element.201.refs_1_), channel_id=1, source_target_pairs={{0,4},{2,6},{4,0},{6,2},{8,12},{10,14},{12,8},{14,10},{16,20},{18,... | collective-permute-start | bytes 884744 | tf_op jit(solution)/shard_map/ppermute | solution.py:37
  207.7 14.3 %copy-start.3 = (f32[512,768]{1,0:T(8,128)S(1)}, f32[512,768]{1,0:T(8,128)}, u32[]{:S(2)}) copy-start(f32[512,768]{1,0:T(8,128)} %copy-done.2) | copy-start | bytes 4718596
  207.7 9.6 %collective-permute-start.51 = (bf16[192,768]{1,0:T(8,128)(2,1)S(1)}, bf16[192,768]{1,0:T(8,128)(2,1)S(1)}, u32[]{:S(2)}, u32[]{:S(2)}) collective-permute-start(bf16[192,768]{1,0:T(8,128)(2,1)S(1)} %get-tuple-element.202.refs_3_.refs_5_), channel_id=1, source_target_pairs={{0,2},{2,0},{4,6},{6,4},{8,10},{10,8},{12,14},{14,12},{16,18},{18,... | collective-permute-start | bytes 884744 | tf_op jit(solution)/shard_map/ppermute | solution.py:37
  218.9 10.2 %collective-permute-start.52 = (bf16[384,768]{1,0:T(8,128)(2,1)}, bf16[384,768]{1,0:T(8,128)(2,1)}, u32[]{:S(2)}, u32[]{:S(2)}) collective-permute-start(bf16[384,768]{1,0:T(8,128)(2,1)} %get-tuple-element.203.refs_1_), channel_id=1, source_target_pairs={{0,2},{2,0},{4,6},{6,4},{8,10},{10,8},{12,14},{14,12},{16,18},{18,... | collective-permute-start | bytes 1769480 | tf_op jit(solution)/shard_map/ppermute | solution.py:37
  218.9 10.6 %collective-permute-start.53 = (bf16[384,768]{1,0:T(8,128)(2,1)}, bf16[384,768]{1,0:T(8,128)(2,1)}, u32[]{:S(2)}, u32[]{:S(2)}) collective-permute-start(bf16[384,768]{1,0:T(8,128)(2,1)} %get-tuple-element.204.refs_3_.refs_5_), channel_id=1, source_target_pairs={{0,4},{2,6},{4,0},{6,2},{8,12},{10,14},{12,8},{14,10},{16,20},{18,... | collective-permute-start | bytes 1769480 | tf_op jit(solution)/shard_map/ppermute | solution.py:37
  (34 other events, 206.6 us)
